TPU v7x, 32 devices: a whole 2x2x4 slice. The times are simulated.
32 devices in a mesh: groups: 2 (over x), dp: 16 (over z, y, core).
Axes of the slice: x: 2, y: 2, z: 4, core: 2. Of those that a mesh axis runs over, the one named last changes fastest.
Arguments:
- token_inputs: bfloat16 [64, 128, 2048], P(('groups', 'dp')), parts along dimension 0, may hold values from -6 to 6
- state_in: bfloat16 [64, 128, 1, 256], P(('groups', 'dp')), parts along dimension 0, may hold values from -0.03125 to 0.03125
- state_out: bfloat16 [64, 128, 1, 256], P(('groups', 'dp')), parts along dimension 0, may hold values from -0.375 to 0.375
- log_decay: float32 [64, 128, 32], P(('groups', 'dp')), parts along dimension 0, may hold values from -0.8 to 0
- skip_gain: float32 [32], replicated, may hold values from 0.25 to 2.5
- conv_weight: float32 [4, 2048], replicated, may hold values from -3 to 3
- out_cotangent: bfloat16 [64, 128, 2048], P(('groups', 'dp')), parts along dimension 0, may hold values from -1.5 to 1.5
- queries: bfloat16 [64, 128, 4096], P(('groups', 'dp')), parts along dimension 0, may hold values from -12 to 12
- own_keys: bfloat16 [64, 128, 512], P(('groups', 'dp')), parts along dimension 0, may hold values from -4 to 4
- own_values: bfloat16 [64, 128, 512], P(('groups', 'dp')), parts along dimension 0, may hold values from -6 to 6
- attn_cotangent: bfloat16 [64, 128, 4096], P(('groups', 'dp')), parts along dimension 0, may hold values from -6 to 6
- resp_length: int32 [64], P(('groups', 'dp')), parts along dimension 0, may hold values from 32 to 128
- resp_prefix: int32 [64], P('groups'), parts along dimension 0, may hold values from 0 to 15, as said below
- prefix_state: bfloat16 [32, 32, 64, 256], P(('groups', 'dp')), parts along dimension 0, may hold values from -3 to 3
- prefix_tail: bfloat16 [32, 3, 2048], P(('groups', 'dp')), parts along dimension 0, may hold values from -6 to 6
- prefix_keys: bfloat16 [32, 128, 512], P(('groups', 'dp')), parts along dimension 0, may hold values from -4 to 4
- prefix_values: bfloat16 [32, 128, 512], P(('groups', 'dp')), parts along dimension 0, may hold values from -6 to 6
- prefix_length: int32 [32], P('groups'), parts along dimension 0, may hold values from 32 to 128
Outputs:
- grad_inputs: bfloat16 [64, 128, 2048], P(('groups', 'dp')), parts along dimension 0
- grad_read: bfloat16 [64, 128, 1, 256], P(('groups', 'dp')), parts along dimension 0
- grad_queries: bfloat16 [64, 128, 4096], P(('groups', 'dp')), parts along dimension 0
- grad_state: bfloat16 [32, 32, 64, 256], P(('groups', 'dp')), parts along dimension 0
- grad_tail: float32 [32, 3, 2048], P(('groups', 'dp')), parts along dimension 0
- grad_prefix_keys: float32 [32, 128, 512], P(('groups', 'dp')), parts along dimension 0
- grad_prefix_values: float32 [32, 128, 512], P(('groups', 'dp')), parts along dimension 0
- grad_conv: float32 [8, 2048], P('groups'), parts along dimension 0
There are 2 independent parts, one for each index of `groups`. A program takes and returns all parts, laid end to end along the dimension named above; an argument that names none is the same for every part. Nothing has to cross between parts.
Inputs may be any that keep to these rules, and one draw needn't show every extreme that they name: `resp_prefix`: prefix p is owned by device p; response r lies on device r // 2, and its prefix's owner is that device or one of the 3 devices before it, counted cyclically over the devices of dp.
All inputs are finite; a program needn't handle non-finite values.
Results may differ from a plain program's by a relative error of at most 0.0098.
Values may be sent and summed in bfloat16 or wider, within the bound.
No kernel may reach another device: no remote copies, remote signals or barrier semaphores. Data moves between devices by JAX's collectives and lax.ppermute only.
A program may use at most 128 MiB of HBM per device.

v0:
```python
import math

import jax
import jax.numpy as jnp
from jax import lax
from jax.sharding import PartitionSpec as P

ATT_HEADS = 32
KV_HEADS = 4
ATT_DIM = 128
SPAN = 4


HIGHEST = lax.Precision.HIGHEST
NEG_FILL = -1e30


def from_behind(value, axis, by):
    length = lax.axis_size(axis)
    return lax.ppermute(value, axis, [(i, (i + by) % length) for i in range(length)])


def mamba_grads(
    inputs,
    conv_tail,
    conv_weight,
    write_proj,
    read_proj,
    log_decay,
    skip_gain,
    carry_state,
    cotangent,
):
    length = inputs.shape[0]
    conv_taps = conv_weight.shape[0]
    head_count, head_width, state_width = carry_state.shape
    group_count = read_proj.shape[1]
    per_group = head_count // group_count

    def activate(inputs, conv_tail, conv_weight):
        padded = jnp.concatenate([conv_tail, inputs], axis=0)
        mixed = conv_weight[0] * padded[0:length]
        for tap_index in range(1, conv_taps):
            mixed = mixed + conv_weight[tap_index] * padded[tap_index : tap_index + length]
        return mixed * jax.nn.sigmoid(mixed)

    act_flat, act_pull = jax.vjp(activate, inputs, conv_tail, conv_weight)
    activated = act_flat.reshape(length, head_count, head_width)
    decay_sum = jnp.cumsum(log_decay, axis=0)
    read_heads = jnp.repeat(read_proj, per_group, axis=1)
    intersection = jnp.einsum(
        "tgn,sgn->gts", read_proj, write_proj, preferred_element_type=jnp.float32
    )
    intersection = jnp.repeat(intersection, per_group, axis=0)
    row_index = lax.broadcasted_iota(jnp.int32, (length, length), 0)
    col_index = lax.broadcasted_iota(jnp.int32, (length, length), 1)
    causal = (col_index <= row_index)[None]
    lagged = decay_sum.T[:, :, None] - decay_sum.T[:, None, :]
    decay_weights = jnp.where(causal, jnp.exp(jnp.where(causal, lagged, 0.0)), 0.0)
    weights = decay_weights * intersection
    d_out = cotangent.reshape(length, head_count, head_width)
    d_carried = jnp.exp(decay_sum)[:, :, None] * d_out
    g_state = jnp.einsum(
        "thp,thn->hpn", d_carried, read_heads.astype(jnp.float32), precision=HIGHEST
    )
    d_read_heads = jnp.einsum(
        "thp,hpn->thn", d_carried, carry_state.astype(jnp.float32), precision=HIGHEST
    )
    g_read = d_read_heads.reshape(length, group_count, per_group, state_width).sum(axis=2)
    d_weights = jnp.einsum("thp,shp->hts", d_out, activated, precision=HIGHEST)
    d_intersection = (
        (d_weights * decay_weights).reshape(group_count, per_group, length, length).sum(axis=1)
    )
    g_read = g_read + jnp.einsum(
        "gts,sgn->tgn", d_intersection, write_proj.astype(jnp.float32), precision=HIGHEST
    )
    d_act = (
        jnp.einsum("hts,thp->shp", weights, d_out, precision=HIGHEST)
        + skip_gain[None, :, None] * d_out
    )
    g_inputs, g_tail, g_conv = act_pull(d_act.reshape(length, head_count * head_width))
    return (g_inputs, g_tail, g_conv, g_read, g_state)


def attention_grads(
    queries, own_keys, own_values, prefix_keys, prefix_values, prefix_length, cotangent
):
    length = queries.shape[0]
    pref_rows = prefix_keys.shape[0]
    scale = 1.0 / math.sqrt(ATT_DIM)
    grouped_q = queries.reshape(length, KV_HEADS, ATT_HEADS // KV_HEADS, ATT_DIM)
    all_keys = jnp.concatenate([prefix_keys, own_keys], axis=0).reshape(
        pref_rows + length, KV_HEADS, ATT_DIM
    )
    all_values = jnp.concatenate([prefix_values, own_values], axis=0).reshape(
        pref_rows + length, KV_HEADS, ATT_DIM
    )
    scores = (
        jnp.einsum("tkrd,skd->krts", grouped_q, all_keys, preferred_element_type=jnp.float32)
        * scale
    )
    row_index = lax.broadcasted_iota(jnp.int32, (length, pref_rows + length), 0)
    col_index = lax.broadcasted_iota(jnp.int32, (length, pref_rows + length), 1)
    allowed = jnp.where(
        col_index < pref_rows, col_index < prefix_length, col_index - pref_rows <= row_index
    )
    scores = jnp.where(allowed[None, None], scores, NEG_FILL)
    top_score = jnp.max(scores, axis=-1, keepdims=True)
    raised = jnp.exp(scores - top_score)
    probs = raised / jnp.sum(raised, axis=-1, keepdims=True)
    probs_low = probs.astype(jnp.bfloat16)
    output = jnp.einsum("krts,skd->tkrd", probs_low, all_values, preferred_element_type=jnp.float32)
    d_out = cotangent.reshape(length, KV_HEADS, ATT_HEADS // KV_HEADS, ATT_DIM)
    d_probs = jnp.einsum("tkrd,skd->krts", d_out, all_values, preferred_element_type=jnp.float32)
    delta = jnp.transpose(jnp.sum(d_out.astype(jnp.float32) * output, axis=-1), (1, 2, 0))
    d_scores = (probs * (d_probs - delta[..., None]) * scale).astype(jnp.bfloat16)
    g_query = jnp.einsum("krts,skd->tkrd", d_scores, all_keys, preferred_element_type=jnp.float32)
    g_keys = jnp.einsum("krts,tkrd->skd", d_scores, grouped_q, preferred_element_type=jnp.float32)
    g_values = jnp.einsum("krts,tkrd->skd", probs_low, d_out, preferred_element_type=jnp.float32)
    return (
        g_query.reshape(length, ATT_HEADS * ATT_DIM),
        g_keys[0:pref_rows].reshape(pref_rows, KV_HEADS * ATT_DIM),
        g_values[0:pref_rows].reshape(pref_rows, KV_HEADS * ATT_DIM),
    )


def response_grads(
    inputs,
    write_proj,
    read_proj,
    log_decay,
    out_cotangent,
    queries,
    own_keys,
    own_values,
    attn_cotangent,
    resp_length,
    prefix_state,
    prefix_tail,
    prefix_keys,
    prefix_values,
    prefix_length,
    conv_weight,
    skip_gain,
):
    live_rows = (lax.broadcasted_iota(jnp.int32, (inputs.shape[0], 1), 0) < resp_length).astype(
        jnp.float32
    )
    g_inputs, g_tail, g_conv, g_read, g_state = mamba_grads(
        inputs.astype(jnp.float32),
        prefix_tail.astype(jnp.float32),
        conv_weight,
        write_proj,
        read_proj,
        log_decay,
        skip_gain,
        prefix_state,
        out_cotangent.astype(jnp.float32) * live_rows,
    )
    masked_cot = jnp.where(live_rows > 0.5, attn_cotangent, jnp.zeros((), attn_cotangent.dtype))
    g_query, g_keys, g_values = attention_grads(
        queries, own_keys, own_values, prefix_keys, prefix_values, prefix_length, masked_cot
    )
    return (g_inputs, g_tail, g_conv, g_read, g_state, g_query, g_keys, g_values)


def on_device(
    token_inputs,
    state_in,
    state_out,
    log_decay,
    skip_gain,
    conv_weight,
    out_cotangent,
    queries,
    own_keys,
    own_values,
    attn_cotangent,
    resp_length,
    resp_prefix,
    prefix_state,
    prefix_tail,
    prefix_keys,
    prefix_values,
    prefix_length,
):
    devices = lax.axis_size("dp")
    rank_here = lax.axis_index("dp")
    per_dev = token_inputs.shape[0]
    owned_count = prefix_state.shape[0]
    owned_items = (prefix_state, prefix_tail, prefix_keys, prefix_values)
    pieces = [owned_items]
    for offset in range(1, SPAN):
        pieces.append(
            from_behind(
                (owned_items[0], owned_items[1], owned_items[2], owned_items[3]), "dp", offset
            )
        )
    fetched = tuple(
        (jnp.concatenate([piece[member] for piece in pieces], axis=0) for member in range(4))
    )
    my_prefix = lax.dynamic_slice_in_dim(resp_prefix, rank_here * per_dev, per_dev)
    owner = my_prefix // owned_count
    distance = jnp.mod(rank_here - owner, devices)
    position = distance * owned_count + jnp.mod(my_prefix, owned_count)
    chosen = tuple((jnp.take(member, position, axis=0) for member in fetched))
    chosen_length = jnp.take(prefix_length, my_prefix, axis=0)

    def one_response(items):
        return response_grads(
            items[0],
            items[1],
            items[2],
            items[3],
            items[4],
            items[5],
            items[6],
            items[7],
            items[8],
            items[9],
            items[10],
            items[11],
            items[12],
            items[13],
            items[14],
            conv_weight,
            skip_gain,
        )

    grads = lax.map(
        one_response,
        (
            token_inputs,
            state_in,
            state_out,
            log_decay,
            out_cotangent,
            queries,
            own_keys,
            own_values,
            attn_cotangent,
            resp_length,
            chosen[0],
            chosen[1],
            chosen[2],
            chosen[3],
            chosen_length,
        ),
    )
    g_inputs, g_tail, g_conv, g_read, g_state, g_query, g_keys, g_values = grads
    adjoint = (g_state, g_tail, g_keys, g_values)
    totals = None
    for offset in range(SPAN):
        sender = jnp.mod(rank_here + offset, devices)
        their_prefix = lax.dynamic_slice_in_dim(resp_prefix, sender * per_dev, per_dev)
        target = their_prefix - rank_here * owned_count
        pick = (target[:, None] == jnp.arange(owned_count, dtype=jnp.int32)[None, :]).astype(
            jnp.float32
        )
        if offset == 0:
            arrived = adjoint
        else:
            arrived = from_behind((adjoint[0], adjoint[1], adjoint[2], adjoint[3]), "dp", -offset)
        added = tuple(
            (jnp.einsum("ri,r...->i...", pick, member, precision=HIGHEST) for member in arrived)
        )
        totals = (
            added if totals is None else tuple((left + right for left, right in zip(totals, added)))
        )
    token_total = per_dev * token_inputs.shape[1] * devices
    conv_total = lax.psum(jnp.sum(g_conv, axis=0), "dp")
    grad_conv = conv_total * (1.0 / math.sqrt(token_total))
    return (
        g_inputs.astype(jnp.bfloat16),
        g_read.astype(jnp.bfloat16),
        g_query.astype(jnp.bfloat16),
        totals[0].astype(jnp.bfloat16),
        totals[1],
        totals[2],
        totals[3],
        grad_conv,
    )


def solution(mesh):
    placed = (
        P(("groups", "dp"), None, None),
        P(("groups", "dp"), None, None, None),
        P(("groups", "dp"), None, None, None),
        P(("groups", "dp"), None, None),
        P(),
        P(),
        P(("groups", "dp"), None, None),
        P(("groups", "dp"), None, None),
        P(("groups", "dp"), None, None),
        P(("groups", "dp"), None, None),
        P(("groups", "dp"), None, None),
        P(("groups", "dp")),
        P("groups"),
        P(("groups", "dp"), None, None, None),
        P(("groups", "dp"), None, None),
        P(("groups", "dp"), None, None),
        P(("groups", "dp"), None, None),
        P("groups"),
    )
    return jax.shard_map(
        on_device,
        mesh=mesh,
        in_specs=placed,
        out_specs=(
            P(("groups", "dp"), None, None),
            P(("groups", "dp"), None, None, None),
            P(("groups", "dp"), None, None),
            P(("groups", "dp"), None, None, None),
            P(("groups", "dp"), None, None),
            P(("groups", "dp"), None, None),
            P(("groups", "dp"), None, None),
            P("groups", None),
        ),
        check_vma=False,
    )
```

profile of v0, /device:TPU:0, one launch (start us, length us, event | category | flops | bytes accessed | tf_op | source)
XLA Modules:
  0.0 621.2 jit_solution(5547317730097307754)
XLA Ops:
  0.7 3.0 collective-permute-start.1
  3.7 2.8 collective-permute-start.2
  11.7 2.8 collective-permute-start.8
  20.3 1.8 collective-permute-start.9
  22.1 47.9 %collective-permute-done.10 = bf16[1,128,512]{2,1,0:T(8,128)(2,1)S(1)} collective-permute-done((bf16[1,128,512]{2,1,0:T(8,128)(2,1)}, bf16[1,128,512]{2,1,0:T(8,128)(2,1)S(1)}, u32[]{:S(2)}, u32[]{:S(2)}) %collective-permute-start.10) | collective-permute-done | bytes 131104 | tf_op jit(solution)/shard_map/ppermute | solution.py:20
  70.1 7.1 %collective-permute-start.11 = (bf16[1,128,512]{2,1,0:T(8,128)(2,1)}, bf16[1,128,512]{2,1,0:T(8,128)(2,1)S(1)}, u32[]{:S(2)}, u32[]{:S(2)}) collective-permute-start(bf16[1,128,512]{2,1,0:T(8,128)(2,1)} %param.38), channel_id=1, source_target_pairs={{0,3},{1,4},{2,5},{3,6},{4,7},{5,8},{6,9},{7,10},{8,11},{9,12},{10... | collective-permute-start | bytes 393224 | tf_op jit(solution)/shard_map/ppermute | solution.py:20
  83.0 3.6 pad_maximum_fusion.1
  86.7 2.9 gather_fusion.1
  91.2 131.3 %while.26 = (s32[]{:T(128)}, bf16[2,128,2048]{2,1,0:T(8,128)(2,1)}, f32[2,3,2048]{2,0,1:T(2,128)}, f32[2,4,2048]{2,1,0:T(4,128)}, bf16[2,128,1,256]{3,1,2,0:T(8,...) while((s32[]{:T(128)}, bf16[2,128,2048]{2,1,0:T(8,128)(2,1)}, ...), condition=%wide.region_10.12_spmd, body=%wide.region_0.11_spmd.sunk | while | flops 4122609152 | bytes 132667032 | solution.py:230
  107.6 2.3 constant_dynamic-slice_fusion.22
  111.5 2.1 constant_dynamic-slice_fusion.19
  115.2 3.3 fusion.180
  118.6 2.8 fusion.178
  121.5 2.8 multiply_reduce_fusion.7
  124.3 4.0 multiply_reduce_fusion.8
  130.9 1.7 pad_add_fusion.2
  135.8 2.3 bitcast_dynamic-update-slice_fusion.5
  138.1 3.4 fusion.183
  141.6 2.8 fusion.184
  169.1 2.3 constant_dynamic-slice_fusion.22
  173.0 2.1 constant_dynamic-slice_fusion.19
  176.7 3.3 fusion.180
  180.1 2.8 fusion.178
  183.0 2.8 multiply_reduce_fusion.7
  185.8 4.0 multiply_reduce_fusion.8
  197.4 2.3 bitcast_dynamic-update-slice_fusion.5
  199.6 3.4 fusion.183
  203.1 2.8 fusion.184
  225.3 1.7 collective-permute-start.22
  228.9 71.5 %psum.7 = f32[4,2048]{1,0:T(4,128)S(1)} all-reduce(f32[4,2048]{1,0:T(4,128)S(1)} %reduce_sum.112), channel_id=1, replica_groups=mesh['groups'=2,'dp'=16] {'dp'}, use_global_device_ids=true, to_apply=%region_12.14 | all-reduce | flops 8192 | bytes 65536 | tf_op jit(solution)/shard_map/psum | solution.py:271
  301.1 13.8 %fusion.77 = f32[1,32,64,256]{3,0,2,1:T(1,128)S(1)} fusion(f32[2,32,64,256]{3,2,1,0:T(8,128)} %get-tuple-element.852, pred[2]{0:T(512)(128)(4,1)S(1)} %copy-done.39), kind=kOutput, calls=%fused_computation.136 | convolution fusion | flops 12582912 | bytes 6291458 | tf_op jit(solution)/shard_map/ri,r...->i.../dot_general | solution.py:265
  316.6 2.1 fusion.101
  319.7 72.4 %collective-permute-done.16 = f32[2,3,2048]{2,0,1:T(2,128)} collective-permute-done((f32[2,3,2048]{2,0,1:T(2,128)S(1)}, f32[2,3,2048]{2,0,1:T(2,128)}, u32[]{:S(2)}, u32[]{:S(2)}) %collective-permute-start.16) | collective-permute-done | bytes 49184 | tf_op jit(solution)/shard_map/ppermute | solution.py:20
  393.0 2.8 fusion.103
  395.8 4.4 collective-permute-start.19
  401.8 142.0 %collective-permute-done.23 = f32[2,128,512]{1,2,0:T(8,128)S(1)} collective-permute-done((f32[2,128,512]{1,2,0:T(8,128)S(1)}, f32[2,128,512]{1,2,0:T(8,128)S(1)}, u32[]{:S(2)}, u32[]{:S(2)}) %collective-permute-start.23) | collective-permute-done | bytes 524320 | tf_op jit(solution)/shard_map/ppermute | solution.py:20
  543.8 5.6 collective-permute-done.19
  552.0 2.0 copy.170
  554.0 2.0 copy.168
  557.1 2.1 copy.162
  559.2 2.0 copy.160
  561.2 4.7 collective-permute-done.20
  565.9 2.1 copy.164
  569.1 2.2 fusion.95
  577.2 13.9 %fusion.73 = f32[1,32,64,256]{3,0,2,1:T(1,128)S(1)} fusion(f32[2,32,64,256]{3,2,1,0:T(8,128)} %collective-permute-done.13, pred[2]{0:T(512)(128)(4,1)S(1)} %copy-done.38), kind=kOutput, calls=%fused_computation.132 | convolution fusion | flops 12582912 | bytes 6291458 | tf_op jit(solution)/shard_map/ri,r...->i.../dot_general | solution.py:265
  591.2 14.2 %fusion.75 = f32[1,32,64,256]{3,0,2,1:T(1,128)S(1)} fusion(f32[2,32,64,256]{3,2,1,0:T(8,128)} %collective-permute-done.12, pred[2]{0:T(512)(128)(4,1)S(1)} %copy-done.37), kind=kOutput, calls=%fused_computation.134 | convolution fusion | flops 12582912 | bytes 6291458 | tf_op jit(solution)/shard_map/ri,r...->i.../dot_general | solution.py:265
  605.4 13.9 %fusion.71 = f32[1,32,64,256]{3,0,2,1:T(1,128)S(1)} fusion(f32[2,32,64,256]{3,2,1,0:T(8,128)} %collective-permute-done.14, pred[2]{0:T(512)(128)(4,1)S(1)} %copy-done.36), kind=kOutput, calls=%fused_computation.130 | convolution fusion | flops 12582912 | bytes 6291458 | tf_op jit(solution)/shard_map/ri,r...->i.../dot_general | solution.py:265
  619.3 1.8 fusion.80
  (334 shorter events, 108.0 us)
Async XLA Ops:
  0.6 8.1 %copy-start = (s32[16]{0:T(128)S(1)}, s32[16]{0:T(128)}, u32[]{:S(2)}) copy-start(s32[16]{0:T(128)} %param.39) | copy-start | bytes 196
  0.6 81.6 %copy-start.33 = (bf16[1,128,512]{2,1,0:T(8,128)(2,1)S(1)}, bf16[1,128,512]{2,1,0:T(8,128)(2,1)}, u32[]{:S(2)}) copy-start(bf16[1,128,512]{2,1,0:T(8,128)(2,1)} %param.38) | copy-start | bytes 393220
  0.7 11.0 %collective-permute-start.1 = (bf16[1,3,2048]{2,1,0:T(4,128)(2,1)}, bf16[1,3,2048]{2,1,0:T(4,128)(2,1)S(1)}, u32[]{:S(2)}, u32[]{:S(2)}) collective-permute-start(bf16[1,3,2048]{2,1,0:T(4,128)(2,1)} %param.36), channel_id=1, source_target_pairs={{0,2},{1,3},{2,4},{3,5},{4,6},{5,7},{6,8},{7,9},{8,10},{9,11},{10,... | collective-permute-start | bytes 36872 | tf_op jit(solution)/shard_map/ppermute | solution.py:20
  3.7 10.8 %collective-permute-start = (bf16[1,3,2048]{2,1,0:T(4,128)(2,1)}, bf16[1,3,2048]{2,1,0:T(4,128)(2,1)S(1)}, u32[]{:S(2)}, u32[]{:S(2)}) collective-permute-start(bf16[1,3,2048]{2,1,0:T(4,128)(2,1)} %param.36), channel_id=1, source_target_pairs={{0,1},{1,2},{2,3},{3,4},{4,5},{5,6},{6,7},{7,8},{8,9},{9,10},{10,1... | collective-permute-start | bytes 36872 | tf_op jit(solution)/shard_map/ppermute | solution.py:20
  3.7 12.3 %collective-permute-start.2 = (bf16[1,3,2048]{2,1,0:T(4,128)(2,1)}, bf16[1,3,2048]{2,1,0:T(4,128)(2,1)S(1)}, u32[]{:S(2)}, u32[]{:S(2)}) collective-permute-start(bf16[1,3,2048]{2,1,0:T(4,128)(2,1)} %param.36), channel_id=1, source_target_pairs={{0,3},{1,4},{2,5},{3,6},{4,7},{5,8},{6,9},{7,10},{8,11},{9,12},{10... | collective-permute-start | bytes 36872 | tf_op jit(solution)/shard_map/ppermute | solution.py:20
  6.4 9.6 %collective-permute-start.7 = (bf16[1,128,512]{2,1,0:T(8,128)(2,1)}, bf16[1,128,512]{2,1,0:T(8,128)(2,1)S(1)}, u32[]{:S(2)}, u32[]{:S(2)}) collective-permute-start(bf16[1,128,512]{2,1,0:T(8,128)(2,1)} %param.37), channel_id=1, source_target_pairs={{0,2},{1,3},{2,4},{3,5},{4,6},{5,7},{6,8},{7,9},{8,10},{9,11},{10,... | collective-permute-start | bytes 393224 | tf_op jit(solution)/shard_map/ppermute | solution.py:20
  8.0 9.5 %collective-permute-start.6 = (bf16[1,128,512]{2,1,0:T(8,128)(2,1)}, bf16[1,128,512]{2,1,0:T(8,128)(2,1)S(1)}, u32[]{:S(2)}, u32[]{:S(2)}) collective-permute-start(bf16[1,128,512]{2,1,0:T(8,128)(2,1)} %param.37), channel_id=1, source_target_pairs={{0,1},{1,2},{2,3},{3,4},{4,5},{5,6},{6,7},{7,8},{8,9},{9,10},{10,1... | collective-permute-start | bytes 393224 | tf_op jit(solution)/shard_map/ppermute | solution.py:20
  11.7 8.6 %collective-permute-start.8 = (bf16[1,128,512]{2,1,0:T(8,128)(2,1)}, bf16[1,128,512]{2,1,0:T(8,128)(2,1)S(1)}, u32[]{:S(2)}, u32[]{:S(2)}) collective-permute-start(bf16[1,128,512]{2,1,0:T(8,128)(2,1)} %param.37), channel_id=1, source_target_pairs={{0,3},{1,4},{2,5},{3,6},{4,7},{5,8},{6,9},{7,10},{8,11},{9,12},{10... | collective-permute-start | bytes 393224 | tf_op jit(solution)/shard_map/ppermute | solution.py:20
  14.5 68.5 %collective-permute-start.4 = (bf16[1,32,64,256]{3,2,1,0:T(8,128)(2,1)}, bf16[1,32,64,256]{3,2,1,0:T(8,128)(2,1)}, u32[]{:S(2)}, u32[]{:S(2)}) collective-permute-start(bf16[1,32,64,256]{3,2,1,0:T(8,128)(2,1)} %param.35), channel_id=1, source_target_pairs={{0,2},{1,3},{2,4},{3,5},{4,6},{5,7},{6,8},{7,9},{8,10},{9,11},{10,... | collective-permute-start | bytes 3145736 | tf_op jit(solution)/shard_map/ppermute | solution.py:20
  16.0 67.0 %collective-permute-start.3 = (bf16[1,32,64,256]{3,2,1,0:T(8,128)(2,1)}, bf16[1,32,64,256]{3,2,1,0:T(8,128)(2,1)}, u32[]{:S(2)}, u32[]{:S(2)}) collective-permute-start(bf16[1,32,64,256]{3,2,1,0:T(8,128)(2,1)} %param.35), channel_id=1, source_target_pairs={{0,1},{1,2},{2,3},{3,4},{4,5},{5,6},{6,7},{7,8},{8,9},{9,10},{10,1... | collective-permute-start | bytes 3145736 | tf_op jit(solution)/shard_map/ppermute | solution.py:20
  16.0 67.0 %collective-permute-start.5 = (bf16[1,32,64,256]{3,2,1,0:T(8,128)(2,1)}, bf16[1,32,64,256]{3,2,1,0:T(8,128)(2,1)}, u32[]{:S(2)}, u32[]{:S(2)}) collective-permute-start(bf16[1,32,64,256]{3,2,1,0:T(8,128)(2,1)} %param.35), channel_id=1, source_target_pairs={{0,3},{1,4},{2,5},{3,6},{4,7},{5,8},{6,9},{7,10},{8,11},{9,12},{10... | collective-permute-start | bytes 3145736 | tf_op jit(solution)/shard_map/ppermute | solution.py:20
  17.4 52.6 %collective-permute-start.10 = (bf16[1,128,512]{2,1,0:T(8,128)(2,1)}, bf16[1,128,512]{2,1,0:T(8,128)(2,1)S(1)}, u32[]{:S(2)}, u32[]{:S(2)}) collective-permute-start(bf16[1,128,512]{2,1,0:T(8,128)(2,1)} %param.38), channel_id=1, source_target_pairs={{0,2},{1,3},{2,4},{3,5},{4,6},{5,7},{6,8},{7,9},{8,10},{9,11},{10,... | collective-permute-start | bytes 393224 | tf_op jit(solution)/shard_map/ppermute | solution.py:20
  20.3 60.6 %collective-permute-start.9 = (bf16[1,128,512]{2,1,0:T(8,128)(2,1)}, bf16[1,128,512]{2,1,0:T(8,128)(2,1)S(1)}, u32[]{:S(2)}, u32[]{:S(2)}) collective-permute-start(bf16[1,128,512]{2,1,0:T(8,128)(2,1)} %param.38), channel_id=1, source_target_pairs={{0,1},{1,2},{2,3},{3,4},{4,5},{5,6},{6,7},{7,8},{8,9},{9,10},{10,1... | collective-permute-start | bytes 393224 | tf_op jit(solution)/shard_map/ppermute | solution.py:20
  70.1 12.2 %collective-permute-start.11 = (bf16[1,128,512]{2,1,0:T(8,128)(2,1)}, bf16[1,128,512]{2,1,0:T(8,128)(2,1)S(1)}, u32[]{:S(2)}, u32[]{:S(2)}) collective-permute-start(bf16[1,128,512]{2,1,0:T(8,128)(2,1)} %param.38), channel_id=1, source_target_pairs={{0,3},{1,4},{2,5},{3,6},{4,7},{5,8},{6,9},{7,10},{8,11},{9,12},{10... | collective-permute-start | bytes 393224 | tf_op jit(solution)/shard_map/ppermute | solution.py:20
  77.9 5.1 copy-start.15
  91.2 209.9 %copy-start.39 = (pred[2]{0:T(512)(128)(4,1)S(1)}, pred[2]{0:T(512)(128)(4,1)}, u32[]{:S(2)}) copy-start(pred[2]{0:T(512)(128)(4,1)} %get-tuple-element.520) | copy-start | bytes 10
  91.6 12.9 %copy-start.11 = (bf16[2,128,512]{2,1,0:T(8,128)(2,1)}, bf16[2,128,512]{2,1,0:T(8,128)(2,1)S(1)}, u32[]{:S(2)}) copy-start(bf16[2,128,512]{2,1,0:T(8,128)(2,1)S(1)} %get-tuple-element.808) | copy-start | bytes 786436 | tf_op jit(solution)/shard_map/while
  91.6 12.9 %copy-start.13 = (bf16[2,128,512]{2,1,0:T(8,128)(2,1)}, bf16[2,128,512]{2,1,0:T(8,128)(2,1)S(1)}, u32[]{:S(2)}) copy-start(bf16[2,128,512]{2,1,0:T(8,128)(2,1)S(1)} %get-tuple-element.804) | copy-start | bytes 786436 | tf_op jit(solution)/shard_map/while
  124.3 4.3 copy-start.5
  124.3 4.3 copy-start.40
  133.5 4.7 copy-start.18
  153.2 12.9 %copy-start.11 = (bf16[2,128,512]{2,1,0:T(8,128)(2,1)}, bf16[2,128,512]{2,1,0:T(8,128)(2,1)S(1)}, u32[]{:S(2)}) copy-start(bf16[2,128,512]{2,1,0:T(8,128)(2,1)S(1)} %get-tuple-element.808) | copy-start | bytes 786436 | tf_op jit(solution)/shard_map/while
  153.2 12.9 %copy-start.13 = (bf16[2,128,512]{2,1,0:T(8,128)(2,1)}, bf16[2,128,512]{2,1,0:T(8,128)(2,1)S(1)}, u32[]{:S(2)}) copy-start(bf16[2,128,512]{2,1,0:T(8,128)(2,1)S(1)} %get-tuple-element.804) | copy-start | bytes 786436 | tf_op jit(solution)/shard_map/while
  195.0 4.7 copy-start.18
  222.5 93.4 %collective-permute-start.15 = (f32[2,3,2048]{2,0,1:T(2,128)}, f32[2,3,2048]{2,0,1:T(2,128)S(1)}, u32[]{:S(2)}, u32[]{:S(2)}) collective-permute-start(f32[2,3,2048]{2,0,1:T(2,128)} %get-tuple-element.849), channel_id=1, source_target_pairs={{0,15},{1,0},{2,1},{3,2},{4,3},{5,4},{6,5},{7,6},{8,7},{9,8},{10,9... | collective-permute-start | bytes 147464 | tf_op jit(solution)/shard_map/ppermute | solution.py:20
  223.8 92.1 %collective-permute-start.17 = (f32[2,3,2048]{2,0,1:T(2,128)}, f32[2,3,2048]{2,0,1:T(2,128)S(1)}, u32[]{:S(2)}, u32[]{:S(2)}) collective-permute-start(f32[2,3,2048]{2,0,1:T(2,128)} %get-tuple-element.849), channel_id=1, source_target_pairs={{0,13},{1,14},{2,15},{3,0},{4,1},{5,2},{6,3},{7,4},{8,5},{9,6},{10... | collective-permute-start | bytes 147464 | tf_op jit(solution)/shard_map/ppermute | solution.py:20
  225.3 170.5 %collective-permute-start.22 = (f32[2,128,512]{1,2,0:T(8,128)}, f32[2,128,512]{1,2,0:T(8,128)}, u32[]{:S(2)}, u32[]{:S(2)}) collective-permute-start(f32[2,128,512]{1,2,0:T(8,128)} %get-tuple-element.855), channel_id=1, source_target_pairs={{0,14},{1,15},{2,0},{3,1},{4,2},{5,3},{6,4},{7,5},{8,6},{9,7},{10,... | collective-permute-start | bytes 1572872 | tf_op jit(solution)/shard_map/ppermute | solution.py:20
  227.0 168.8 %collective-permute-start.21 = (f32[2,128,512]{1,2,0:T(8,128)}, f32[2,128,512]{1,2,0:T(8,128)}, u32[]{:S(2)}, u32[]{:S(2)}) collective-permute-start(f32[2,128,512]{1,2,0:T(8,128)} %get-tuple-element.855), channel_id=1, source_target_pairs={{0,15},{1,0},{2,1},{3,2},{4,3},{5,4},{6,5},{7,6},{8,7},{9,8},{10,9... | collective-permute-start | bytes 1572872 | tf_op jit(solution)/shard_map/ppermute | solution.py:20
  301.1 276.1 %collective-permute-start.13 = (f32[2,32,64,256]{3,2,1,0:T(8,128)}, f32[2,32,64,256]{3,2,1,0:T(8,128)}, u32[]{:S(2)}, u32[]{:S(2)}) collective-permute-start(f32[2,32,64,256]{3,2,1,0:T(8,128)} %get-tuple-element.852), channel_id=1, source_target_pairs={{0,14},{1,15},{2,0},{3,1},{4,2},{5,3},{6,4},{7,5},{8,6},{9,7},{10,... | collective-permute-start | bytes 12582920 | tf_op jit(solution)/shard_map/ppermute | solution.py:20
  301.1 13.8 %copy-start.21 = (f32[2,128,512]{1,2,0:T(8,128)S(1)}, f32[2,128,512]{1,2,0:T(8,128)}, u32[]{:S(2)}) copy-start(f32[2,128,512]{1,2,0:T(8,128)} %get-tuple-element.855) | copy-start | bytes 1572868
  301.1 14.8 %copy-start.42 = (f32[2,3,2048]{2,0,1:T(2,128)S(1)}, f32[2,3,2048]{2,0,1:T(2,128)}, u32[]{:S(2)}) copy-start(f32[2,3,2048]{2,0,1:T(2,128)} %get-tuple-element.849) | copy-start | bytes 147460
  314.9 85.6 %copy-start.37 = (pred[2]{0:T(512)(128)(4,1)S(1)}, pred[2]{0:T(512)(128)(4,1)}, u32[]{:S(2)}) copy-start(pred[2]{0:T(512)(128)(4,1)} %get-tuple-element.521) | copy-start | bytes 10
  314.9 85.8 %copy-start.36 = (pred[2]{0:T(512)(128)(4,1)S(1)}, pred[2]{0:T(512)(128)(4,1)}, u32[]{:S(2)}) copy-start(pred[2]{0:T(512)(128)(4,1)} %get-tuple-element.524) | copy-start | bytes 10
  314.9 235.3 %copy-start.38 = (pred[2]{0:T(512)(128)(4,1)S(1)}, pred[2]{0:T(512)(128)(4,1)}, u32[]{:S(2)}) copy-start(pred[2]{0:T(512)(128)(4,1)} %get-tuple-element.525) | copy-start | bytes 10
  315.9 76.2 %collective-permute-start.16 = (f32[2,3,2048]{2,0,1:T(2,128)S(1)}, f32[2,3,2048]{2,0,1:T(2,128)}, u32[]{:S(2)}, u32[]{:S(2)}) collective-permute-start(f32[2,3,2048]{2,0,1:T(2,128)S(1)} %copy-done.42), channel_id=1, source_target_pairs={{0,14},{1,15},{2,0},{3,1},{4,2},{5,3},{6,4},{7,5},{8,6},{9,7},{10,... | collective-permute-start | bytes 147464 | tf_op jit(solution)/shard_map/ppermute | solution.py:20
  316.6 274.6 %collective-permute-start.12 = (f32[2,32,64,256]{3,2,1,0:T(8,128)}, f32[2,32,64,256]{3,2,1,0:T(8,128)}, u32[]{:S(2)}, u32[]{:S(2)}) collective-permute-start(f32[2,32,64,256]{3,2,1,0:T(8,128)} %get-tuple-element.852), channel_id=1, source_target_pairs={{0,15},{1,0},{2,1},{3,2},{4,3},{5,4},{6,5},{7,6},{8,7},{9,8},{10,9... | collective-permute-start | bytes 12582920 | tf_op jit(solution)/shard_map/ppermute | solution.py:20
  392.1 213.2 %collective-permute-start.14 = (f32[2,32,64,256]{3,2,1,0:T(8,128)}, f32[2,32,64,256]{3,2,1,0:T(8,128)}, u32[]{:S(2)}, u32[]{:S(2)}) collective-permute-start(f32[2,32,64,256]{3,2,1,0:T(8,128)} %get-tuple-element.852), channel_id=1, source_target_pairs={{0,13},{1,14},{2,15},{3,0},{4,1},{5,2},{6,3},{7,4},{8,5},{9,6},{10... | collective-permute-start | bytes 12582920 | tf_op jit(solution)/shard_map/ppermute | solution.py:20
  395.8 148.0 %collective-permute-start.23 = (f32[2,128,512]{1,2,0:T(8,128)S(1)}, f32[2,128,512]{1,2,0:T(8,128)S(1)}, u32[]{:S(2)}, u32[]{:S(2)}) collective-permute-start(f32[2,128,512]{1,2,0:T(8,128)S(1)} %copy-done.21), channel_id=1, source_target_pairs={{0,13},{1,14},{2,15},{3,0},{4,1},{5,2},{6,3},{7,4},{8,5},{9,6},{10... | collective-permute-start | bytes 1572872 | tf_op jit(solution)/shard_map/ppermute | solution.py:20
  395.8 153.6 %collective-permute-start.19 = (f32[2,128,512]{1,2,0:T(8,128)S(1)}, f32[2,128,512]{1,2,0:T(8,128)S(1)}, u32[]{:S(2)}, u32[]{:S(2)}) collective-permute-start(f32[2,128,512]{1,2,0:T(8,128)S(1)} %copy-done.22), channel_id=1, source_target_pairs={{0,14},{1,15},{2,0},{3,1},{4,2},{5,3},{6,4},{7,5},{8,6},{9,7},{10,... | collective-permute-start | bytes 1572872 | tf_op jit(solution)/shard_map/ppermute | solution.py:20
  543.8 5.8 copy-start.23
  543.8 15.4 %collective-permute-start.18 = (f32[2,128,512]{1,2,0:T(8,128)S(1)}, f32[2,128,512]{1,2,0:T(8,128)}, u32[]{:S(2)}, u32[]{:S(2)}) collective-permute-start(f32[2,128,512]{1,2,0:T(8,128)S(1)} %copy-done.22), channel_id=1, source_target_pairs={{0,15},{1,0},{2,1},{3,2},{4,3},{5,4},{6,5},{7,6},{8,7},{9,8},{10,9... | collective-permute-start | bytes 1572872 | tf_op jit(solution)/shard_map/ppermute | solution.py:20
  549.4 16.5 %collective-permute-start.20 = (f32[2,128,512]{1,2,0:T(8,128)S(1)}, f32[2,128,512]{1,2,0:T(8,128)}, u32[]{:S(2)}, u32[]{:S(2)}) collective-permute-start(f32[2,128,512]{1,2,0:T(8,128)S(1)} %copy-done.22), channel_id=1, source_target_pairs={{0,13},{1,14},{2,15},{3,0},{4,1},{5,2},{6,3},{7,4},{8,5},{9,6},{10... | collective-permute-start | bytes 1572872 | tf_op jit(solution)/shard_map/ppermute | solution.py:20
  550.2 5.9 copy-start.24
  557.1 11.0 %copy-start.26 = (f32[2,128,512]{2,0,1:T(2,128)S(1)}, f32[2,128,512]{2,0,1:T(2,128)}, u32[]{:S(2)}) copy-start(f32[2,128,512]{2,0,1:T(2,128)} %copy.170) | copy-start | bytes 1572868
  565.9 5.4 copy-start.27
  568.0 4.3 copy-start.28
  568.0 5.4 copy-start.29
  569.1 5.5 copy-start.30
  (46 other events, 105.4 us)
where the time goes:
time: 626 us; the launch traced here: 621 us
  waiting for transfers between devices  275 us (44%)
  matrix products  110 us (18%)
  local copies, waits for them, and re-layouts  72.2 us (12%)
  blocking collectives  71.5 us (11%)
  other arithmetic  47.1 us (8%)
  starting transfers between devices  34.5 us (6%)
  loops' own time  9.24 us (1%)
    ppermute x24, waiting for transfers between devices, from_behind(): lax.ppermute(value, axis, [(i, (i + by) % length) for i in range(length)])  275 us
    psum x1, blocking collectives, on_device(): conv_total = lax.psum(jnp.sum(g_conv, axis=0), 'dp')  71.5 us
    dot_general x16, matrix products, on_device(): jnp.einsum('ri,r...->i...', pick, member, precision=HIGHEST)  70.7 us
    ppermute x24, starting transfers between devices, from_behind(): lax.ppermute(value, axis, [(i, (i + by) % length) for i in range(length)])  34.5 us
    dynamic_slice x42, local copies, waits for them, and re-layouts, on_device(): lax.map(one_response, (token_inputs, state_in, state_out, log_decay, out_...  31.2 us
  transfers between devices with their start and end apart: 24, of which 7 were waited for; matrix products, arithmetic and copies ran while one was open for 13% of the time, Pallas kernels for 0%

commit v1 on v0

v1 whole, which is shorter than its diff:
```python
import functools
import math

import jax
import jax.numpy as jnp
from jax import lax
from jax.experimental import pallas as pl
from jax.experimental.pallas import tpu as pltpu
from jax.sharding import PartitionSpec as P

ATT_HEADS = 32
KV_HEADS = 4
ATT_DIM = 128
HEADS = 32
HEAD_DIM = 64
SPAN = 4
REPEAT = ATT_HEADS // KV_HEADS
NEG_FILL = -1e30
F32 = jnp.float32
BF16 = jnp.bfloat16

SMEM = pl.BlockSpec(memory_space=pltpu.SMEM)
VMEM = pl.BlockSpec(memory_space=pltpu.VMEM)


def shift(value, by):
    length = lax.axis_size("dp")
    return lax.ppermute(value, "dp", [(i, (i + by) % length) for i in range(length)])


def nt(a, b):
    return lax.dot_general(a, b, (((1,), (1,)), ((), ())), preferred_element_type=F32)


def tn(a, b):
    return lax.dot_general(a, b, (((0,), (0,)), ((), ())), preferred_element_type=F32)


def nn(a, b):
    return lax.dot_general(a, b, (((1,), (0,)), ((), ())), preferred_element_type=F32)


def pack_kernel(keys, values, tail, out, rows8):
    rows = keys.shape[1]
    out[0, 0:rows, :] = keys[0]
    out[1, 0:rows, :] = values[0]
    rows8[...] = jnp.zeros_like(rows8)
    rows8[5:8, :] = tail[0].astype(F32)
    for half in range(2):
        upper = rows8[:, half * 1024 : half * 1024 + 512]
        lower = rows8[:, half * 1024 + 512 : half * 1024 + 1024]
        out[half, rows : rows + 16, :] = jnp.concatenate([upper, lower], axis=0).astype(BF16)


def pack(prefix_keys, prefix_values, prefix_tail):
    rows, width = prefix_keys.shape[1:]
    return pl.pallas_call(
        pack_kernel,
        out_shape=jax.ShapeDtypeStruct((2, rows + 16, width), BF16),
        in_specs=[VMEM] * 3,
        out_specs=VMEM,
        scratch_shapes=[pltpu.VMEM((8, prefix_tail.shape[2]), F32)],
        name="pack_prefix",
    )(prefix_keys, prefix_values, prefix_tail)


def running_sum(log_decay):
    length = log_decay.shape[0]
    row = lax.broadcasted_iota(jnp.int32, (length, length), 0)
    col = lax.broadcasted_iota(jnp.int32, (length, length), 1)
    lower = (col <= row).astype(F32)
    return lax.dot_general(
        lower,
        log_decay,
        (((1,), (0,)), ((), ())),
        precision=lax.Precision.HIGHEST,
        preferred_element_type=F32,
    )


def carry_kernel(resp_length, log_decay, cotangent, read, out):
    length = log_decay.shape[1]
    width = cotangent.shape[2]
    live_to = resp_length[pl.program_id(0)]
    raised = jnp.exp(running_sum(log_decay[0]))
    live = lax.broadcasted_iota(jnp.int32, (length, 2 * HEAD_DIM), 0) < live_to
    first = lax.broadcasted_iota(jnp.int32, (length, 2 * HEAD_DIM), 1) < HEAD_DIM
    for pair in range(width // (2 * HEAD_DIM)):
        lanes = slice(pair * 2 * HEAD_DIM, (pair + 1) * 2 * HEAD_DIM)
        factor = jnp.where(first, raised[:, 2 * pair : 2 * pair + 1], raised[:, 2 * pair + 1 : 2 * pair + 2])
        factor = jnp.where(live, factor, 0.0)
        out[0, :, lanes] = (factor * cotangent[0, :, lanes].astype(F32)).astype(BF16)
    out[0, :, width:] = read[0]


def carry(resp_length, log_decay, out_cotangent, state_out):
    count, length, width = out_cotangent.shape
    heads = log_decay.shape[2]
    states = state_out.shape[2]
    return pl.pallas_call(
        carry_kernel,
        grid=(count,),
        out_shape=jax.ShapeDtypeStruct((count, length, width + states), BF16),
        in_specs=[
            SMEM,
            pl.BlockSpec((1, length, heads), lambda r: (r, 0, 0)),
            pl.BlockSpec((1, length, width), lambda r: (r, 0, 0)),
            pl.BlockSpec((1, length, states), lambda r: (r, 0, 0)),
        ],
        out_specs=pl.BlockSpec((1, length, width + states), lambda r: (r, 0, 0)),
        name="carry_cotangent",
    )(resp_length, log_decay, out_cotangent, state_out)


def distance_to(rank, owner, devices):
    gap = rank - owner
    return jnp.where(gap < 0, gap + devices, gap)


def mamba_kernel(
    devices,
    rank_ref,
    resp_prefix,
    resp_length,
    skip_gain,
    inputs,
    pack0,
    pack1,
    pack2,
    pack3,
    conv_weight,
    write,
    read,
    log_decay,
    cotangent,
    g_inputs,
    g_tail,
    g_conv,
    g_read,
    padded,
    shifted,
    tail_rows,
    inner,
):
    resp = pl.program_id(0)
    length = inputs.shape[1]
    width = inputs.shape[2]
    taps = conv_weight.shape[0]
    rank = rank_ref[0]
    live_to = resp_length[resp]
    gap = distance_to(rank, resp_prefix[2 * rank + resp], devices)
    for step, packed in enumerate((pack0, pack1, pack2, pack3)):

        @pl.when(gap == step)
        def _(packed=packed):
            for half in range(2):
                tail_rows[half] = packed[half, length : length + 16, :].astype(F32)

    for part in range(4):
        padded[0:8, part * 512 : part * 512 + 512] = tail_rows[part // 2, 8 * (part % 2) : 8 * (part % 2) + 8, :]
    padded[8 : 8 + length, :] = inputs[0].astype(F32)
    decay_sum = running_sum(log_decay[0])
    decay_rows = jnp.concatenate(
        [decay_sum, jnp.zeros((length, 128 - decay_sum.shape[1]), F32)], axis=1
    ).T
    s_index = lax.broadcasted_iota(jnp.int32, (length, length), 0)
    t_index = lax.broadcasted_iota(jnp.int32, (length, length), 1)
    causal = s_index <= t_index
    mixing = nt(write[0], read[0])
    live = lax.broadcasted_iota(jnp.int32, (length, 2 * HEAD_DIM), 0) < live_to
    first = lax.broadcasted_iota(jnp.int32, (length, 2 * HEAD_DIM), 1) < HEAD_DIM
    inner[...] = jnp.zeros_like(inner)
    for pair in range(width // (2 * HEAD_DIM)):
        lo = pair * 2 * HEAD_DIM
        lanes = slice(lo, lo + 2 * HEAD_DIM)
        weight = [conv_weight[k : k + 1, lanes] for k in range(taps)]
        mixed = weight[0] * padded[5 : 5 + length, lanes]
        for k in range(1, taps):
            mixed = mixed + weight[k] * padded[5 + k : 5 + k + length, lanes]
        gate = jax.nn.sigmoid(mixed)
        activated = (mixed * gate).astype(BF16)
        d_out = jnp.where(live, cotangent[0, :, lanes].astype(F32), 0.0)
        both = jnp.concatenate(
            [jnp.where(first, d_out, 0.0).astype(BF16), jnp.where(first, 0.0, d_out).astype(BF16)], axis=0
        )
        d_weights = nt(activated, both)
        decays = []
        for head in (2 * pair, 2 * pair + 1):
            lag = decay_rows[head : head + 1, :] - decay_sum[:, head : head + 1]
            decays.append(jnp.exp(jnp.where(causal, lag, NEG_FILL)))
        weights = jnp.concatenate([(d * mixing).astype(BF16) for d in decays], axis=1)
        inner[...] += decays[0] * d_weights[:, :length] + decays[1] * d_weights[:, length:]
        gain = jnp.where(first[0:1], skip_gain[2 * pair], skip_gain[2 * pair + 1])
        d_act = nn(weights, both) + gain * d_out
        d_mixed = d_act * (gate * (1.0 + mixed * (1.0 - gate)))
        shifted[0:8, lanes] = jnp.zeros((8, 2 * HEAD_DIM), F32)
        shifted[8 : 8 + length, lanes] = d_mixed
        shifted[8 + length : 16 + length, lanes] = jnp.zeros((8, 2 * HEAD_DIM), F32)
        total = weight[0] * shifted[11 : 11 + length, lanes]
        early = weight[0] * shifted[8:16, lanes]
        for k in range(1, taps):
            total = total + weight[k] * shifted[11 - k : 11 - k + length, lanes]
            early = early + weight[k] * shifted[8 - k : 16 - k, lanes]
        g_inputs[0, :, lanes] = total.astype(BF16)
        g_tail[0, lo // 512, :, lo % 512 : lo % 512 + 2 * HEAD_DIM] = early
        rows = [
            jnp.sum(d_mixed * padded[5 + k : 5 + k + length, lanes], axis=0, keepdims=True) for k in range(taps)
        ]
        rows = jnp.concatenate(rows, axis=0)

        @pl.when(resp == 0)
        def _(rows=rows, lanes=lanes):
            g_conv[:, lanes] = rows

        @pl.when(resp > 0)
        def _(rows=rows, lanes=lanes):
            g_conv[:, lanes] += rows

    g_read[0] = tn(inner[...].astype(BF16), write[0])


def mamba(rank, resp_prefix, resp_length, skip_gain, inputs, packs, conv_weight, write, read, log_decay, cotangent, devices):
    count, length, width = inputs.shape
    heads = log_decay.shape[2]
    states = read.shape[2]
    taps = conv_weight.shape[0]
    whole = pl.BlockSpec(packs[0].shape, lambda r: (0, 0, 0))
    return pl.pallas_call(
        functools.partial(mamba_kernel, devices),
        grid=(count,),
        out_shape=[
            jax.ShapeDtypeStruct((count, length, width), BF16),
            jax.ShapeDtypeStruct((count, 4, 8, 512), F32),
            jax.ShapeDtypeStruct((taps, width), F32),
            jax.ShapeDtypeStruct((count, length, states), F32),
        ],
        in_specs=[
            SMEM,
            SMEM,
            SMEM,
            SMEM,
            pl.BlockSpec((1, length, width), lambda r: (r, 0, 0)),
            whole,
            whole,
            whole,
            whole,
            pl.BlockSpec((taps, width), lambda r: (0, 0)),
            pl.BlockSpec((1, length, states), lambda r: (r, 0, 0)),
            pl.BlockSpec((1, length, states), lambda r: (r, 0, 0)),
            pl.BlockSpec((1, length, heads), lambda r: (r, 0, 0)),
            pl.BlockSpec((1, length, width), lambda r: (r, 0, 0)),
        ],
        out_specs=[
            pl.BlockSpec((1, length, width), lambda r: (r, 0, 0)),
            pl.BlockSpec((1, 4, 8, 512), lambda r: (r, 0, 0, 0)),
            pl.BlockSpec((taps, width), lambda r: (0, 0)),
            pl.BlockSpec((1, length, states), lambda r: (r, 0, 0)),
        ],
        scratch_shapes=[
            pltpu.VMEM((length + 8, width), F32),
            pltpu.VMEM((length + 16, width), F32),
            pltpu.VMEM((2, 16, 512), F32),
            pltpu.VMEM((length, length), F32),
        ],
        compiler_params=pltpu.CompilerParams(vmem_limit_bytes=32 * 2**20),
        cost_estimate=pl.CostEstimate(flops=2 * 10**9, bytes_accessed=8 * 2**20, transcendentals=10**6),
        name="mamba_grads",
    )(rank, resp_prefix, resp_length, skip_gain, inputs, *packs, conv_weight, write, read, log_decay, cotangent)


def attention_kernel(
    devices,
    rank_ref,
    resp_prefix,
    resp_length,
    prefix_length,
    queries,
    cotangent,
    own_keys,
    own_values,
    pack0,
    pack1,
    pack2,
    pack3,
    g_tail,
    g_queries,
    back0,
    back1,
    back2,
    back3,
    keys,
    values,
    kept,
):
    resp = pl.program_id(1)
    length = queries.shape[1]
    rows = keys.shape[0] - length
    rank = rank_ref[0]
    prefix = resp_prefix[2 * rank + resp]
    pref_len = prefix_length[prefix]
    live_to = resp_length[resp]
    scale = 1.0 / math.sqrt(ATT_DIM)
    gap = distance_to(rank, prefix, devices)
    for step, packed in enumerate((pack0, pack1, pack2, pack3)):

        @pl.when(gap == step)
        def _(packed=packed):
            keys[0:rows, :] = packed[0, 0:rows, :]
            values[0:rows, :] = packed[1, 0:rows, :]

    keys[rows : rows + length, :] = own_keys[0]
    values[rows : rows + length, :] = own_values[0]
    j_index = lax.broadcasted_iota(jnp.int32, (rows + length, 2 * length), 0)
    t_index = lax.broadcasted_iota(jnp.int32, (rows + length, 2 * length), 1)
    t_index = jnp.where(t_index >= length, t_index - length, t_index)
    bound = jnp.where(j_index < rows, pref_len, t_index + rows + 1)
    bias = jnp.where(j_index < bound, 0.0, NEG_FILL)
    live = lax.broadcasted_iota(jnp.int32, (length, ATT_DIM), 0) < live_to
    all_keys = keys[...]
    all_values = values[...]
    g_keys = jnp.zeros((rows, ATT_DIM), F32)
    g_values = jnp.zeros((rows, ATT_DIM), F32)
    for duo in range(REPEAT // 2):
        spans = [slice((2 * duo + i) * ATT_DIM, (2 * duo + i + 1) * ATT_DIM) for i in range(2)]
        query = jnp.concatenate([queries[0, :, span] for span in spans], axis=0)
        d_out = jnp.concatenate(
            [jnp.where(live, cotangent[0, :, span].astype(F32), 0.0).astype(BF16) for span in spans], axis=0
        )
        scores = nt(all_keys, query) * scale + bias
        top = jnp.max(scores, axis=0, keepdims=True)
        raised = jnp.exp(scores - top)
        probs = raised * (1.0 / jnp.sum(raised, axis=0, keepdims=True))
        probs_low = probs.astype(BF16)
        d_probs = nt(all_values, d_out)
        delta = jnp.sum(probs_low.astype(F32) * d_probs, axis=0, keepdims=True)
        d_scores = (probs * ((d_probs - delta) * scale)).astype(BF16)
        g_query = tn(d_scores, all_keys)
        for i, span in enumerate(spans):
            g_queries[0, :, span] = g_query[i * length : (i + 1) * length].astype(BF16)
        g_keys = g_keys + nn(d_scores[0:rows], query)
        g_values = g_values + nn(probs_low[0:rows], d_out)

    @pl.when(resp == 0)
    def _():
        kept[0] = g_keys
        kept[1] = g_values

    @pl.when(resp == 1)
    def _():
        before = distance_to(rank, resp_prefix[2 * rank], devices)
        for step, back in enumerate((back0, back1, back2, back3)):
            one = jnp.where(before == step, 1.0, 0.0)
            two = jnp.where(gap == step, 1.0, 0.0)
            back[0, 0:rows, :] = (kept[0] * one + g_keys * two).astype(back.dtype)
            back[1, 0:rows, :] = (kept[1] * one + g_values * two).astype(back.dtype)
            for half in range(2):
                upper = g_tail[0, 2 * half] * one + g_tail[1, 2 * half] * two
                lower = g_tail[0, 2 * half + 1] * one + g_tail[1, 2 * half + 1] * two
                back[half, rows : rows + 16, :] = jnp.concatenate([upper, lower], axis=0).astype(back.dtype)


def attention(rank, resp_prefix, resp_length, prefix_length, queries, cotangent, own_keys, own_values, packs, g_tail, devices):
    count, length, width = queries.shape
    rows = packs[0].shape[1] - 16
    group = REPEAT * ATT_DIM
    packed = pl.BlockSpec((2, rows + 16, ATT_DIM), lambda h, r: (0, 0, h))
    back = (2, rows + 16, KV_HEADS * ATT_DIM)
    return pl.pallas_call(
        functools.partial(attention_kernel, devices),
        grid=(KV_HEADS, count),
        out_shape=[
            jax.ShapeDtypeStruct((count, length, width), BF16),
            jax.ShapeDtypeStruct(back, F32),
            jax.ShapeDtypeStruct(back, BF16),
            jax.ShapeDtypeStruct(back, BF16),
            jax.ShapeDtypeStruct(back, BF16),
        ],
        in_specs=[
            SMEM,
            SMEM,
            SMEM,
            SMEM,
            pl.BlockSpec((1, length, group), lambda h, r: (r, 0, h)),
            pl.BlockSpec((1, length, group), lambda h, r: (r, 0, h)),
            pl.BlockSpec((1, length, ATT_DIM), lambda h, r: (r, 0, h)),
            pl.BlockSpec((1, length, ATT_DIM), lambda h, r: (r, 0, h)),
            packed,
            packed,
            packed,
            packed,
            pl.BlockSpec((count, 4, 8, ATT_DIM), lambda h, r: (0, 0, 0, h)),
        ],
        out_specs=[
            pl.BlockSpec((1, length, group), lambda h, r: (r, 0, h)),
            packed,
            packed,
            packed,
            packed,
        ],
        scratch_shapes=[
            pltpu.VMEM((rows + length, ATT_DIM), BF16),
            pltpu.VMEM((rows + length, ATT_DIM), BF16),
            pltpu.VMEM((2, rows, ATT_DIM), F32),
        ],
        compiler_params=pltpu.CompilerParams(vmem_limit_bytes=32 * 2**20),
        cost_estimate=pl.CostEstimate(flops=4 * 10**9, bytes_accessed=8 * 2**20, transcendentals=2 * 10**6),
        name="attention_grads",
    )(rank, resp_prefix, resp_length, prefix_length, queries, cotangent, own_keys, own_values, *packs, g_tail)


def owner_kernel(devices, rank_ref, resp_prefix, state, car0, car1, car2, car3, g_state, dr0, dr1, dr2, dr3, total):
    rank = rank_ref[0]
    width = state.shape[0]
    chunk = 512
    total[...] = jnp.zeros_like(total)
    for step, (carried, d_read) in enumerate(zip((car0, car1, car2, car3), (dr0, dr1, dr2, dr3))):
        sender = rank + step
        sender = jnp.where(sender >= devices, sender - devices, sender)
        for resp in range(2):
            mine = resp_prefix[2 * sender + resp] == rank

            @pl.when(mine)
            def _(carried=carried, d_read=d_read, resp=resp):
                read = carried[resp, :, width:]
                acc = None
                for at in range(0, width, chunk):
                    piece = carried[resp, :, at : at + chunk]
                    term = nn(piece, state[at : at + chunk, :])
                    acc = term if acc is None else acc + term
                    total[at : at + chunk, :] += tn(piece, read)
                d_read[resp] = acc.astype(d_read.dtype)

            @pl.when(jnp.logical_not(mine))
            def _(d_read=d_read, resp=resp):
                d_read[resp] = jnp.zeros(d_read.shape[1:], d_read.dtype)

    g_state[...] = total[...].astype(BF16)


def owner(rank, resp_prefix, state, carried, devices):
    width, states = state.shape
    count, length = carried[0].shape[:2]
    return pl.pallas_call(
        functools.partial(owner_kernel, devices),
        out_shape=[jax.ShapeDtypeStruct((width, states), BF16), jax.ShapeDtypeStruct((count, length, states), F32)]
        + [jax.ShapeDtypeStruct((count, length, states), BF16)] * 3,
        in_specs=[SMEM, SMEM] + [VMEM] * 5,
        out_specs=[VMEM] * 5,
        scratch_shapes=[pltpu.VMEM((width, states), F32)],
        compiler_params=pltpu.CompilerParams(vmem_limit_bytes=32 * 2**20),
        cost_estimate=pl.CostEstimate(flops=2 * 10**9, bytes_accessed=8 * 2**20, transcendentals=0),
        name="owner_state",
    )(rank, resp_prefix, state, *carried)


def sum_kernel(back0, back1, back2, back3, g_keys, g_values, g_tail):
    rows = g_keys.shape[1]
    for half, out in enumerate((g_keys, g_values)):
        total = back0[half]
        for back in (back1, back2, back3):
            total = total + back[half].astype(F32)
        out[0] = total[0:rows]
        for part in range(2):
            lo = half * 1024 + part * 512
            g_tail[0, :, lo : lo + 512] = total[rows + 8 * part : rows + 8 * part + 3]


def sum_back(backs, tail_shape):
    rows = backs[0].shape[1] - 16
    width = backs[0].shape[2]
    return pl.pallas_call(
        sum_kernel,
        out_shape=[
            jax.ShapeDtypeStruct((1, rows, width), F32),
            jax.ShapeDtypeStruct((1, rows, width), F32),
            jax.ShapeDtypeStruct(tail_shape, F32),
        ],
        in_specs=[VMEM] * 4,
        out_specs=[VMEM] * 3,
        name="sum_prefix",
    )(*backs)


def all_sum(value):
    length = lax.axis_size("dp")
    if length & (length - 1):
        return lax.psum(value, "dp")
    by = 1
    while by < length:
        value = value + lax.ppermute(value, "dp", [(i, i ^ by) for i in range(length)])
        by *= 2
    return value


def on_device(
    token_inputs,
    state_in,
    state_out,
    log_decay,
    skip_gain,
    conv_weight,
    out_cotangent,
    queries,
    own_keys,
    own_values,
    attn_cotangent,
    resp_length,
    resp_prefix,
    prefix_state,
    prefix_tail,
    prefix_keys,
    prefix_values,
    prefix_length,
):
    devices = lax.axis_size("dp")
    rank = lax.axis_index("dp").astype(jnp.int32).reshape(1)
    count, length, _ = token_inputs.shape
    states = state_out.shape[3]
    write = state_in.reshape(count, length, states)
    read = state_out.reshape(count, length, states)
    state = prefix_state.reshape(-1, states)

    packed = pack(prefix_keys, prefix_values, prefix_tail)
    packs = [packed] + [shift(packed, by) for by in range(1, SPAN)]
    carried = carry(resp_length, log_decay, out_cotangent, read)
    carries = [carried] + [shift(carried, -by) for by in range(1, SPAN)]
    g_inputs, g_tail, g_conv, g_read = mamba(
        rank, resp_prefix, resp_length, skip_gain, token_inputs, packs, conv_weight, write, read, log_decay, out_cotangent, devices
    )
    g_queries, *backs = attention(
        rank, resp_prefix, resp_length, prefix_length, queries, attn_cotangent, own_keys, own_values, packs, g_tail, devices
    )
    backs = [backs[0]] + [shift(backs[by], -by) for by in range(1, SPAN)]
    g_state, *reads = owner(rank, resp_prefix, state, carries, devices)
    for by in range(SPAN):
        g_read = g_read + (reads[by] if by == 0 else shift(reads[by], by).astype(F32))
    g_prefix_keys, g_prefix_values, g_prefix_tail = sum_back(backs, prefix_tail.shape)
    token_total = count * length * devices
    grad_conv = all_sum(g_conv) * (1.0 / math.sqrt(token_total))
    return (
        g_inputs,
        g_read.astype(BF16).reshape(state_out.shape),
        g_queries,
        g_state.reshape(prefix_state.shape),
        g_prefix_tail,
        g_prefix_keys,
        g_prefix_values,
        grad_conv,
    )


def solution(mesh):
    split = ("groups", "dp")
    placed = (
        P(split, None, None),
        P(split, None, None, None),
        P(split, None, None, None),
        P(split, None, None),
        P(),
        P(),
        P(split, None, None),
        P(split, None, None),
        P(split, None, None),
        P(split, None, None),
        P(split, None, None),
        P(split),
        P("groups"),
        P(split, None, None, None),
        P(split, None, None),
        P(split, None, None),
        P(split, None, None),
        P("groups"),
    )
    return jax.shard_map(
        on_device,
        mesh=mesh,
        in_specs=placed,
        out_specs=(
            P(split, None, None),
            P(split, None, None, None),
            P(split, None, None),
            P(split, None, None, None),
            P(split, None, None),
            P(split, None, None),
            P(split, None, None),
            P("groups", None),
        ),
        check_vma=False,
    )
```

time: 626 us -> 113 us (0.18)
  the two profiles are of different devices: /device:TPU:0 before, /device:TPU:1 now
where the time goes in v1:
time: 113 us
  Pallas kernels  42.6 us (38%)
  waiting for transfers between devices  34.9 us (31%)
  starting transfers between devices  27.5 us (24%)
  local copies, waits for them, and re-layouts  5.85 us (5%)
  other arithmetic  1.38 us (1%)
    ppermute x12, starting transfers between devices, shift(): lax.ppermute(value, 'dp', [(i, (i + by) % length) for i in range(length)])  26 us
    ppermute x12, waiting for transfers between devices, shift(): lax.ppermute(value, 'dp', [(i, (i + by) % length) for i in range(length)])  20.3 us
    pallas_call x1, Pallas kernels, attention(): pl.pallas_call(functools.partial(attention_kernel, devices), grid=(KV_HEA...  18.1 us
    ppermute x4, waiting for transfers between devices, all_sum(): lax.ppermute(value, 'dp', [(i, i ^ by) for i in range(length)])  14.6 us
    pallas_call x1, Pallas kernels, mamba(): pl.pallas_call(functools.partial(mamba_kernel, devices), grid=(count,), o...  12.4 us
    unnamed x44, local copies, waits for them, and re-layouts  5.85 us
    pallas_call x1, Pallas kernels, owner(): pl.pallas_call(functools.partial(owner_kernel, devices), out_shape=[jax.S...  4.35 us
    pallas_call x1, Pallas kernels, carry(): pl.pallas_call(carry_kernel, grid=(count,), out_shape=jax.ShapeDtypeStruc...  3.84 us
  transfers between devices with their start and end apart: 16, of which 7 were waited for; matrix products, arithmetic and copies ran while one was open for 3% of the time, Pallas kernels for 36%

profile of v1, /device:TPU:1, one launch (start us, length us, event | category | flops | bytes accessed | tf_op | source)
XLA Modules:
  0.0 113.0 jit_solution(6288967430628969096)
XLA Ops:
  0.6 1.7 %pack_prefix.1.pack0 = bf16[2,144,512]{2,1,0:T(8,128)(2,1)} custom-call(bf16[1,128,512]{2,1,0:T(8,128)(2,1)} %keys.1, bf16[1,128,512]{2,1,0:T(8,128)(2,1)} %values.1, bf16[1,3,2048]{2,1,0:T(4,128)(2,1)} %tail.1), custom_call_target="tpu_custom_call" | custom-call | tf_op jit(solution)/shard_map/pack_prefix/pallas_call | solution.py:57
  2.4 2.7 %collective-permute-start.2 = (bf16[2,144,512]{2,1,0:T(8,128)(2,1)}, bf16[2,144,512]{2,1,0:T(8,128)(2,1)S(1)}, u32[]{:S(2)}, u32[]{:S(2)}) collective-permute-start(bf16[2,144,512]{2,1,0:T(8,128)(2,1)} %pack_prefix.1.pack0), channel_id=1, source_target_pairs={{0,3},{1,4},{2,5},{3,6},{4,7},{5,8},{6,9},{7,10},{8,11},{9,12},{10... | collective-permute-start | bytes 884744 | tf_op jit(solution)/shard_map/ppermute | solution.py:28
  5.0 1.5 %copy.26.log_decay = f32[2,128,32]{2,1,0:T(8,128)} copy(f32[2,128,32]{1,2,0:T(8,128)} %param.21) | data formatting | bytes 65536 | tf_op args[3]
  6.6 0.0 copy-start.6
  6.6 0.0 copy-start.13
  6.6 0.0 copy-start.14
  6.6 0.0 copy-start.15
  6.6 0.0 copy-start.17
  6.6 3.8 %carry_cotangent.1.car0 = bf16[2,128,2304]{2,1,0:T(8,128)(2,1)} custom-call(s32[2]{0:T(128)} %resp_length.5, f32[2,128,32]{2,1,0:T(8,128)} %copy.26.log_decay, bf16[2,128,2048]{2,1,0:T(8,128)(2,1)} %cotangent.4, bf16[2,128,256]{2,1,0:T(8,128)(2,1)} %bitcast.9), custom_call_target="tpu_custom_call" | custom-call | tf_op jit(solution)/shard_map/carry_cotangent/pallas_call | solution.py:100
  10.5 3.0 %collective-permute-start.5 = (bf16[2,128,2304]{2,1,0:T(8,128)(2,1)}, bf16[2,128,2304]{2,1,0:T(8,128)(2,1)S(1)}, u32[]{:S(2)}, u32[]{:S(2)}) collective-permute-start(bf16[2,128,2304]{2,1,0:T(8,128)(2,1)} %carry_cotangent.1.car0), channel_id=1, source_target_pairs={{0,13},{1,14},{2,15},{3,0},{4,1},{5,2},{6,3},{7,4},{8,5},{9,6},{10... | collective-permute-start | bytes 3538952 | tf_op jit(solution)/shard_map/ppermute | solution.py:28
  13.4 1.2 %collective-permute-start.4 = (bf16[2,128,2304]{2,1,0:T(8,128)(2,1)}, bf16[2,128,2304]{2,1,0:T(8,128)(2,1)}, u32[]{:S(2)}, u32[]{:S(2)}) collective-permute-start(bf16[2,128,2304]{2,1,0:T(8,128)(2,1)} %carry_cotangent.1.car0), channel_id=1, source_target_pairs={{0,14},{1,15},{2,0},{3,1},{4,2},{5,3},{6,4},{7,5},{8,6},{9,7},{10,... | collective-permute-start | bytes 3538952 | tf_op jit(solution)/shard_map/ppermute | solution.py:28
  14.6 1.0 collective-permute-start.3
  15.6 0.0 collective-permute-start.1
  15.6 0.0 collective-permute-done.2.pack3
  15.6 2.2 %collective-permute-start = (bf16[2,144,512]{2,1,0:T(8,128)(2,1)S(1)}, bf16[2,144,512]{2,1,0:T(8,128)(2,1)}, u32[]{:S(2)}, u32[]{:S(2)}) collective-permute-start(bf16[2,144,512]{2,1,0:T(8,128)(2,1)S(1)} %copy-done.4), channel_id=1, source_target_pairs={{0,1},{1,2},{2,3},{3,4},{4,5},{5,6},{6,7},{7,8},{8,9},{9,10},{10,1... | collective-permute-start | bytes 884744 | tf_op jit(solution)/shard_map/ppermute | solution.py:28
  17.8 9.3 %collective-permute-done.1.pack2 = bf16[2,144,512]{2,1,0:T(8,128)(2,1)} collective-permute-done((bf16[2,144,512]{2,1,0:T(8,128)(2,1)S(1)}, bf16[2,144,512]{2,1,0:T(8,128)(2,1)}, u32[]{:S(2)}, u32[]{:S(2)}) %collective-permute-start.1) | collective-permute-done | bytes 294944 | tf_op jit(solution)/shard_map/ppermute | solution.py:28
  27.2 7.7 %collective-permute-done.pack1 = bf16[2,144,512]{2,1,0:T(8,128)(2,1)} collective-permute-done((bf16[2,144,512]{2,1,0:T(8,128)(2,1)S(1)}, bf16[2,144,512]{2,1,0:T(8,128)(2,1)}, u32[]{:S(2)}, u32[]{:S(2)}) %collective-permute-start) | collective-permute-done | bytes 294944 | tf_op jit(solution)/shard_map/ppermute | solution.py:28
  35.0 0.0 copy-start.9
  35.0 1.2 %copy-done.9 = bf16[2,128,2048]{2,1,0:T(8,128)(2,1)S(1)} copy-done((bf16[2,128,2048]{2,1,0:T(8,128)(2,1)S(1)}, bf16[2,128,2048]{2,1,0:T(8,128)(2,1)}, u32[]{:S(2)}) %copy-start.9) | copy-done | bytes 1048600
  36.2 0.0 copy-start.16
  36.2 12.4 %mamba_grads.1 = (bf16[2,128,2048]{2,1,0:T(8,128)(2,1)}, f32[2,4,8,512]{3,2,1,0:T(8,128)S(1)}, f32[4,2048]{1,0:T(4,128)S(1)}, f32[2,128,256]{2,1,0:T(8,128)S(1)}) custom-call(s32[1]{0:T(128)} %bitcast.rank_ref, s32[32]{0:T(128)S(1)} %copy-done.17, s32[2]{0:T(128)S(1)} %copy-done.6, f32[32]{0:T(128)S(1)} %copy-done.15, bf16[2,128,2048]{2,1,0:T(8,128)(2,1)S(1)} %copy-done.9, ...), custom_call_target="tpu_custom_call" | custom-call | flops 2000000000 | bytes 8388608 | tf_op jit(solution)/shard_map/mamba_grads/pallas_call | solution.py:228
  48.7 0.0 copy-start.10
  48.7 18.1 %attention_grads.1 = (bf16[2,128,4096]{2,1,0:T(8,128)(2,1)}, f32[2,144,512]{2,1,0:T(8,128)S(1)}, bf16[2,144,512]{2,1,0:T(8,128)(2,1)S(1)}, bf16[2,144,512]{2,1,0:T(8,128)(2,1)S(1)}, bf16[2,144,512]{2,1,0:T(8,128)(2,1)S(1)}) custom-call(s32[1]{0:T(128)} %bitcast.rank_ref, s32[32]{0:T(128)S(1)} %copy-done.17, s32[2]{0:T(128)S(1)} %copy-done.6, ...), custom_call_target="tpu_custom_call" | custom-call | flops 4000000000 | bytes 8388608 | tf_op jit(solution)/shard_map/attention_grads/pallas_call | solution.py:368
  66.8 0.8 copy-done.2
  67.6 4.8 %collective-permute-start.9 = (bf16[2,144,512]{2,1,0:T(8,128)(2,1)S(1)}, bf16[2,144,512]{2,1,0:T(8,128)(2,1)S(1)}, u32[]{:S(2)}, u32[]{:S(2)}) collective-permute-start(bf16[2,144,512]{2,1,0:T(8,128)(2,1)S(1)} %get-tuple-element.35), channel_id=1, source_target_pairs={{0,15},{1,0},{2,1},{3,2},{4,3},{5,4},{6,5},{7,6},{8,7},{9,8},{10,9... | collective-permute-start | bytes 884744 | tf_op jit(solution)/shard_map/ppermute | solution.py:28
  72.4 0.0 collective-permute-start.12
  72.4 1.3 %collective-permute-done.12 = f32[4,2048]{1,0:T(4,128)S(1)} collective-permute-done((f32[4,2048]{1,0:T(4,128)S(1)}, f32[4,2048]{1,0:T(4,128)S(1)}, u32[]{:S(2)}, u32[]{:S(2)}) %collective-permute-start.12) | collective-permute-done | bytes 32800 | tf_op jit(solution)/shard_map/ppermute | solution.py:490
  73.6 0.1 collective-permute-start.13
  73.7 6.1 %collective-permute-done.13 = f32[4,2048]{1,0:T(4,128)S(1)} collective-permute-done((f32[4,2048]{1,0:T(4,128)S(1)}, f32[4,2048]{1,0:T(4,128)S(1)}, u32[]{:S(2)}, u32[]{:S(2)}) %collective-permute-start.13) | collective-permute-done | bytes 32800 | tf_op jit(solution)/shard_map/ppermute | solution.py:490
  79.8 1.4 %collective-permute-start.14 = (f32[4,2048]{1,0:T(4,128)S(1)}, f32[4,2048]{1,0:T(4,128)S(1)}, u32[]{:S(2)}, u32[]{:S(2)}) collective-permute-start(f32[4,2048]{1,0:T(4,128)S(1)} %add.29), channel_id=1, source_target_pairs={{0,4},{1,5},{2,6},{3,7},{4,0},{5,1},{6,2},{7,3},{8,12},{9,13},{10,... | collective-permute-start | bytes 98312 | tf_op jit(solution)/shard_map/ppermute | solution.py:490
  81.2 1.5 %collective-permute-done.14 = f32[4,2048]{1,0:T(4,128)S(1)} collective-permute-done((f32[4,2048]{1,0:T(4,128)S(1)}, f32[4,2048]{1,0:T(4,128)S(1)}, u32[]{:S(2)}, u32[]{:S(2)}) %collective-permute-start.14) | collective-permute-done | bytes 32800 | tf_op jit(solution)/shard_map/ppermute | solution.py:490
  82.6 5.3 %collective-permute-start.10 = (bf16[2,144,512]{2,1,0:T(8,128)(2,1)S(1)}, bf16[2,144,512]{2,1,0:T(8,128)(2,1)S(1)}, u32[]{:S(2)}, u32[]{:S(2)}) collective-permute-start(bf16[2,144,512]{2,1,0:T(8,128)(2,1)S(1)} %get-tuple-element.36), channel_id=1, source_target_pairs={{0,14},{1,15},{2,0},{3,1},{4,2},{5,3},{6,4},{7,5},{8,6},{9,7},{10,... | collective-permute-start | bytes 884744 | tf_op jit(solution)/shard_map/ppermute | solution.py:28
  88.0 0.0 collective-permute-done.5.car3
  88.0 1.5 %collective-permute-start.11 = (bf16[2,144,512]{2,1,0:T(8,128)(2,1)S(1)}, bf16[2,144,512]{2,1,0:T(8,128)(2,1)S(1)}, u32[]{:S(2)}, u32[]{:S(2)}) collective-permute-start(bf16[2,144,512]{2,1,0:T(8,128)(2,1)S(1)} %get-tuple-element.37), channel_id=1, source_target_pairs={{0,13},{1,14},{2,15},{3,0},{4,1},{5,2},{6,3},{7,4},{8,5},{9,6},{10... | collective-permute-start | bytes 884744 | tf_op jit(solution)/shard_map/ppermute | solution.py:28
  89.5 0.0 collective-permute-done.4.car2
  89.6 4.3 %owner_state.1 = (bf16[2048,256]{1,0:T(8,128)(2,1)}, f32[2,128,256]{2,1,0:T(8,128)S(1)}, bf16[2,128,256]{2,1,0:T(8,128)(2,1)S(1)}, bf16[2,128,256]{2,1,0:T(8,128)(2,1)S(1)}, bf16[2,128,256]{2,1,0:T(8,128)(2,1)S(1)}) custom-call(s32[1]{0:T(128)} %bitcast.rank_ref, s32[32]{0:T(128)S(1)} %copy-done.17, bf16[2048,256]{1,0:T(8,128)(2,1)S(1)} %bitcast.11, ...), custom_call_target="tpu_custom_call" | custom-call | flops 2000000000 | bytes 8388608 | tf_op jit(solution)/shard_map/owner_state/pallas_call | solution.py:443
  93.9 5.8 %collective-permute-done.15 = f32[4,2048]{1,0:T(4,128)S(1)} collective-permute-done((f32[4,2048]{1,0:T(4,128)S(1)}, f32[4,2048]{1,0:T(4,128)S(1)}, u32[]{:S(2)}, u32[]{:S(2)}) %collective-permute-start.15) | collective-permute-done | bytes 32800 | tf_op jit(solution)/shard_map/ppermute | solution.py:490
  99.7 0.0 collective-permute-start.7
  99.7 0.0 collective-permute-done.9.back1
  99.7 4.3 %collective-permute-start.8 = (bf16[2,128,256]{2,1,0:T(8,128)(2,1)S(1)}, bf16[2,128,256]{2,1,0:T(8,128)(2,1)S(1)}, u32[]{:S(2)}, u32[]{:S(2)}) collective-permute-start(bf16[2,128,256]{2,1,0:T(8,128)(2,1)S(1)} %get-tuple-element.30), channel_id=1, source_target_pairs={{0,3},{1,4},{2,5},{3,6},{4,7},{5,8},{6,9},{7,10},{8,11},{9,12},{10... | collective-permute-start | bytes 393224 | tf_op jit(solution)/shard_map/ppermute | solution.py:28
  104.1 0.6 add_multiply_fusion
  104.7 0.0 collective-permute-done.10.back2
  104.7 0.7 copy-done.19
  105.4 0.1 copy-done.20
  105.5 2.2 %sum_prefix.1 = (f32[1,128,512]{2,1,0:T(8,128)}, f32[1,128,512]{2,1,0:T(8,128)}, f32[1,3,2048]{2,1,0:T(4,128)}) custom-call(f32[2,144,512]{2,1,0:T(8,128)} %copy-done.2, bf16[2,144,512]{2,1,0:T(8,128)(2,1)} %copy-done.18, bf16[2,144,512]{2,1,0:T(8,128)(2,1)} %copy-done.19, bf16[2,144,512]{2,1,0:T(8,128)(2,1)} %copy-done.20), custom_call_target="tpu_custom_call" | custom-call | tf_op jit(solution)/shard_map/sum_prefix/pallas_call | solution.py:471
  107.7 1.4 %copy.29 = f32[1,3,2048]{2,0,1:T(1,128)} copy(f32[1,3,2048]{2,1,0:T(4,128)} %get-tuple-element.46) | data formatting | bytes 49152
  109.1 3.2 %collective-permute-done.8 = bf16[2,128,256]{2,1,0:T(8,128)(2,1)S(1)} collective-permute-done((bf16[2,128,256]{2,1,0:T(8,128)(2,1)S(1)}, bf16[2,128,256]{2,1,0:T(8,128)(2,1)S(1)}, u32[]{:S(2)}, u32[]{:S(2)}) %collective-permute-start.8) | collective-permute-done | bytes 131104 | tf_op jit(solution)/shard_map/ppermute | solution.py:28
  112.3 0.7 fusion
  (39 shorter events, 0.1 us)
Async XLA Ops:
  2.4 13.3 %collective-permute-start.2 = (bf16[2,144,512]{2,1,0:T(8,128)(2,1)}, bf16[2,144,512]{2,1,0:T(8,128)(2,1)S(1)}, u32[]{:S(2)}, u32[]{:S(2)}) collective-permute-start(bf16[2,144,512]{2,1,0:T(8,128)(2,1)} %pack_prefix.1.pack0), channel_id=1, source_target_pairs={{0,3},{1,4},{2,5},{3,6},{4,7},{5,8},{6,9},{7,10},{8,11},{9,12},{10... | collective-permute-start | bytes 884744 | tf_op jit(solution)/shard_map/ppermute | solution.py:28
  6.6 9.0 %copy-start.4 = (bf16[2,144,512]{2,1,0:T(8,128)(2,1)S(1)}, bf16[2,144,512]{2,1,0:T(8,128)(2,1)}, u32[]{:S(2)}) copy-start(bf16[2,144,512]{2,1,0:T(8,128)(2,1)} %pack_prefix.1.pack0) | copy-start | bytes 884740
  6.6 28.4 %copy-start.1 = (bf16[2,128,2048]{2,1,0:T(8,128)(2,1)S(1)}, bf16[2,128,2048]{2,1,0:T(8,128)(2,1)}, u32[]{:S(2)}) copy-start(bf16[2,128,2048]{2,1,0:T(8,128)(2,1)} %cotangent.4) | copy-start | bytes 3145732
  6.6 28.4 %copy-start.3 = (f32[2,128,32]{2,1,0:T(8,128)S(1)}, f32[2,128,32]{2,1,0:T(8,128)}, u32[]{:S(2)}) copy-start(f32[2,128,32]{2,1,0:T(8,128)} %copy.26.log_decay) | copy-start | bytes 98308
  6.6 28.4 %copy-start.5 = (bf16[2,128,1,256]{3,1,2,0:T(8,128)(2,1)S(1)}, bf16[2,128,1,256]{3,1,2,0:T(8,128)(2,1)}, u32[]{:S(2)}) copy-start(bf16[2,128,1,256]{3,1,2,0:T(8,128)(2,1)} %param.20) | copy-start | bytes 393220
  6.6 28.4 %copy-start.6 = (s32[2]{0:T(128)S(1)}, s32[2]{0:T(128)}, u32[]{:S(2)}) copy-start(s32[2]{0:T(128)} %resp_length.5) | copy-start | bytes 28
  6.6 28.4 %copy-start.13 = (bf16[2,128,1,256]{3,1,2,0:T(8,128)(2,1)S(1)}, bf16[2,128,1,256]{3,1,2,0:T(8,128)(2,1)}, u32[]{:S(2)}) copy-start(bf16[2,128,1,256]{3,1,2,0:T(8,128)(2,1)} %param.19) | copy-start | bytes 393220
  6.6 28.4 %copy-start.14 = (f32[4,2048]{1,0:T(4,128)S(1)}, f32[4,2048]{1,0:T(4,128)}, u32[]{:S(2)}) copy-start(f32[4,2048]{1,0:T(4,128)} %conv_weight.1) | copy-start | bytes 98308
  6.6 28.4 %copy-start.15 = (f32[32]{0:T(128)S(1)}, f32[32]{0:T(128)}, u32[]{:S(2)}) copy-start(f32[32]{0:T(128)} %skip_gain.1) | copy-start | bytes 388
  6.6 28.4 %copy-start.17 = (s32[32]{0:T(128)S(1)}, s32[32]{0:T(128)}, u32[]{:S(2)}) copy-start(s32[32]{0:T(128)} %resp_prefix.5) | copy-start | bytes 388
  10.5 77.5 %collective-permute-start.5 = (bf16[2,128,2304]{2,1,0:T(8,128)(2,1)}, bf16[2,128,2304]{2,1,0:T(8,128)(2,1)S(1)}, u32[]{:S(2)}, u32[]{:S(2)}) collective-permute-start(bf16[2,128,2304]{2,1,0:T(8,128)(2,1)} %carry_cotangent.1.car0), channel_id=1, source_target_pairs={{0,13},{1,14},{2,15},{3,0},{4,1},{5,2},{6,3},{7,4},{8,5},{9,6},{10... | collective-permute-start | bytes 3538952 | tf_op jit(solution)/shard_map/ppermute | solution.py:28
  13.4 76.1 %collective-permute-start.4 = (bf16[2,128,2304]{2,1,0:T(8,128)(2,1)}, bf16[2,128,2304]{2,1,0:T(8,128)(2,1)}, u32[]{:S(2)}, u32[]{:S(2)}) collective-permute-start(bf16[2,128,2304]{2,1,0:T(8,128)(2,1)} %carry_cotangent.1.car0), channel_id=1, source_target_pairs={{0,14},{1,15},{2,0},{3,1},{4,2},{5,3},{6,4},{7,5},{8,6},{9,7},{10,... | collective-permute-start | bytes 3538952 | tf_op jit(solution)/shard_map/ppermute | solution.py:28
  14.6 74.9 %collective-permute-start.3 = (bf16[2,128,2304]{2,1,0:T(8,128)(2,1)}, bf16[2,128,2304]{2,1,0:T(8,128)(2,1)}, u32[]{:S(2)}, u32[]{:S(2)}) collective-permute-start(bf16[2,128,2304]{2,1,0:T(8,128)(2,1)} %carry_cotangent.1.car0), channel_id=1, source_target_pairs={{0,15},{1,0},{2,1},{3,2},{4,3},{5,4},{6,5},{7,6},{8,7},{9,8},{10,9... | collective-permute-start | bytes 3538952 | tf_op jit(solution)/shard_map/ppermute | solution.py:28
  15.6 11.6 %collective-permute-start.1 = (bf16[2,144,512]{2,1,0:T(8,128)(2,1)S(1)}, bf16[2,144,512]{2,1,0:T(8,128)(2,1)}, u32[]{:S(2)}, u32[]{:S(2)}) collective-permute-start(bf16[2,144,512]{2,1,0:T(8,128)(2,1)S(1)} %copy-done.4), channel_id=1, source_target_pairs={{0,2},{1,3},{2,4},{3,5},{4,6},{5,7},{6,8},{7,9},{8,10},{9,11},{10,... | collective-permute-start | bytes 884744 | tf_op jit(solution)/shard_map/ppermute | solution.py:28
  15.6 19.3 %collective-permute-start = (bf16[2,144,512]{2,1,0:T(8,128)(2,1)S(1)}, bf16[2,144,512]{2,1,0:T(8,128)(2,1)}, u32[]{:S(2)}, u32[]{:S(2)}) collective-permute-start(bf16[2,144,512]{2,1,0:T(8,128)(2,1)S(1)} %copy-done.4), channel_id=1, source_target_pairs={{0,1},{1,2},{2,3},{3,4},{4,5},{5,6},{6,7},{7,8},{8,9},{9,10},{10,1... | collective-permute-start | bytes 884744 | tf_op jit(solution)/shard_map/ppermute | solution.py:28
  35.0 1.2 %copy-start.9 = (bf16[2,128,2048]{2,1,0:T(8,128)(2,1)S(1)}, bf16[2,128,2048]{2,1,0:T(8,128)(2,1)}, u32[]{:S(2)}) copy-start(bf16[2,128,2048]{2,1,0:T(8,128)(2,1)} %inputs.1) | copy-start | bytes 3145732
  36.2 12.4 %copy-start.7 = (bf16[2,128,4096]{2,1,0:T(8,128)(2,1)S(1)}, bf16[2,128,4096]{2,1,0:T(8,128)(2,1)}, u32[]{:S(2)}) copy-start(bf16[2,128,4096]{2,1,0:T(8,128)(2,1)} %queries.1) | copy-start | bytes 6291460
  36.2 12.4 %copy-start.8 = (bf16[2,128,4096]{2,1,0:T(8,128)(2,1)S(1)}, bf16[2,128,4096]{2,1,0:T(8,128)(2,1)}, u32[]{:S(2)}) copy-start(bf16[2,128,4096]{2,1,0:T(8,128)(2,1)} %cotangent.5) | copy-start | bytes 6291460
  36.2 12.4 %copy-start.11 = (bf16[2,128,512]{2,1,0:T(8,128)(2,1)S(1)}, bf16[2,128,512]{2,1,0:T(8,128)(2,1)}, u32[]{:S(2)}) copy-start(bf16[2,128,512]{2,1,0:T(8,128)(2,1)} %own_keys.1) | copy-start | bytes 786436
  36.2 12.4 %copy-start.12 = (bf16[2,128,512]{2,1,0:T(8,128)(2,1)S(1)}, bf16[2,128,512]{2,1,0:T(8,128)(2,1)}, u32[]{:S(2)}) copy-start(bf16[2,128,512]{2,1,0:T(8,128)(2,1)} %own_values.1) | copy-start | bytes 786436
  36.2 12.4 %copy-start.16 = (s32[16]{0:T(128)S(1)}, s32[16]{0:T(128)}, u32[]{:S(2)}) copy-start(s32[16]{0:T(128)} %prefix_length.1) | copy-start | bytes 196
  48.6 40.9 %copy-start = (bf16[2,128,2304]{2,1,0:T(8,128)(2,1)S(1)}, bf16[2,128,2304]{2,1,0:T(8,128)(2,1)}, u32[]{:S(2)}) copy-start(bf16[2,128,2304]{2,1,0:T(8,128)(2,1)} %carry_cotangent.1.car0) | copy-start | bytes 3538948
  48.7 40.9 %copy-start.10 = (bf16[1,32,64,256]{3,2,1,0:T(8,128)(2,1)S(1)}, bf16[1,32,64,256]{3,2,1,0:T(8,128)(2,1)}, u32[]{:S(2)}) copy-start(bf16[1,32,64,256]{3,2,1,0:T(8,128)(2,1)} %param.31) | copy-start | bytes 3145732
  66.8 0.8 copy-start.2
  67.6 32.1 %collective-permute-start.9 = (bf16[2,144,512]{2,1,0:T(8,128)(2,1)S(1)}, bf16[2,144,512]{2,1,0:T(8,128)(2,1)S(1)}, u32[]{:S(2)}, u32[]{:S(2)}) collective-permute-start(bf16[2,144,512]{2,1,0:T(8,128)(2,1)S(1)} %get-tuple-element.35), channel_id=1, source_target_pairs={{0,15},{1,0},{2,1},{3,2},{4,3},{5,4},{6,5},{7,6},{8,7},{9,8},{10,9... | collective-permute-start | bytes 884744 | tf_op jit(solution)/shard_map/ppermute | solution.py:28
  72.4 1.3 %collective-permute-start.12 = (f32[4,2048]{1,0:T(4,128)S(1)}, f32[4,2048]{1,0:T(4,128)S(1)}, u32[]{:S(2)}, u32[]{:S(2)}) collective-permute-start(f32[4,2048]{1,0:T(4,128)S(1)} %get-tuple-element.41), channel_id=1, source_target_pairs={{0,1},{1,0},{2,3},{3,2},{4,5},{5,4},{6,7},{7,6},{8,9},{9,8},{10,11... | collective-permute-start | bytes 98312 | tf_op jit(solution)/shard_map/ppermute | solution.py:490
  73.6 6.2 %collective-permute-start.13 = (f32[4,2048]{1,0:T(4,128)S(1)}, f32[4,2048]{1,0:T(4,128)S(1)}, u32[]{:S(2)}, u32[]{:S(2)}) collective-permute-start(f32[4,2048]{1,0:T(4,128)S(1)} %add.28), channel_id=1, source_target_pairs={{0,2},{1,3},{2,0},{3,1},{4,6},{5,7},{6,4},{7,5},{8,10},{9,11},{10,... | collective-permute-start | bytes 98312 | tf_op jit(solution)/shard_map/ppermute | solution.py:490
  79.8 2.8 %collective-permute-start.14 = (f32[4,2048]{1,0:T(4,128)S(1)}, f32[4,2048]{1,0:T(4,128)S(1)}, u32[]{:S(2)}, u32[]{:S(2)}) collective-permute-start(f32[4,2048]{1,0:T(4,128)S(1)} %add.29), channel_id=1, source_target_pairs={{0,4},{1,5},{2,6},{3,7},{4,0},{5,1},{6,2},{7,3},{8,12},{9,13},{10,... | collective-permute-start | bytes 98312 | tf_op jit(solution)/shard_map/ppermute | solution.py:490
  82.6 22.1 %collective-permute-start.10 = (bf16[2,144,512]{2,1,0:T(8,128)(2,1)S(1)}, bf16[2,144,512]{2,1,0:T(8,128)(2,1)S(1)}, u32[]{:S(2)}, u32[]{:S(2)}) collective-permute-start(bf16[2,144,512]{2,1,0:T(8,128)(2,1)S(1)} %get-tuple-element.36), channel_id=1, source_target_pairs={{0,14},{1,15},{2,0},{3,1},{4,2},{5,3},{6,4},{7,5},{8,6},{9,7},{10,... | collective-permute-start | bytes 884744 | tf_op jit(solution)/shard_map/ppermute | solution.py:28
  88.0 16.7 %collective-permute-start.11 = (bf16[2,144,512]{2,1,0:T(8,128)(2,1)S(1)}, bf16[2,144,512]{2,1,0:T(8,128)(2,1)S(1)}, u32[]{:S(2)}, u32[]{:S(2)}) collective-permute-start(bf16[2,144,512]{2,1,0:T(8,128)(2,1)S(1)} %get-tuple-element.37), channel_id=1, source_target_pairs={{0,13},{1,14},{2,15},{3,0},{4,1},{5,2},{6,3},{7,4},{8,5},{9,6},{10... | collective-permute-start | bytes 884744 | tf_op jit(solution)/shard_map/ppermute | solution.py:28
  89.5 10.2 %collective-permute-start.15 = (f32[4,2048]{1,0:T(4,128)S(1)}, f32[4,2048]{1,0:T(4,128)S(1)}, u32[]{:S(2)}, u32[]{:S(2)}) collective-permute-start(f32[4,2048]{1,0:T(4,128)S(1)} %add.30), channel_id=1, source_target_pairs={{0,8},{1,9},{2,10},{3,11},{4,12},{5,13},{6,14},{7,15},{8,0},{9,1},... | collective-permute-start | bytes 98312 | tf_op jit(solution)/shard_map/ppermute | solution.py:490
  93.9 15.2 %collective-permute-start.6 = (bf16[2,128,256]{2,1,0:T(8,128)(2,1)S(1)}, bf16[2,128,256]{2,1,0:T(8,128)(2,1)S(1)}, u32[]{:S(2)}, u32[]{:S(2)}) collective-permute-start(bf16[2,128,256]{2,1,0:T(8,128)(2,1)S(1)} %get-tuple-element.28), channel_id=1, source_target_pairs={{0,1},{1,2},{2,3},{3,4},{4,5},{5,6},{6,7},{7,8},{8,9},{9,10},{10,1... | collective-permute-start | bytes 393224 | tf_op jit(solution)/shard_map/ppermute | solution.py:28
  99.7 9.4 %collective-permute-start.7 = (bf16[2,128,256]{2,1,0:T(8,128)(2,1)S(1)}, bf16[2,128,256]{2,1,0:T(8,128)(2,1)S(1)}, u32[]{:S(2)}, u32[]{:S(2)}) collective-permute-start(bf16[2,128,256]{2,1,0:T(8,128)(2,1)S(1)} %get-tuple-element.29), channel_id=1, source_target_pairs={{0,2},{1,3},{2,4},{3,5},{4,6},{5,7},{6,8},{7,9},{8,10},{9,11},{10,... | collective-permute-start | bytes 393224 | tf_op jit(solution)/shard_map/ppermute | solution.py:28
  99.7 5.0 %copy-start.18 = (bf16[2,144,512]{2,1,0:T(8,128)(2,1)}, bf16[2,144,512]{2,1,0:T(8,128)(2,1)S(1)}, u32[]{:S(2)}) copy-start(bf16[2,144,512]{2,1,0:T(8,128)(2,1)S(1)} %collective-permute-done.9.back1) | copy-start | bytes 884740
  99.7 12.6 %collective-permute-start.8 = (bf16[2,128,256]{2,1,0:T(8,128)(2,1)S(1)}, bf16[2,128,256]{2,1,0:T(8,128)(2,1)S(1)}, u32[]{:S(2)}, u32[]{:S(2)}) collective-permute-start(bf16[2,128,256]{2,1,0:T(8,128)(2,1)S(1)} %get-tuple-element.30), channel_id=1, source_target_pairs={{0,3},{1,4},{2,5},{3,6},{4,7},{5,8},{6,9},{7,10},{8,11},{9,12},{10... | collective-permute-start | bytes 393224 | tf_op jit(solution)/shard_map/ppermute | solution.py:28
  104.7 0.7 copy-start.19
  104.7 0.8 copy-start.20

commit v2 on v1

--- a/solution.py
+++ b/solution.py
@@ -40,49 +40,41 @@
     return lax.dot_general(a, b, (((1,), (0,)), ((), ())), preferred_element_type=F32)
 
 
-def pack_kernel(keys, values, tail, out, rows8):
-    rows = keys.shape[1]
-    out[0, 0:rows, :] = keys[0]
-    out[1, 0:rows, :] = values[0]
-    rows8[...] = jnp.zeros_like(rows8)
-    rows8[5:8, :] = tail[0].astype(F32)
-    for half in range(2):
-        upper = rows8[:, half * 1024 : half * 1024 + 512]
-        lower = rows8[:, half * 1024 + 512 : half * 1024 + 1024]
-        out[half, rows : rows + 16, :] = jnp.concatenate([upper, lower], axis=0).astype(BF16)
-
-
-def pack(prefix_keys, prefix_values, prefix_tail):
-    rows, width = prefix_keys.shape[1:]
+def pack_kernel(keys, values, out):
+    out[0] = keys[0]
+    out[1] = values[0]
+
+
+def pack(prefix_keys, prefix_values):
     return pl.pallas_call(
         pack_kernel,
-        out_shape=jax.ShapeDtypeStruct((2, rows + 16, width), BF16),
-        in_specs=[VMEM] * 3,
+        out_shape=jax.ShapeDtypeStruct((2,) + prefix_keys.shape[1:], BF16),
+        in_specs=[VMEM] * 2,
         out_specs=VMEM,
-        scratch_shapes=[pltpu.VMEM((8, prefix_tail.shape[2]), F32)],
         name="pack_prefix",
-    )(prefix_keys, prefix_values, prefix_tail)
+    )(prefix_keys, prefix_values)
 
 
 def running_sum(log_decay):
-    length = log_decay.shape[0]
+    heads, length = log_decay.shape
     row = lax.broadcasted_iota(jnp.int32, (length, length), 0)
     col = lax.broadcasted_iota(jnp.int32, (length, length), 1)
-    lower = (col <= row).astype(F32)
-    return lax.dot_general(
-        lower,
+    upper = (row <= col).astype(F32)
+    rows = lax.dot_general(
         log_decay,
+        upper,
         (((1,), (0,)), ((), ())),
         precision=lax.Precision.HIGHEST,
         preferred_element_type=F32,
     )
+    return jnp.concatenate([rows, jnp.zeros((128 - heads, length), F32)], axis=0).T, rows
 
 
 def carry_kernel(resp_length, log_decay, cotangent, read, out):
-    length = log_decay.shape[1]
+    length = cotangent.shape[1]
     width = cotangent.shape[2]
     live_to = resp_length[pl.program_id(0)]
-    raised = jnp.exp(running_sum(log_decay[0]))
+    raised = jnp.exp(running_sum(log_decay[0])[0])
     live = lax.broadcasted_iota(jnp.int32, (length, 2 * HEAD_DIM), 0) < live_to
     first = lax.broadcasted_iota(jnp.int32, (length, 2 * HEAD_DIM), 1) < HEAD_DIM
     for pair in range(width // (2 * HEAD_DIM)):
@@ -95,7 +87,7 @@
 
 def carry(resp_length, log_decay, out_cotangent, state_out):
     count, length, width = out_cotangent.shape
-    heads = log_decay.shape[2]
+    heads = log_decay.shape[1]
     states = state_out.shape[2]
     return pl.pallas_call(
         carry_kernel,
@@ -103,13 +95,29 @@
         out_shape=jax.ShapeDtypeStruct((count, length, width + states), BF16),
         in_specs=[
             SMEM,
-            pl.BlockSpec((1, length, heads), lambda r: (r, 0, 0)),
+            pl.BlockSpec((1, heads, length), lambda r: (r, 0, 0)),
             pl.BlockSpec((1, length, width), lambda r: (r, 0, 0)),
             pl.BlockSpec((1, length, states), lambda r: (r, 0, 0)),
         ],
         out_specs=pl.BlockSpec((1, length, width + states), lambda r: (r, 0, 0)),
         name="carry_cotangent",
     )(resp_length, log_decay, out_cotangent, state_out)
+
+
+def relayed(rank):
+    even = rank % 2 == 0
+    return 0, 2, jnp.where(even, 1, 3), jnp.where(even, 3, 1)
+
+
+def gather(value, sign):
+    length = lax.axis_size("dp")
+    two = shift(value, 2 * sign)
+    if sign > 0:
+        pairs = [(i, (i + (3 if i % 2 else 1)) % length) for i in range(length)]
+    else:
+        pairs = [(i, (i - (1 if i % 2 else 3)) % length) for i in range(length)]
+    last = lax.ppermute(value, "dp", pairs)
+    return [value, two, lax.ppermute(two, "dp", [(i, i ^ 1) for i in range(length)]), last]
 
 
 def distance_to(rank, owner, devices):
@@ -124,10 +132,10 @@
     resp_length,
     skip_gain,
     inputs,
-    pack0,
-    pack1,
-    pack2,
-    pack3,
+    tail0,
+    tail1,
+    tail2,
+    tail3,
     conv_weight,
     write,
     read,
@@ -139,7 +147,6 @@
     g_read,
     padded,
     shifted,
-    tail_rows,
     inner,
 ):
     resp = pl.program_id(0)
@@ -149,20 +156,14 @@
     rank = rank_ref[0]
     live_to = resp_length[resp]
     gap = distance_to(rank, resp_prefix[2 * rank + resp], devices)
-    for step, packed in enumerate((pack0, pack1, pack2, pack3)):
+    for step, tail in enumerate((tail0, tail1, tail2, tail3)):
 
         @pl.when(gap == step)
-        def _(packed=packed):
-            for half in range(2):
-                tail_rows[half] = packed[half, length : length + 16, :].astype(F32)
-
-    for part in range(4):
-        padded[0:8, part * 512 : part * 512 + 512] = tail_rows[part // 2, 8 * (part % 2) : 8 * (part % 2) + 8, :]
+        def _(tail=tail):
+            padded[5:8, :] = tail[0].astype(F32)
+
     padded[8 : 8 + length, :] = inputs[0].astype(F32)
-    decay_sum = running_sum(log_decay[0])
-    decay_rows = jnp.concatenate(
-        [decay_sum, jnp.zeros((length, 128 - decay_sum.shape[1]), F32)], axis=1
-    ).T
+    decay_sum, decay_rows = running_sum(log_decay[0])
     s_index = lax.broadcasted_iota(jnp.int32, (length, length), 0)
     t_index = lax.broadcasted_iota(jnp.int32, (length, length), 1)
     causal = s_index <= t_index
@@ -219,12 +220,12 @@
     g_read[0] = tn(inner[...].astype(BF16), write[0])
 
 
-def mamba(rank, resp_prefix, resp_length, skip_gain, inputs, packs, conv_weight, write, read, log_decay, cotangent, devices):
+def mamba(rank, resp_prefix, resp_length, skip_gain, inputs, tails, conv_weight, write, read, log_decay, cotangent, devices):
     count, length, width = inputs.shape
-    heads = log_decay.shape[2]
+    heads = log_decay.shape[1]
     states = read.shape[2]
     taps = conv_weight.shape[0]
-    whole = pl.BlockSpec(packs[0].shape, lambda r: (0, 0, 0))
+    whole = pl.BlockSpec(tails[0].shape, lambda r: (0, 0, 0))
     return pl.pallas_call(
         functools.partial(mamba_kernel, devices),
         grid=(count,),
@@ -247,7 +248,7 @@
             pl.BlockSpec((taps, width), lambda r: (0, 0)),
             pl.BlockSpec((1, length, states), lambda r: (r, 0, 0)),
             pl.BlockSpec((1, length, states), lambda r: (r, 0, 0)),
-            pl.BlockSpec((1, length, heads), lambda r: (r, 0, 0)),
+            pl.BlockSpec((1, heads, length), lambda r: (r, 0, 0)),
             pl.BlockSpec((1, length, width), lambda r: (r, 0, 0)),
         ],
         out_specs=[
@@ -259,13 +260,12 @@
         scratch_shapes=[
             pltpu.VMEM((length + 8, width), F32),
             pltpu.VMEM((length + 16, width), F32),
-            pltpu.VMEM((2, 16, 512), F32),
             pltpu.VMEM((length, length), F32),
         ],
         compiler_params=pltpu.CompilerParams(vmem_limit_bytes=32 * 2**20),
         cost_estimate=pl.CostEstimate(flops=2 * 10**9, bytes_accessed=8 * 2**20, transcendentals=10**6),
         name="mamba_grads",
-    )(rank, resp_prefix, resp_length, skip_gain, inputs, *packs, conv_weight, write, read, log_decay, cotangent)
+    )(rank, resp_prefix, resp_length, skip_gain, inputs, *tails, conv_weight, write, read, log_decay, cotangent)
 
 
 def attention_kernel(
@@ -301,7 +301,7 @@
     live_to = resp_length[resp]
     scale = 1.0 / math.sqrt(ATT_DIM)
     gap = distance_to(rank, prefix, devices)
-    for step, packed in enumerate((pack0, pack1, pack2, pack3)):
+    for step, packed in zip(relayed(rank), (pack0, pack1, pack2, pack3)):
 
         @pl.when(gap == step)
         def _(packed=packed):
@@ -361,9 +361,10 @@
 
 def attention(rank, resp_prefix, resp_length, prefix_length, queries, cotangent, own_keys, own_values, packs, g_tail, devices):
     count, length, width = queries.shape
-    rows = packs[0].shape[1] - 16
+    rows = packs[0].shape[1]
     group = REPEAT * ATT_DIM
-    packed = pl.BlockSpec((2, rows + 16, ATT_DIM), lambda h, r: (0, 0, h))
+    packed = pl.BlockSpec((2, rows, ATT_DIM), lambda h, r: (0, 0, h))
+    back_block = pl.BlockSpec((2, rows + 16, ATT_DIM), lambda h, r: (0, 0, h))
     back = (2, rows + 16, KV_HEADS * ATT_DIM)
     return pl.pallas_call(
         functools.partial(attention_kernel, devices),
@@ -392,10 +393,10 @@
         ],
         out_specs=[
             pl.BlockSpec((1, length, group), lambda h, r: (r, 0, h)),
-            packed,
-            packed,
-            packed,
-            packed,
+            back_block,
+            back_block,
+            back_block,
+            back_block,
         ],
         scratch_shapes=[
             pltpu.VMEM((rows + length, ATT_DIM), BF16),
@@ -408,19 +409,22 @@
     )(rank, resp_prefix, resp_length, prefix_length, queries, cotangent, own_keys, own_values, *packs, g_tail)
 
 
-def owner_kernel(devices, rank_ref, resp_prefix, state, car0, car1, car2, car3, g_state, dr0, dr1, dr2, dr3, total):
+def owner_kernel(devices, rank_ref, resp_prefix, state, car0, car1, car2, car3, g_state, dr0, dr1, dr2, dr3, total, parts):
     rank = rank_ref[0]
+    even = rank % 2 == 0
     width = state.shape[0]
     chunk = 512
     total[...] = jnp.zeros_like(total)
-    for step, (carried, d_read) in enumerate(zip((car0, car1, car2, car3), (dr0, dr1, dr2, dr3))):
+    for slot, (step, carried) in enumerate(
+        zip((0, 2, jnp.where(even, 3, 1), jnp.where(even, 1, 3)), (car0, car1, car2, car3))
+    ):
         sender = rank + step
         sender = jnp.where(sender >= devices, sender - devices, sender)
         for resp in range(2):
             mine = resp_prefix[2 * sender + resp] == rank
 
             @pl.when(mine)
-            def _(carried=carried, d_read=d_read, resp=resp):
+            def _(carried=carried, slot=slot, resp=resp):
                 read = carried[resp, :, width:]
                 acc = None
                 for at in range(0, width, chunk):
@@ -428,13 +432,25 @@
                     term = nn(piece, state[at : at + chunk, :])
                     acc = term if acc is None else acc + term
                     total[at : at + chunk, :] += tn(piece, read)
-                d_read[resp] = acc.astype(d_read.dtype)
+                parts[slot, resp] = acc
 
             @pl.when(jnp.logical_not(mine))
-            def _(d_read=d_read, resp=resp):
-                d_read[resp] = jnp.zeros(d_read.shape[1:], d_read.dtype)
+            def _(slot=slot, resp=resp):
+                parts[slot, resp] = jnp.zeros(parts.shape[2:], F32)
 
     g_state[...] = total[...].astype(BF16)
+    dr0[...] = parts[0]
+    dr2[...] = parts[1].astype(BF16)
+
+    @pl.when(even)
+    def _():
+        dr3[...] = parts[2].astype(BF16)
+        dr1[...] = parts[3].astype(BF16)
+
+    @pl.when(jnp.logical_not(even))
+    def _():
+        dr1[...] = parts[2].astype(BF16)
+        dr3[...] = parts[3].astype(BF16)
 
 
 def owner(rank, resp_prefix, state, carried, devices):
@@ -446,7 +462,7 @@
         + [jax.ShapeDtypeStruct((count, length, states), BF16)] * 3,
         in_specs=[SMEM, SMEM] + [VMEM] * 5,
         out_specs=[VMEM] * 5,
-        scratch_shapes=[pltpu.VMEM((width, states), F32)],
+        scratch_shapes=[pltpu.VMEM((width, states), F32), pltpu.VMEM((SPAN, count, length, states), F32)],
         compiler_params=pltpu.CompilerParams(vmem_limit_bytes=32 * 2**20),
         cost_estimate=pl.CostEstimate(flops=2 * 10**9, bytes_accessed=8 * 2**20, transcendentals=0),
         name="owner_state",
@@ -520,12 +536,12 @@
     read = state_out.reshape(count, length, states)
     state = prefix_state.reshape(-1, states)
 
-    packed = pack(prefix_keys, prefix_values, prefix_tail)
-    packs = [packed] + [shift(packed, by) for by in range(1, SPAN)]
-    carried = carry(resp_length, log_decay, out_cotangent, read)
-    carries = [carried] + [shift(carried, -by) for by in range(1, SPAN)]
+    decay = jnp.swapaxes(log_decay, 1, 2)
+    carries = gather(carry(resp_length, decay, out_cotangent, read), -1)
+    tails = [prefix_tail] + [shift(prefix_tail, by) for by in range(1, SPAN)]
+    packs = gather(pack(prefix_keys, prefix_values), 1)
     g_inputs, g_tail, g_conv, g_read = mamba(
-        rank, resp_prefix, resp_length, skip_gain, token_inputs, packs, conv_weight, write, read, log_decay, out_cotangent, devices
+        rank, resp_prefix, resp_length, skip_gain, token_inputs, tails, conv_weight, write, read, decay, out_cotangent, devices
     )
     g_queries, *backs = attention(
         rank, resp_prefix, resp_length, prefix_length, queries, attn_cotangent, own_keys, own_values, packs, g_tail, devices

time: 113 us -> 131 us (1.16)
  the two profiles are of different devices: /device:TPU:1 before, /device:TPU:0 now
where the time goes in v2:
time: 131 us
  waiting for transfers between devices  68.3 us (52%)
  Pallas kernels  41.6 us (32%)
  starting transfers between devices  13.3 us (10%)
  local copies, waits for them, and re-layouts  5.14 us (4%)
  other arithmetic  1.45 us (1%)
    ppermute x11, waiting for transfers between devices, shift(): lax.ppermute(value, 'dp', [(i, (i + by) % length) for i in range(length)])  59.3 us
    pallas_call x1, Pallas kernels, attention(): pl.pallas_call(functools.partial(attention_kernel, devices), grid=(KV_HEA...  17.7 us
    ppermute x11, starting transfers between devices, shift(): lax.ppermute(value, 'dp', [(i, (i + by) % length) for i in range(length)])  12.3 us
    pallas_call x1, Pallas kernels, mamba(): pl.pallas_call(functools.partial(mamba_kernel, devices), grid=(count,), o...  11.7 us
    ppermute x4, waiting for transfers between devices, all_sum(): lax.ppermute(value, 'dp', [(i, i ^ by) for i in range(length)])  8.92 us
    unnamed x45, local copies, waits for them, and re-layouts  5.14 us
    pallas_call x1, Pallas kernels, owner(): pl.pallas_call(functools.partial(owner_kernel, devices), out_shape=[jax.S...  4.42 us
    pallas_call x1, Pallas kernels, carry(): pl.pallas_call(carry_kernel, grid=(count,), out_shape=jax.ShapeDtypeStruc...  3.99 us
  transfers between devices with their start and end apart: 19, of which 9 were waited for; matrix products, arithmetic and copies ran while one was open for 2% of the time, Pallas kernels for 29%

profile of v2, /device:TPU:0, one launch (start us, length us, event | category | flops | bytes accessed | tf_op | source)
XLA Modules:
  0.0 130.6 jit_solution(8987904360068594447)
XLA Ops:
  0.7 4.0 %carry_cotangent.1.car0 = bf16[2,128,2304]{2,1,0:T(8,128)(2,1)} custom-call(s32[2]{0:T(128)} %resp_length.5, f32[2,32,128]{2,1,0:T(8,128)} %bitcast.12, bf16[2,128,2048]{2,1,0:T(8,128)(2,1)} %cotangent.4, bf16[2,128,256]{2,1,0:T(8,128)(2,1)} %bitcast.10), custom_call_target="tpu_custom_call" | custom-call | tf_op jit(solution)/shard_map/carry_cotangent/pallas_call | solution.py:92
  4.7 6.0 %collective-permute-start.3 = (bf16[2,128,2304]{2,1,0:T(8,128)(2,1)}, bf16[2,128,2304]{2,1,0:T(8,128)(2,1)S(1)}, u32[]{:S(2)}, u32[]{:S(2)}) collective-permute-start(bf16[2,128,2304]{2,1,0:T(8,128)(2,1)} %carry_cotangent.1.car0), channel_id=1, source_target_pairs={{0,14},{1,15},{2,0},{3,1},{4,2},{5,3},{6,4},{7,5},{8,6},{9,7},{10,... | collective-permute-start | bytes 3538952 | tf_op jit(solution)/shard_map/ppermute | solution.py:28
  10.7 25.5 %collective-permute-done.3.car1 = bf16[2,128,2304]{2,1,0:T(8,128)(2,1)S(1)} collective-permute-done((bf16[2,128,2304]{2,1,0:T(8,128)(2,1)}, bf16[2,128,2304]{2,1,0:T(8,128)(2,1)S(1)}, u32[]{:S(2)}, u32[]{:S(2)}) %collective-permute-start.3) | collective-permute-done | bytes 1179680 | tf_op jit(solution)/shard_map/ppermute | solution.py:28
  36.2 0.0 collective-permute-start.4
  36.3 1.7 %pack_prefix.1.pack0 = bf16[2,128,512]{2,1,0:T(8,128)(2,1)} custom-call(bf16[1,128,512]{2,1,0:T(8,128)(2,1)} %keys.1, bf16[1,128,512]{2,1,0:T(8,128)(2,1)} %values.1), custom_call_target="tpu_custom_call" | custom-call | tf_op jit(solution)/shard_map/pack_prefix/pallas_call | solution.py:49
  37.9 0.2 collective-permute-start.9
  38.2 0.3 collective-permute-start.11
  38.5 11.9 %collective-permute-done.9.pack1 = bf16[2,128,512]{2,1,0:T(8,128)(2,1)S(1)} collective-permute-done((bf16[2,128,512]{2,1,0:T(8,128)(2,1)}, bf16[2,128,512]{2,1,0:T(8,128)(2,1)S(1)}, u32[]{:S(2)}, u32[]{:S(2)}) %collective-permute-start.9) | collective-permute-done | bytes 262176 | tf_op jit(solution)/shard_map/ppermute | solution.py:28
  50.4 0.0 collective-permute-start.10
  50.4 6.4 %collective-permute-done.1.tail2 = bf16[1,3,2048]{2,1,0:T(4,128)(2,1)S(1)} collective-permute-done((bf16[1,3,2048]{2,1,0:T(4,128)(2,1)S(1)}, bf16[1,3,2048]{2,1,0:T(4,128)(2,1)S(1)}, u32[]{:S(2)}, u32[]{:S(2)}) %collective-permute-start.1) | collective-permute-done | bytes 12320 | tf_op jit(solution)/shard_map/ppermute | solution.py:28
  56.8 0.0 collective-permute-start
  56.8 5.9 %collective-permute-done.tail1 = bf16[1,3,2048]{2,1,0:T(4,128)(2,1)S(1)} collective-permute-done((bf16[1,3,2048]{2,1,0:T(4,128)(2,1)S(1)}, bf16[1,3,2048]{2,1,0:T(4,128)(2,1)S(1)}, u32[]{:S(2)}, u32[]{:S(2)}) %collective-permute-start) | collective-permute-done | bytes 12320 | tf_op jit(solution)/shard_map/ppermute | solution.py:28
  62.7 0.0 collective-permute-start.2
  62.7 5.0 %collective-permute-done.2.tail3 = bf16[1,3,2048]{2,1,0:T(4,128)(2,1)S(1)} collective-permute-done((bf16[1,3,2048]{2,1,0:T(4,128)(2,1)S(1)}, bf16[1,3,2048]{2,1,0:T(4,128)(2,1)S(1)}, u32[]{:S(2)}, u32[]{:S(2)}) %collective-permute-start.2) | collective-permute-done | bytes 12320 | tf_op jit(solution)/shard_map/ppermute | solution.py:28
  67.7 0.0 copy-start.9
  67.7 1.2 copy-done.9
  68.9 0.9 copy-done.13
  69.8 0.0 copy-start.12
  69.9 0.0 copy-start.17
  69.9 11.7 %mamba_grads.1 = (bf16[2,128,2048]{2,1,0:T(8,128)(2,1)}, f32[2,4,8,512]{3,2,1,0:T(8,128)S(1)}, f32[4,2048]{1,0:T(4,128)S(1)}, f32[2,128,256]{2,1,0:T(8,128)S(1)}) custom-call(s32[1]{0:T(128)} %bitcast.rank_ref, s32[32]{0:T(128)S(1)} %copy-done.18, s32[2]{0:T(128)S(1)} %copy-done.6, f32[32]{0:T(128)S(1)} %copy-done.16, bf16[2,128,2048]{2,1,0:T(8,128)(2,1)S(1)} %copy-done.9, ...), custom_call_target="tpu_custom_call" | custom-call | flops 2000000000 | bytes 8388608 | tf_op jit(solution)/shard_map/mamba_grads/pallas_call | solution.py:229
  81.5 0.0 collective-permute-done.11.pack3
  81.5 0.0 collective-permute-done.10.pack2
  81.6 0.0 copy-start.10
  81.6 17.7 %attention_grads.1 = (bf16[2,128,4096]{2,1,0:T(8,128)(2,1)}, f32[2,144,512]{2,1,0:T(8,128)S(1)}, bf16[2,144,512]{2,1,0:T(8,128)(2,1)S(1)}, bf16[2,144,512]{2,1,0:T(8,128)(2,1)S(1)}, bf16[2,144,512]{2,1,0:T(8,128)(2,1)S(1)}) custom-call(s32[1]{0:T(128)} %bitcast.rank_ref, s32[32]{0:T(128)S(1)} %copy-done.18, s32[2]{0:T(128)S(1)} %copy-done.6, ...), custom_call_target="tpu_custom_call" | custom-call | flops 4000000000 | bytes 8388608 | tf_op jit(solution)/shard_map/attention_grads/pallas_call | solution.py:369
  99.3 0.8 copy-done.2
  100.1 0.5 collective-permute-start.15
  100.6 1.1 collective-permute-done.15
  101.8 0.1 collective-permute-start.16
  101.9 3.9 %collective-permute-done.16 = f32[4,2048]{1,0:T(4,128)S(1)} collective-permute-done((f32[4,2048]{1,0:T(4,128)S(1)}, f32[4,2048]{1,0:T(4,128)S(1)}, u32[]{:S(2)}, u32[]{:S(2)}) %collective-permute-start.16) | collective-permute-done | bytes 32800 | tf_op jit(solution)/shard_map/ppermute | solution.py:506
  105.8 0.1 collective-permute-start.17
  105.8 3.9 %collective-permute-done.17 = f32[4,2048]{1,0:T(4,128)S(1)} collective-permute-done((f32[4,2048]{1,0:T(4,128)S(1)}, f32[4,2048]{1,0:T(4,128)S(1)}, u32[]{:S(2)}, u32[]{:S(2)}) %collective-permute-start.17) | collective-permute-done | bytes 32800 | tf_op jit(solution)/shard_map/ppermute | solution.py:506
  109.8 0.1 collective-permute-start.18
  109.8 2.7 %collective-permute-start.13 = (bf16[2,144,512]{2,1,0:T(8,128)(2,1)S(1)}, bf16[2,144,512]{2,1,0:T(8,128)(2,1)S(1)}, u32[]{:S(2)}, u32[]{:S(2)}) collective-permute-start(bf16[2,144,512]{2,1,0:T(8,128)(2,1)S(1)} %get-tuple-element.36), channel_id=1, source_target_pairs={{0,14},{1,15},{2,0},{3,1},{4,2},{5,3},{6,4},{7,5},{8,6},{9,7},{10,... | collective-permute-start | bytes 884744 | tf_op jit(solution)/shard_map/ppermute | solution.py:28
  112.5 0.0 collective-permute-done.4.car2
  112.6 4.4 %owner_state.1 = (bf16[2048,256]{1,0:T(8,128)(2,1)}, f32[2,128,256]{2,1,0:T(8,128)S(1)}, bf16[2,128,256]{2,1,0:T(8,128)(2,1)S(1)}, bf16[2,128,256]{2,1,0:T(8,128)(2,1)S(1)}, bf16[2,128,256]{2,1,0:T(8,128)(2,1)S(1)}) custom-call(s32[1]{0:T(128)} %bitcast.rank_ref, s32[32]{0:T(128)S(1)} %copy-done.18, bf16[2048,256]{1,0:T(8,128)(2,1)S(1)} %bitcast.14, ...), custom_call_target="tpu_custom_call" | custom-call | flops 2000000000 | bytes 8388608 | tf_op jit(solution)/shard_map/owner_state/pallas_call | solution.py:459
  117.0 2.4 %collective-permute-start.6 = (bf16[2,128,256]{2,1,0:T(8,128)(2,1)S(1)}, bf16[2,128,256]{2,1,0:T(8,128)(2,1)S(1)}, u32[]{:S(2)}, u32[]{:S(2)}) collective-permute-start(bf16[2,128,256]{2,1,0:T(8,128)(2,1)S(1)} %get-tuple-element.28), channel_id=1, source_target_pairs={{0,1},{1,2},{2,3},{3,4},{4,5},{5,6},{6,7},{7,8},{8,9},{9,10},{10,1... | collective-permute-start | bytes 393224 | tf_op jit(solution)/shard_map/ppermute | solution.py:28
  119.4 0.0 collective-permute-done.18
  119.4 0.9 collective-permute-start.7
  120.3 0.0 collective-permute-start.8
  120.3 0.7 add_multiply_fusion
  121.0 0.0 collective-permute-done.13.back2
  121.0 4.6 %collective-permute-done.14.back3 = bf16[2,144,512]{2,1,0:T(8,128)(2,1)S(1)} collective-permute-done((bf16[2,144,512]{2,1,0:T(8,128)(2,1)S(1)}, bf16[2,144,512]{2,1,0:T(8,128)(2,1)S(1)}, u32[]{:S(2)}, u32[]{:S(2)}) %collective-permute-start.14) | collective-permute-done | bytes 294944 | tf_op jit(solution)/shard_map/ppermute | solution.py:28
  125.6 0.7 copy-done.21
  126.3 2.2 %sum_prefix.1 = (f32[1,128,512]{2,1,0:T(8,128)}, f32[1,128,512]{2,1,0:T(8,128)}, f32[1,3,2048]{2,1,0:T(4,128)}) custom-call(f32[2,144,512]{2,1,0:T(8,128)} %copy-done.2, bf16[2,144,512]{2,1,0:T(8,128)(2,1)} %copy-done.19, bf16[2,144,512]{2,1,0:T(8,128)(2,1)} %copy-done.20, bf16[2,144,512]{2,1,0:T(8,128)(2,1)} %copy-done.21), custom_call_target="tpu_custom_call" | custom-call | tf_op jit(solution)/shard_map/sum_prefix/pallas_call | solution.py:487
  128.5 1.4 %copy.27 = f32[1,3,2048]{2,0,1:T(1,128)} copy(f32[1,3,2048]{2,1,0:T(4,128)} %get-tuple-element.46) | data formatting | bytes 49152
  129.9 0.0 collective-permute-done.6
  129.9 0.0 collective-permute-done.7
  129.9 0.7 fusion
  (46 shorter events, 0.1 us)
Async XLA Ops:
  0.6 49.7 %copy-start.15 = (bf16[1,3,2048]{2,1,0:T(4,128)(2,1)S(1)}, bf16[1,3,2048]{2,1,0:T(4,128)(2,1)}, u32[]{:S(2)}) copy-start(bf16[1,3,2048]{2,1,0:T(4,128)(2,1)} %tail0.1) | copy-start | bytes 36868
  0.6 67.0 %copy-start.1 = (bf16[2,128,2048]{2,1,0:T(8,128)(2,1)S(1)}, bf16[2,128,2048]{2,1,0:T(8,128)(2,1)}, u32[]{:S(2)}) copy-start(bf16[2,128,2048]{2,1,0:T(8,128)(2,1)} %cotangent.4) | copy-start | bytes 3145732
  0.7 67.0 %copy-start.4 = (bf16[2,128,1,256]{3,1,2,0:T(8,128)(2,1)S(1)}, bf16[2,128,1,256]{3,1,2,0:T(8,128)(2,1)}, u32[]{:S(2)}) copy-start(bf16[2,128,1,256]{3,1,2,0:T(8,128)(2,1)} %param.20) | copy-start | bytes 393220
  0.7 67.0 %copy-start.5 = (f32[2,128,32]{1,2,0:T(8,128)S(1)}, f32[2,128,32]{1,2,0:T(8,128)}, u32[]{:S(2)}) copy-start(f32[2,128,32]{1,2,0:T(8,128)} %param.21) | copy-start | bytes 98308
  0.7 67.0 %copy-start.6 = (s32[2]{0:T(128)S(1)}, s32[2]{0:T(128)}, u32[]{:S(2)}) copy-start(s32[2]{0:T(128)} %resp_length.5) | copy-start | bytes 28
  0.7 67.0 %copy-start.14 = (f32[4,2048]{1,0:T(4,128)S(1)}, f32[4,2048]{1,0:T(4,128)}, u32[]{:S(2)}) copy-start(f32[4,2048]{1,0:T(4,128)} %conv_weight.1) | copy-start | bytes 98308
  0.7 67.0 %copy-start.16 = (f32[32]{0:T(128)S(1)}, f32[32]{0:T(128)}, u32[]{:S(2)}) copy-start(f32[32]{0:T(128)} %skip_gain.1) | copy-start | bytes 388
  0.7 67.0 %copy-start.18 = (s32[32]{0:T(128)S(1)}, s32[32]{0:T(128)}, u32[]{:S(2)}) copy-start(s32[32]{0:T(128)} %resp_prefix.5) | copy-start | bytes 388
  4.7 31.5 %collective-permute-start.3 = (bf16[2,128,2304]{2,1,0:T(8,128)(2,1)}, bf16[2,128,2304]{2,1,0:T(8,128)(2,1)S(1)}, u32[]{:S(2)}, u32[]{:S(2)}) collective-permute-start(bf16[2,128,2304]{2,1,0:T(8,128)(2,1)} %carry_cotangent.1.car0), channel_id=1, source_target_pairs={{0,14},{1,15},{2,0},{3,1},{4,2},{5,3},{6,4},{7,5},{8,6},{9,7},{10,... | collective-permute-start | bytes 3538952 | tf_op jit(solution)/shard_map/ppermute | solution.py:28
  10.7 101.8 %collective-permute-start.5 = (bf16[2,128,2304]{2,1,0:T(8,128)(2,1)}, bf16[2,128,2304]{2,1,0:T(8,128)(2,1)}, u32[]{:S(2)}, u32[]{:S(2)}) collective-permute-start(bf16[2,128,2304]{2,1,0:T(8,128)(2,1)} %carry_cotangent.1.car0), channel_id=1, source_target_pairs={{0,13},{1,0},{2,15},{3,2},{4,1},{5,4},{6,3},{7,6},{8,5},{9,8},{10,... | collective-permute-start | bytes 3538952 | tf_op jit(solution)/shard_map/ppermute | solution.py:119
  36.2 76.3 %collective-permute-start.4 = (bf16[2,128,2304]{2,1,0:T(8,128)(2,1)S(1)}, bf16[2,128,2304]{2,1,0:T(8,128)(2,1)}, u32[]{:S(2)}, u32[]{:S(2)}) collective-permute-start(bf16[2,128,2304]{2,1,0:T(8,128)(2,1)S(1)} %collective-permute-done.3.car1), channel_id=1, source_target_pairs={{0,1},{1,0},{2,3},{3,2},{4,5},{5,4},{6,7},{7,6},{8,9},{9,8},{10,11... | collective-permute-start | bytes 3538952 | tf_op jit(solution)/shard_map/ppermute | solution.py:120
  37.9 12.4 %collective-permute-start.9 = (bf16[2,128,512]{2,1,0:T(8,128)(2,1)}, bf16[2,128,512]{2,1,0:T(8,128)(2,1)S(1)}, u32[]{:S(2)}, u32[]{:S(2)}) collective-permute-start(bf16[2,128,512]{2,1,0:T(8,128)(2,1)} %pack_prefix.1.pack0), channel_id=1, source_target_pairs={{0,2},{1,3},{2,4},{3,5},{4,6},{5,7},{6,8},{7,9},{8,10},{9,11},{10,... | collective-permute-start | bytes 786440 | tf_op jit(solution)/shard_map/ppermute | solution.py:28
  38.2 43.3 %collective-permute-start.11 = (bf16[2,128,512]{2,1,0:T(8,128)(2,1)}, bf16[2,128,512]{2,1,0:T(8,128)(2,1)S(1)}, u32[]{:S(2)}, u32[]{:S(2)}) collective-permute-start(bf16[2,128,512]{2,1,0:T(8,128)(2,1)} %pack_prefix.1.pack0), channel_id=1, source_target_pairs={{0,1},{1,4},{2,3},{3,6},{4,5},{5,8},{6,7},{7,10},{8,9},{9,12},{10,... | collective-permute-start | bytes 786440 | tf_op jit(solution)/shard_map/ppermute | solution.py:119
  50.4 31.1 %collective-permute-start.10 = (bf16[2,128,512]{2,1,0:T(8,128)(2,1)S(1)}, bf16[2,128,512]{2,1,0:T(8,128)(2,1)S(1)}, u32[]{:S(2)}, u32[]{:S(2)}) collective-permute-start(bf16[2,128,512]{2,1,0:T(8,128)(2,1)S(1)} %collective-permute-done.9.pack1), channel_id=1, source_target_pairs={{0,1},{1,0},{2,3},{3,2},{4,5},{5,4},{6,7},{7,6},{8,9},{9,8},{10,11... | collective-permute-start | bytes 786440 | tf_op jit(solution)/shard_map/ppermute | solution.py:120
  50.4 6.4 %collective-permute-start.1 = (bf16[1,3,2048]{2,1,0:T(4,128)(2,1)S(1)}, bf16[1,3,2048]{2,1,0:T(4,128)(2,1)S(1)}, u32[]{:S(2)}, u32[]{:S(2)}) collective-permute-start(bf16[1,3,2048]{2,1,0:T(4,128)(2,1)S(1)} %copy-done.15), channel_id=1, source_target_pairs={{0,2},{1,3},{2,4},{3,5},{4,6},{5,7},{6,8},{7,9},{8,10},{9,11},{10,... | collective-permute-start | bytes 36872 | tf_op jit(solution)/shard_map/ppermute | solution.py:28
  56.8 5.9 %collective-permute-start = (bf16[1,3,2048]{2,1,0:T(4,128)(2,1)S(1)}, bf16[1,3,2048]{2,1,0:T(4,128)(2,1)S(1)}, u32[]{:S(2)}, u32[]{:S(2)}) collective-permute-start(bf16[1,3,2048]{2,1,0:T(4,128)(2,1)S(1)} %copy-done.15), channel_id=1, source_target_pairs={{0,1},{1,2},{2,3},{3,4},{4,5},{5,6},{6,7},{7,8},{8,9},{9,10},{10,1... | collective-permute-start | bytes 36872 | tf_op jit(solution)/shard_map/ppermute | solution.py:28
  62.7 5.0 %collective-permute-start.2 = (bf16[1,3,2048]{2,1,0:T(4,128)(2,1)S(1)}, bf16[1,3,2048]{2,1,0:T(4,128)(2,1)S(1)}, u32[]{:S(2)}, u32[]{:S(2)}) collective-permute-start(bf16[1,3,2048]{2,1,0:T(4,128)(2,1)S(1)} %copy-done.15), channel_id=1, source_target_pairs={{0,3},{1,4},{2,5},{3,6},{4,7},{5,8},{6,9},{7,10},{8,11},{9,12},{10... | collective-permute-start | bytes 36872 | tf_op jit(solution)/shard_map/ppermute | solution.py:28
  67.7 1.2 copy-start.9
  68.9 0.9 copy-start.13
  69.8 11.7 %copy-start.3 = (bf16[2,128,512]{2,1,0:T(8,128)(2,1)S(1)}, bf16[2,128,512]{2,1,0:T(8,128)(2,1)}, u32[]{:S(2)}) copy-start(bf16[2,128,512]{2,1,0:T(8,128)(2,1)} %pack_prefix.1.pack0) | copy-start | bytes 786436
  69.8 11.7 %copy-start.7 = (bf16[2,128,4096]{2,1,0:T(8,128)(2,1)S(1)}, bf16[2,128,4096]{2,1,0:T(8,128)(2,1)}, u32[]{:S(2)}) copy-start(bf16[2,128,4096]{2,1,0:T(8,128)(2,1)} %queries.1) | copy-start | bytes 6291460
  69.8 11.7 %copy-start.8 = (bf16[2,128,4096]{2,1,0:T(8,128)(2,1)S(1)}, bf16[2,128,4096]{2,1,0:T(8,128)(2,1)}, u32[]{:S(2)}) copy-start(bf16[2,128,4096]{2,1,0:T(8,128)(2,1)} %cotangent.5) | copy-start | bytes 6291460
  69.8 11.7 %copy-start.11 = (bf16[2,128,512]{2,1,0:T(8,128)(2,1)S(1)}, bf16[2,128,512]{2,1,0:T(8,128)(2,1)}, u32[]{:S(2)}) copy-start(bf16[2,128,512]{2,1,0:T(8,128)(2,1)} %own_keys.1) | copy-start | bytes 786436
  69.8 11.7 %copy-start.12 = (bf16[2,128,512]{2,1,0:T(8,128)(2,1)S(1)}, bf16[2,128,512]{2,1,0:T(8,128)(2,1)}, u32[]{:S(2)}) copy-start(bf16[2,128,512]{2,1,0:T(8,128)(2,1)} %own_values.1) | copy-start | bytes 786436
  69.9 11.7 %copy-start.17 = (s32[16]{0:T(128)S(1)}, s32[16]{0:T(128)}, u32[]{:S(2)}) copy-start(s32[16]{0:T(128)} %prefix_length.1) | copy-start | bytes 196
  81.6 31.0 %copy-start = (bf16[2,128,2304]{2,1,0:T(8,128)(2,1)S(1)}, bf16[2,128,2304]{2,1,0:T(8,128)(2,1)}, u32[]{:S(2)}) copy-start(bf16[2,128,2304]{2,1,0:T(8,128)(2,1)} %carry_cotangent.1.car0) | copy-start | bytes 3538948
  81.6 31.0 %copy-start.10 = (bf16[1,32,64,256]{3,2,1,0:T(8,128)(2,1)S(1)}, bf16[1,32,64,256]{3,2,1,0:T(8,128)(2,1)}, u32[]{:S(2)}) copy-start(bf16[1,32,64,256]{3,2,1,0:T(8,128)(2,1)} %param.31) | copy-start | bytes 3145732
  99.3 0.8 copy-start.2
  100.1 20.2 %collective-permute-start.12 = (bf16[2,144,512]{2,1,0:T(8,128)(2,1)S(1)}, bf16[2,144,512]{2,1,0:T(8,128)(2,1)S(1)}, u32[]{:S(2)}, u32[]{:S(2)}) collective-permute-start(bf16[2,144,512]{2,1,0:T(8,128)(2,1)S(1)} %get-tuple-element.35), channel_id=1, source_target_pairs={{0,15},{1,0},{2,1},{3,2},{4,3},{5,4},{6,5},{7,6},{8,7},{9,8},{10,9... | collective-permute-start | bytes 884744 | tf_op jit(solution)/shard_map/ppermute | solution.py:28
  100.1 1.6 %collective-permute-start.15 = (f32[4,2048]{1,0:T(4,128)S(1)}, f32[4,2048]{1,0:T(4,128)S(1)}, u32[]{:S(2)}, u32[]{:S(2)}) collective-permute-start(f32[4,2048]{1,0:T(4,128)S(1)} %get-tuple-element.41), channel_id=1, source_target_pairs={{0,1},{1,0},{2,3},{3,2},{4,5},{5,4},{6,7},{7,6},{8,9},{9,8},{10,11... | collective-permute-start | bytes 98312 | tf_op jit(solution)/shard_map/ppermute | solution.py:506
  101.8 4.0 %collective-permute-start.16 = (f32[4,2048]{1,0:T(4,128)S(1)}, f32[4,2048]{1,0:T(4,128)S(1)}, u32[]{:S(2)}, u32[]{:S(2)}) collective-permute-start(f32[4,2048]{1,0:T(4,128)S(1)} %add.28), channel_id=1, source_target_pairs={{0,2},{1,3},{2,0},{3,1},{4,6},{5,7},{6,4},{7,5},{8,10},{9,11},{10,... | collective-permute-start | bytes 98312 | tf_op jit(solution)/shard_map/ppermute | solution.py:506
  105.8 4.0 %collective-permute-start.17 = (f32[4,2048]{1,0:T(4,128)S(1)}, f32[4,2048]{1,0:T(4,128)S(1)}, u32[]{:S(2)}, u32[]{:S(2)}) collective-permute-start(f32[4,2048]{1,0:T(4,128)S(1)} %add.29), channel_id=1, source_target_pairs={{0,4},{1,5},{2,6},{3,7},{4,0},{5,1},{6,2},{7,3},{8,12},{9,13},{10,... | collective-permute-start | bytes 98312 | tf_op jit(solution)/shard_map/ppermute | solution.py:506
  109.8 9.6 %collective-permute-start.18 = (f32[4,2048]{1,0:T(4,128)S(1)}, f32[4,2048]{1,0:T(4,128)S(1)}, u32[]{:S(2)}, u32[]{:S(2)}) collective-permute-start(f32[4,2048]{1,0:T(4,128)S(1)} %add.30), channel_id=1, source_target_pairs={{0,8},{1,9},{2,10},{3,11},{4,12},{5,13},{6,14},{7,15},{8,0},{9,1},... | collective-permute-start | bytes 98312 | tf_op jit(solution)/shard_map/ppermute | solution.py:506
  109.8 11.2 %collective-permute-start.13 = (bf16[2,144,512]{2,1,0:T(8,128)(2,1)S(1)}, bf16[2,144,512]{2,1,0:T(8,128)(2,1)S(1)}, u32[]{:S(2)}, u32[]{:S(2)}) collective-permute-start(bf16[2,144,512]{2,1,0:T(8,128)(2,1)S(1)} %get-tuple-element.36), channel_id=1, source_target_pairs={{0,14},{1,15},{2,0},{3,1},{4,2},{5,3},{6,4},{7,5},{8,6},{9,7},{10,... | collective-permute-start | bytes 884744 | tf_op jit(solution)/shard_map/ppermute | solution.py:28
  112.5 13.1 %collective-permute-start.14 = (bf16[2,144,512]{2,1,0:T(8,128)(2,1)S(1)}, bf16[2,144,512]{2,1,0:T(8,128)(2,1)S(1)}, u32[]{:S(2)}, u32[]{:S(2)}) collective-permute-start(bf16[2,144,512]{2,1,0:T(8,128)(2,1)S(1)} %get-tuple-element.37), channel_id=1, source_target_pairs={{0,13},{1,14},{2,15},{3,0},{4,1},{5,2},{6,3},{7,4},{8,5},{9,6},{10... | collective-permute-start | bytes 884744 | tf_op jit(solution)/shard_map/ppermute | solution.py:28
  117.0 12.9 %collective-permute-start.6 = (bf16[2,128,256]{2,1,0:T(8,128)(2,1)S(1)}, bf16[2,128,256]{2,1,0:T(8,128)(2,1)S(1)}, u32[]{:S(2)}, u32[]{:S(2)}) collective-permute-start(bf16[2,128,256]{2,1,0:T(8,128)(2,1)S(1)} %get-tuple-element.28), channel_id=1, source_target_pairs={{0,1},{1,2},{2,3},{3,4},{4,5},{5,6},{6,7},{7,8},{8,9},{9,10},{10,1... | collective-permute-start | bytes 393224 | tf_op jit(solution)/shard_map/ppermute | solution.py:28
  119.4 10.5 %collective-permute-start.7 = (bf16[2,128,256]{2,1,0:T(8,128)(2,1)S(1)}, bf16[2,128,256]{2,1,0:T(8,128)(2,1)S(1)}, u32[]{:S(2)}, u32[]{:S(2)}) collective-permute-start(bf16[2,128,256]{2,1,0:T(8,128)(2,1)S(1)} %get-tuple-element.29), channel_id=1, source_target_pairs={{0,2},{1,3},{2,4},{3,5},{4,6},{5,7},{6,8},{7,9},{8,10},{9,11},{10,... | collective-permute-start | bytes 393224 | tf_op jit(solution)/shard_map/ppermute | solution.py:28
  120.3 5.3 %copy-start.19 = (bf16[2,144,512]{2,1,0:T(8,128)(2,1)}, bf16[2,144,512]{2,1,0:T(8,128)(2,1)S(1)}, u32[]{:S(2)}) copy-start(bf16[2,144,512]{2,1,0:T(8,128)(2,1)S(1)} %collective-permute-done.12.back1) | copy-start | bytes 884740
  120.3 9.6 %collective-permute-start.8 = (bf16[2,128,256]{2,1,0:T(8,128)(2,1)S(1)}, bf16[2,128,256]{2,1,0:T(8,128)(2,1)S(1)}, u32[]{:S(2)}, u32[]{:S(2)}) collective-permute-start(bf16[2,128,256]{2,1,0:T(8,128)(2,1)S(1)} %get-tuple-element.30), channel_id=1, source_target_pairs={{0,3},{1,4},{2,5},{3,6},{4,7},{5,8},{6,9},{7,10},{8,11},{9,12},{10... | collective-permute-start | bytes 393224 | tf_op jit(solution)/shard_map/ppermute | solution.py:28
  121.0 4.6 %copy-start.20 = (bf16[2,144,512]{2,1,0:T(8,128)(2,1)}, bf16[2,144,512]{2,1,0:T(8,128)(2,1)S(1)}, u32[]{:S(2)}) copy-start(bf16[2,144,512]{2,1,0:T(8,128)(2,1)S(1)} %collective-permute-done.13.back2) | copy-start | bytes 884740
  125.6 0.7 copy-start.21

commit v3 on v2

--- a/solution.py
+++ b/solution.py
@@ -40,19 +40,28 @@
     return lax.dot_general(a, b, (((1,), (0,)), ((), ())), preferred_element_type=F32)
 
 
-def pack_kernel(keys, values, out):
-    out[0] = keys[0]
-    out[1] = values[0]
-
-
-def pack(prefix_keys, prefix_values):
+def pack_kernel(keys, values, tail, out, rows8):
+    rows = keys.shape[1]
+    out[0, 0:rows, :] = keys[0]
+    out[1, 0:rows, :] = values[0]
+    rows8[...] = jnp.zeros_like(rows8)
+    rows8[5:8, :] = tail[0].astype(F32)
+    for half in range(2):
+        upper = rows8[:, half * 1024 : half * 1024 + 512]
+        lower = rows8[:, half * 1024 + 512 : half * 1024 + 1024]
+        out[half, rows : rows + 16, :] = jnp.concatenate([upper, lower], axis=0).astype(BF16)
+
+
+def pack(prefix_keys, prefix_values, prefix_tail):
+    rows, width = prefix_keys.shape[1:]
     return pl.pallas_call(
         pack_kernel,
-        out_shape=jax.ShapeDtypeStruct((2,) + prefix_keys.shape[1:], BF16),
-        in_specs=[VMEM] * 2,
+        out_shape=jax.ShapeDtypeStruct((2, rows + 16, width), BF16),
+        in_specs=[VMEM] * 3,
         out_specs=VMEM,
+        scratch_shapes=[pltpu.VMEM((8, prefix_tail.shape[2]), F32)],
         name="pack_prefix",
-    )(prefix_keys, prefix_values)
+    )(prefix_keys, prefix_values, prefix_tail)
 
 
 def running_sum(log_decay):
@@ -109,15 +118,21 @@
     return 0, 2, jnp.where(even, 1, 3), jnp.where(even, 3, 1)
 
 
-def gather(value, sign):
+def swap(value, by):
+    return lax.ppermute(value, "dp", [(i, i ^ by) for i in range(lax.axis_size("dp"))])
+
+
+def two_and_last(value, sign):
     length = lax.axis_size("dp")
-    two = shift(value, 2 * sign)
     if sign > 0:
         pairs = [(i, (i + (3 if i % 2 else 1)) % length) for i in range(length)]
     else:
         pairs = [(i, (i - (1 if i % 2 else 3)) % length) for i in range(length)]
-    last = lax.ppermute(value, "dp", pairs)
-    return [value, two, lax.ppermute(two, "dp", [(i, i ^ 1) for i in range(length)]), last]
+    return shift(value, 2 * sign), lax.ppermute(value, "dp", pairs)
+
+
+def after(value, *others):
+    return lax.optimization_barrier((value,) + others)[0]
 
 
 def distance_to(rank, owner, devices):
@@ -132,10 +147,10 @@
     resp_length,
     skip_gain,
     inputs,
-    tail0,
-    tail1,
-    tail2,
-    tail3,
+    pack0,
+    pack1,
+    pack2,
+    pack3,
     conv_weight,
     write,
     read,
@@ -156,11 +171,15 @@
     rank = rank_ref[0]
     live_to = resp_length[resp]
     gap = distance_to(rank, resp_prefix[2 * rank + resp], devices)
-    for step, tail in enumerate((tail0, tail1, tail2, tail3)):
+    for step, packed in zip(relayed(rank), (pack0, pack1, pack2, pack3)):
 
         @pl.when(gap == step)
-        def _(tail=tail):
-            padded[5:8, :] = tail[0].astype(F32)
+        def _(packed=packed):
+            for half in range(2):
+                rows = packed[half].astype(F32)
+                for part in range(2):
+                    lo = half * 1024 + part * 512
+                    padded[0:8, lo : lo + 512] = rows[8 * part : 8 * part + 8]
 
     padded[8 : 8 + length, :] = inputs[0].astype(F32)
     decay_sum, decay_rows = running_sum(log_decay[0])
@@ -220,12 +239,12 @@
     g_read[0] = tn(inner[...].astype(BF16), write[0])
 
 
-def mamba(rank, resp_prefix, resp_length, skip_gain, inputs, tails, conv_weight, write, read, log_decay, cotangent, devices):
+def mamba(rank, resp_prefix, resp_length, skip_gain, inputs, packs, conv_weight, write, read, log_decay, cotangent, devices):
     count, length, width = inputs.shape
     heads = log_decay.shape[1]
     states = read.shape[2]
     taps = conv_weight.shape[0]
-    whole = pl.BlockSpec(tails[0].shape, lambda r: (0, 0, 0))
+    whole = pl.BlockSpec((2, 16, packs[0].shape[2]), lambda r: (0, (packs[0].shape[1] - 16) // 16, 0))
     return pl.pallas_call(
         functools.partial(mamba_kernel, devices),
         grid=(count,),
@@ -265,7 +284,7 @@
         compiler_params=pltpu.CompilerParams(vmem_limit_bytes=32 * 2**20),
         cost_estimate=pl.CostEstimate(flops=2 * 10**9, bytes_accessed=8 * 2**20, transcendentals=10**6),
         name="mamba_grads",
-    )(rank, resp_prefix, resp_length, skip_gain, inputs, *tails, conv_weight, write, read, log_decay, cotangent)
+    )(rank, resp_prefix, resp_length, skip_gain, inputs, *packs, conv_weight, write, read, log_decay, cotangent)
 
 
 def attention_kernel(
@@ -361,7 +380,7 @@
 
 def attention(rank, resp_prefix, resp_length, prefix_length, queries, cotangent, own_keys, own_values, packs, g_tail, devices):
     count, length, width = queries.shape
-    rows = packs[0].shape[1]
+    rows = packs[0].shape[1] - 16
     group = REPEAT * ATT_DIM
     packed = pl.BlockSpec((2, rows, ATT_DIM), lambda h, r: (0, 0, h))
     back_block = pl.BlockSpec((2, rows + 16, ATT_DIM), lambda h, r: (0, 0, h))
@@ -478,7 +497,7 @@
         out[0] = total[0:rows]
         for part in range(2):
             lo = half * 1024 + part * 512
-            g_tail[0, :, lo : lo + 512] = total[rows + 8 * part : rows + 8 * part + 3]
+            g_tail[:, 0, lo : lo + 512] = total[rows + 8 * part : rows + 8 * part + 3]
 
 
 def sum_back(backs, tail_shape):
@@ -489,23 +508,12 @@
         out_shape=[
             jax.ShapeDtypeStruct((1, rows, width), F32),
             jax.ShapeDtypeStruct((1, rows, width), F32),
-            jax.ShapeDtypeStruct(tail_shape, F32),
+            jax.ShapeDtypeStruct((tail_shape[1], 1, tail_shape[2]), F32),
         ],
         in_specs=[VMEM] * 4,
         out_specs=[VMEM] * 3,
         name="sum_prefix",
     )(*backs)
-
-
-def all_sum(value):
-    length = lax.axis_size("dp")
-    if length & (length - 1):
-        return lax.psum(value, "dp")
-    by = 1
-    while by < length:
-        value = value + lax.ppermute(value, "dp", [(i, i ^ by) for i in range(length)])
-        by *= 2
-    return value
 
 
 def on_device(
@@ -537,28 +545,41 @@
     state = prefix_state.reshape(-1, states)
 
     decay = jnp.swapaxes(log_decay, 1, 2)
-    carries = gather(carry(resp_length, decay, out_cotangent, read), -1)
-    tails = [prefix_tail] + [shift(prefix_tail, by) for by in range(1, SPAN)]
-    packs = gather(pack(prefix_keys, prefix_values), 1)
+    packed = pack(prefix_keys, prefix_values, prefix_tail)
+    pack_two, pack_last = two_and_last(packed, 1)
+    carried = carry(after(resp_length, packed), decay, out_cotangent, read)
+    pack_two, pack_last, carried = lax.optimization_barrier((pack_two, pack_last, carried))
+    carry_two, carry_last = two_and_last(carried, -1)
+    pack_relay = swap(pack_two, 1)
+    packs = [packed, pack_two, pack_relay, pack_last]
     g_inputs, g_tail, g_conv, g_read = mamba(
-        rank, resp_prefix, resp_length, skip_gain, token_inputs, tails, conv_weight, write, read, decay, out_cotangent, devices
+        rank, resp_prefix, resp_length, skip_gain, token_inputs, packs, conv_weight, write, read, decay, out_cotangent, devices
     )
+    conv = g_conv + swap(g_conv, 1)
     g_queries, *backs = attention(
-        rank, resp_prefix, resp_length, prefix_length, queries, attn_cotangent, own_keys, own_values, packs, g_tail, devices
+        rank, resp_prefix, after(resp_length, carry_last), prefix_length, queries, attn_cotangent, own_keys, own_values, packs, g_tail, devices
     )
+    carry_two = after(carry_two, backs[1])
+    carry_relay = swap(carry_two, 1)
+    conv = after(conv, carry_two)
+    conv = conv + swap(conv, 2)
     backs = [backs[0]] + [shift(backs[by], -by) for by in range(1, SPAN)]
-    g_state, *reads = owner(rank, resp_prefix, state, carries, devices)
+    g_state, *reads = owner(rank, resp_prefix, state, [carried, carry_two, carry_relay, carry_last], devices)
+    by = 4
+    while by < devices:
+        conv = conv + (swap(conv, by) if devices & (devices - 1) == 0 else 0)
+        by *= 2
     for by in range(SPAN):
         g_read = g_read + (reads[by] if by == 0 else shift(reads[by], by).astype(F32))
     g_prefix_keys, g_prefix_values, g_prefix_tail = sum_back(backs, prefix_tail.shape)
     token_total = count * length * devices
-    grad_conv = all_sum(g_conv) * (1.0 / math.sqrt(token_total))
+    grad_conv = conv * (1.0 / math.sqrt(token_total))
     return (
         g_inputs,
         g_read.astype(BF16).reshape(state_out.shape),
         g_queries,
         g_state.reshape(prefix_state.shape),
-        g_prefix_tail,
+        jnp.swapaxes(g_prefix_tail, 0, 1),
         g_prefix_keys,
         g_prefix_values,
         grad_conv,

time: 131 us -> 101 us (0.77)
  waiting for transfers between devices: 68.3 us -> 35.1 us
  Pallas kernels: 41.6 us -> 43.3 us
  starting transfers between devices: 13.3 us -> 14.9 us
    ppermute x11 -> x8, waiting for transfers between devices: 59.3 us -> 9.96 us  [shift(): lax.ppermute(value, 'dp', [(i, (i + by) % length) for i in range(length)])]
    ppermute x8, waiting for transfers between devices: 8.93 us -> 25.1 us  [the longest x6 15.2 us: swap(): lax.ppermute(value, 'dp', [(i, i ^ by) for i in range(lax.axis_size('dp'))])]
    ppermute x8, starting transfers between devices: 1 us -> 9.69 us  [the longest x6 5.12 us: swap(): lax.ppermute(value, 'dp', [(i, i ^ by) for i in range(lax.axis_size('dp'))])]
    ppermute x11 -> x8, starting transfers between devices: 12.3 us -> 5.2 us  [shift(): lax.ppermute(value, 'dp', [(i, (i + by) % length) for i in range(length)])]
    unnamed x45 -> x42, local copies, waits for them, and re-layouts: 5.14 us -> 4.57 us
  transfers between devices with their start and end apart: 19 -> 16, of which waited for: 9 -> 8; matrix products, arithmetic and copies ran while one was open for 2% -> 1% of each run, Pallas kernels for 29% -> 42%
where the time goes in v3:
time: 101 us; the launch traced here: 100 us
  Pallas kernels  43.3 us (43%)
  waiting for transfers between devices  35.1 us (35%)
  starting transfers between devices  14.9 us (15%)
  local copies, waits for them, and re-layouts  4.57 us (5%)
  other arithmetic  1.4 us (1%)
    pallas_call x1, Pallas kernels, attention(): pl.pallas_call(functools.partial(attention_kernel, devices), grid=(KV_HEA...  18.1 us
    ppermute x6, waiting for transfers between devices, swap(): lax.ppermute(value, 'dp', [(i, i ^ by) for i in range(lax.axis_size('dp'))])  15.2 us
    pallas_call x1, Pallas kernels, mamba(): pl.pallas_call(functools.partial(mamba_kernel, devices), grid=(count,), o...  12.1 us
    ppermute x8, waiting for transfers between devices, shift(): lax.ppermute(value, 'dp', [(i, (i + by) % length) for i in range(length)])  9.96 us
    ppermute x2, waiting for transfers between devices, two_and_last(): return (shift(value, 2 * sign), lax.ppermute(value, 'dp', pairs))  9.92 us
    pallas_call x1, Pallas kernels, owner(): pl.pallas_call(functools.partial(owner_kernel, devices), out_shape=[jax.S...  5.23 us
    ppermute x8, starting transfers between devices, shift(): lax.ppermute(value, 'dp', [(i, (i + by) % length) for i in range(length)])  5.2 us
    ppermute x6, starting transfers between devices, swap(): lax.ppermute(value, 'dp', [(i, i ^ by) for i in range(lax.axis_size('dp'))])  5.12 us
  transfers between devices with their start and end apart: 16, of which 8 were waited for; matrix products, arithmetic and copies ran while one was open for 1% of the time, Pallas kernels for 42%

profile of v3, /device:TPU:0, one launch (start us, length us, event | category | flops | bytes accessed | tf_op | source)
XLA Modules:
  0.0 100.1 jit_solution(7795291848468632514)
XLA Ops:
  0.6 1.7 %pack_prefix.1.pack0 = bf16[2,144,512]{2,1,0:T(8,128)(2,1)} custom-call(bf16[1,128,512]{2,1,0:T(8,128)(2,1)} %keys.1, bf16[1,128,512]{2,1,0:T(8,128)(2,1)} %values.1, bf16[1,3,2048]{2,1,0:T(4,128)(2,1)} %tail.1), custom_call_target="tpu_custom_call" | custom-call | tf_op jit(solution)/shard_map/pack_prefix/pallas_call | solution.py:57
  2.4 0.5 collective-permute-start.1
  2.8 2.5 %collective-permute-start = (bf16[2,144,512]{2,1,0:T(8,128)(2,1)}, bf16[2,144,512]{2,1,0:T(8,128)(2,1)S(1)}, u32[]{:S(2)}, u32[]{:S(2)}) collective-permute-start(bf16[2,144,512]{2,1,0:T(8,128)(2,1)} %pack_prefix.1.pack0), channel_id=1, source_target_pairs={{0,2},{1,3},{2,4},{3,5},{4,6},{5,7},{6,8},{7,9},{8,10},{9,11},{10,... | collective-permute-start | bytes 884744 | tf_op jit(solution)/shard_map/ppermute | solution.py:28
  5.3 0.0 copy-start.6
  5.3 0.0 copy-start.15
  5.4 0.0 copy-start.17
  5.4 4.0 %carry_cotangent.1.car0 = bf16[2,128,2304]{2,1,0:T(8,128)(2,1)} custom-call(s32[2]{0:T(128)} %resp_length.3, f32[2,32,128]{2,1,0:T(8,128)} %bitcast.13, bf16[2,128,2048]{2,1,0:T(8,128)(2,1)} %cotangent.4, bf16[2,128,256]{2,1,0:T(8,128)(2,1)} %bitcast.11), custom_call_target="tpu_custom_call" | custom-call | tf_op jit(solution)/shard_map/carry_cotangent/pallas_call | solution.py:101
  9.4 2.1 %collective-permute-done.1.pack3 = bf16[2,144,512]{2,1,0:T(8,128)(2,1)S(1)} collective-permute-done((bf16[2,144,512]{2,1,0:T(8,128)(2,1)}, bf16[2,144,512]{2,1,0:T(8,128)(2,1)S(1)}, u32[]{:S(2)}, u32[]{:S(2)}) %collective-permute-start.1) | collective-permute-done | bytes 294944 | tf_op jit(solution)/shard_map/ppermute | solution.py:131
  11.5 4.9 %collective-permute-done.pack1 = bf16[2,144,512]{2,1,0:T(8,128)(2,1)S(1)} collective-permute-done((bf16[2,144,512]{2,1,0:T(8,128)(2,1)}, bf16[2,144,512]{2,1,0:T(8,128)(2,1)S(1)}, u32[]{:S(2)}, u32[]{:S(2)}) %collective-permute-start) | collective-permute-done | bytes 294944 | tf_op jit(solution)/shard_map/ppermute | solution.py:28
  16.3 4.1 %collective-permute-start.4 = (bf16[2,128,2304]{2,1,0:T(8,128)(2,1)}, bf16[2,128,2304]{2,1,0:T(8,128)(2,1)S(1)}, u32[]{:S(2)}, u32[]{:S(2)}) collective-permute-start(bf16[2,128,2304]{2,1,0:T(8,128)(2,1)} %carry_cotangent.1.car0), channel_id=1, source_target_pairs={{0,13},{1,0},{2,15},{3,2},{4,1},{5,4},{6,3},{7,6},{8,5},{9,8},{10,... | collective-permute-start | bytes 3538952 | tf_op jit(solution)/shard_map/ppermute | solution.py:131
  20.5 0.0 collective-permute-start.3
  20.5 0.0 collective-permute-start.2
  20.5 1.7 %collective-permute-done.2.pack2 = bf16[2,144,512]{2,1,0:T(8,128)(2,1)} collective-permute-done((bf16[2,144,512]{2,1,0:T(8,128)(2,1)S(1)}, bf16[2,144,512]{2,1,0:T(8,128)(2,1)}, u32[]{:S(2)}, u32[]{:S(2)}) %collective-permute-start.2) | collective-permute-done | bytes 294944 | tf_op jit(solution)/shard_map/ppermute | solution.py:122
  22.2 0.0 copy-start.9
  22.2 1.2 %copy-done.9 = bf16[2,128,2048]{2,1,0:T(8,128)(2,1)S(1)} copy-done((bf16[2,128,2048]{2,1,0:T(8,128)(2,1)S(1)}, bf16[2,128,2048]{2,1,0:T(8,128)(2,1)}, u32[]{:S(2)}) %copy-start.9) | copy-done | bytes 1048600
  23.5 0.9 copy-done.13
  24.4 0.8 copy-done.14
  25.1 0.0 copy-start.16
  25.1 12.1 %mamba_grads.1 = (bf16[2,128,2048]{2,1,0:T(8,128)(2,1)}, f32[2,4,8,512]{3,2,1,0:T(8,128)S(1)}, f32[4,2048]{1,0:T(4,128)S(1)}, f32[2,128,256]{2,1,0:T(8,128)S(1)}) custom-call(s32[1]{0:T(128)} %bitcast.rank_ref, s32[32]{0:T(128)S(1)} %copy-done.17, s32[2]{0:T(128)S(1)} %copy-done.6, f32[32]{0:T(128)S(1)} %copy-done.15, bf16[2,128,2048]{2,1,0:T(8,128)(2,1)S(1)} %copy-done.9, ...), custom_call_target="tpu_custom_call" | custom-call | flops 2000000000 | bytes 8388608 | tf_op jit(solution)/shard_map/mamba_grads/pallas_call | solution.py:248
  37.2 7.8 %collective-permute-done.4.car3 = bf16[2,128,2304]{2,1,0:T(8,128)(2,1)S(1)} collective-permute-done((bf16[2,128,2304]{2,1,0:T(8,128)(2,1)}, bf16[2,128,2304]{2,1,0:T(8,128)(2,1)S(1)}, u32[]{:S(2)}, u32[]{:S(2)}) %collective-permute-start.4) | collective-permute-done | bytes 1179680 | tf_op jit(solution)/shard_map/ppermute | solution.py:131
  45.1 0.0 copy-start.10
  45.1 18.1 %attention_grads.1 = (bf16[2,128,4096]{2,1,0:T(8,128)(2,1)}, f32[2,144,512]{2,1,0:T(8,128)S(1)}, bf16[2,144,512]{2,1,0:T(8,128)(2,1)S(1)}, bf16[2,144,512]{2,1,0:T(8,128)(2,1)S(1)}, bf16[2,144,512]{2,1,0:T(8,128)(2,1)S(1)}) custom-call(s32[1]{0:T(128)} %bitcast.rank_ref, s32[32]{0:T(128)S(1)} %copy-done.17, s32[2]{0:T(128)S(1)} %copy-done.6, ...), custom_call_target="tpu_custom_call" | custom-call | flops 4000000000 | bytes 8388608 | tf_op jit(solution)/shard_map/attention_grads/pallas_call | solution.py:388
  63.2 0.8 copy-done.2
  64.0 0.0 collective-permute-done.3.car1
  64.0 0.4 collective-permute-start.5
  64.4 0.0 collective-permute-start.10
  64.4 0.2 collective-permute-start.12
  64.5 2.4 %collective-permute-done.12 = f32[4,2048]{1,0:T(4,128)S(1)} collective-permute-done((f32[4,2048]{1,0:T(4,128)S(1)}, f32[4,2048]{1,0:T(4,128)S(1)}, u32[]{:S(2)}, u32[]{:S(2)}) %collective-permute-start.12) | collective-permute-done | bytes 32800 | tf_op jit(solution)/shard_map/ppermute | solution.py:122
  66.9 0.8 collective-permute-start.13
  67.7 6.5 %collective-permute-done.13 = f32[4,2048]{1,0:T(4,128)S(1)} collective-permute-done((f32[4,2048]{1,0:T(4,128)S(1)}, f32[4,2048]{1,0:T(4,128)S(1)}, u32[]{:S(2)}, u32[]{:S(2)}) %collective-permute-start.13) | collective-permute-done | bytes 32800 | tf_op jit(solution)/shard_map/ppermute | solution.py:122
  74.2 1.5 %collective-permute-start.14 = (f32[4,2048]{1,0:T(4,128)S(1)}, f32[4,2048]{1,0:T(4,128)S(1)}, u32[]{:S(2)}, u32[]{:S(2)}) collective-permute-start(f32[4,2048]{1,0:T(4,128)S(1)} %add.29), channel_id=1, source_target_pairs={{0,4},{1,5},{2,6},{3,7},{4,0},{5,1},{6,2},{7,3},{8,12},{9,13},{10,... | collective-permute-start | bytes 98312 | tf_op jit(solution)/shard_map/ppermute | solution.py:122
  75.7 2.6 %collective-permute-start.9 = (bf16[2,144,512]{2,1,0:T(8,128)(2,1)S(1)}, bf16[2,144,512]{2,1,0:T(8,128)(2,1)S(1)}, u32[]{:S(2)}, u32[]{:S(2)}) collective-permute-start(bf16[2,144,512]{2,1,0:T(8,128)(2,1)S(1)} %get-tuple-element.40), channel_id=1, source_target_pairs={{0,15},{1,0},{2,1},{3,2},{4,3},{5,4},{6,5},{7,6},{8,7},{9,8},{10,9... | collective-permute-start | bytes 884744 | tf_op jit(solution)/shard_map/ppermute | solution.py:28
  78.3 2.4 %collective-permute-start.15 = (f32[4,2048]{1,0:T(4,128)S(1)}, f32[4,2048]{1,0:T(4,128)S(1)}, u32[]{:S(2)}, u32[]{:S(2)}) collective-permute-start(f32[4,2048]{1,0:T(4,128)S(1)} %add.30), channel_id=1, source_target_pairs={{0,8},{1,9},{2,10},{3,11},{4,12},{5,13},{6,14},{7,15},{8,0},{9,1},... | collective-permute-start | bytes 98312 | tf_op jit(solution)/shard_map/ppermute | solution.py:122
  80.7 0.0 collective-permute-done.5.car2
  80.7 5.2 %owner_state.1 = (bf16[2048,256]{1,0:T(8,128)(2,1)}, f32[2,128,256]{2,1,0:T(8,128)S(1)}, bf16[2,128,256]{2,1,0:T(8,128)(2,1)S(1)}, bf16[2,128,256]{2,1,0:T(8,128)(2,1)S(1)}, bf16[2,128,256]{2,1,0:T(8,128)(2,1)S(1)}) custom-call(s32[1]{0:T(128)} %bitcast.rank_ref, s32[32]{0:T(128)S(1)} %copy-done.17, bf16[2048,256]{1,0:T(8,128)(2,1)S(1)} %bitcast.15, ...), custom_call_target="tpu_custom_call" | custom-call | flops 2000000000 | bytes 8388608 | tf_op jit(solution)/shard_map/owner_state/pallas_call | solution.py:478
  85.9 0.0 collective-permute-start.6
  85.9 4.6 %collective-permute-done.15 = f32[4,2048]{1,0:T(4,128)S(1)} collective-permute-done((f32[4,2048]{1,0:T(4,128)S(1)}, f32[4,2048]{1,0:T(4,128)S(1)}, u32[]{:S(2)}, u32[]{:S(2)}) %collective-permute-start.15) | collective-permute-done | bytes 32800 | tf_op jit(solution)/shard_map/ppermute | solution.py:122
  90.5 0.0 collective-permute-start.7
  90.6 0.0 collective-permute-done.10.back2
  90.6 0.1 collective-permute-start.8
  90.6 0.6 add_multiply_fusion
  91.3 0.0 collective-permute-done.11.back3
  91.3 0.0 collective-permute-done.9.back1
  91.3 0.7 copy-done.20
  92.0 0.1 copy-done.19
  92.1 2.2 %sum_prefix.1 = (f32[1,128,512]{2,1,0:T(8,128)}, f32[1,128,512]{2,1,0:T(8,128)}, f32[3,1,2048]{2,1,0:T(1,128)}) custom-call(f32[2,144,512]{2,1,0:T(8,128)} %copy-done.2, bf16[2,144,512]{2,1,0:T(8,128)(2,1)} %copy-done.19, bf16[2,144,512]{2,1,0:T(8,128)(2,1)} %copy-done.18, bf16[2,144,512]{2,1,0:T(8,128)(2,1)} %copy-done.20), custom_call_target="tpu_custom_call" | custom-call | tf_op jit(solution)/shard_map/sum_prefix/pallas_call | solution.py:506
  94.3 5.1 %collective-permute-done.7 = bf16[2,128,256]{2,1,0:T(8,128)(2,1)S(1)} collective-permute-done((bf16[2,128,256]{2,1,0:T(8,128)(2,1)S(1)}, bf16[2,128,256]{2,1,0:T(8,128)(2,1)S(1)}, u32[]{:S(2)}, u32[]{:S(2)}) %collective-permute-start.7) | collective-permute-done | bytes 131104 | tf_op jit(solution)/shard_map/ppermute | solution.py:28
  99.3 0.7 fusion
  (37 shorter events, 0.1 us)
Async XLA Ops:
  2.4 9.1 %collective-permute-start.1 = (bf16[2,144,512]{2,1,0:T(8,128)(2,1)}, bf16[2,144,512]{2,1,0:T(8,128)(2,1)S(1)}, u32[]{:S(2)}, u32[]{:S(2)}) collective-permute-start(bf16[2,144,512]{2,1,0:T(8,128)(2,1)} %pack_prefix.1.pack0), channel_id=1, source_target_pairs={{0,1},{1,4},{2,3},{3,6},{4,5},{5,8},{6,7},{7,10},{8,9},{9,12},{10,... | collective-permute-start | bytes 884744 | tf_op jit(solution)/shard_map/ppermute | solution.py:131
  2.8 13.5 %collective-permute-start = (bf16[2,144,512]{2,1,0:T(8,128)(2,1)}, bf16[2,144,512]{2,1,0:T(8,128)(2,1)S(1)}, u32[]{:S(2)}, u32[]{:S(2)}) collective-permute-start(bf16[2,144,512]{2,1,0:T(8,128)(2,1)} %pack_prefix.1.pack0), channel_id=1, source_target_pairs={{0,2},{1,3},{2,4},{3,5},{4,6},{5,7},{6,8},{7,9},{8,10},{9,11},{10,... | collective-permute-start | bytes 884744 | tf_op jit(solution)/shard_map/ppermute | solution.py:28
  5.3 16.9 %copy-start.1 = (bf16[2,128,2048]{2,1,0:T(8,128)(2,1)S(1)}, bf16[2,128,2048]{2,1,0:T(8,128)(2,1)}, u32[]{:S(2)}) copy-start(bf16[2,128,2048]{2,1,0:T(8,128)(2,1)} %cotangent.4) | copy-start | bytes 3145732
  5.3 16.9 %copy-start.3 = (bf16[2,144,512]{2,1,0:T(8,128)(2,1)S(1)}, bf16[2,144,512]{2,1,0:T(8,128)(2,1)}, u32[]{:S(2)}) copy-start(bf16[2,144,512]{2,1,0:T(8,128)(2,1)} %pack_prefix.1.pack0) | copy-start | bytes 884740
  5.3 16.9 %copy-start.4 = (bf16[2,128,1,256]{3,1,2,0:T(8,128)(2,1)S(1)}, bf16[2,128,1,256]{3,1,2,0:T(8,128)(2,1)}, u32[]{:S(2)}) copy-start(bf16[2,128,1,256]{3,1,2,0:T(8,128)(2,1)} %param.20) | copy-start | bytes 393220
  5.3 16.9 %copy-start.5 = (f32[2,128,32]{1,2,0:T(8,128)S(1)}, f32[2,128,32]{1,2,0:T(8,128)}, u32[]{:S(2)}) copy-start(f32[2,128,32]{1,2,0:T(8,128)} %param.21) | copy-start | bytes 98308
  5.3 16.9 %copy-start.6 = (s32[2]{0:T(128)S(1)}, s32[2]{0:T(128)}, u32[]{:S(2)}) copy-start(s32[2]{0:T(128)} %resp_length.3) | copy-start | bytes 28
  5.3 16.9 %copy-start.15 = (f32[32]{0:T(128)S(1)}, f32[32]{0:T(128)}, u32[]{:S(2)}) copy-start(f32[32]{0:T(128)} %skip_gain.1) | copy-start | bytes 388
  5.4 16.9 %copy-start.17 = (s32[32]{0:T(128)S(1)}, s32[32]{0:T(128)}, u32[]{:S(2)}) copy-start(s32[32]{0:T(128)} %resp_prefix.5) | copy-start | bytes 388
  16.3 28.7 %collective-permute-start.4 = (bf16[2,128,2304]{2,1,0:T(8,128)(2,1)}, bf16[2,128,2304]{2,1,0:T(8,128)(2,1)S(1)}, u32[]{:S(2)}, u32[]{:S(2)}) collective-permute-start(bf16[2,128,2304]{2,1,0:T(8,128)(2,1)} %carry_cotangent.1.car0), channel_id=1, source_target_pairs={{0,13},{1,0},{2,15},{3,2},{4,1},{5,4},{6,3},{7,6},{8,5},{9,8},{10,... | collective-permute-start | bytes 3538952 | tf_op jit(solution)/shard_map/ppermute | solution.py:131
  20.5 43.6 %collective-permute-start.3 = (bf16[2,128,2304]{2,1,0:T(8,128)(2,1)}, bf16[2,128,2304]{2,1,0:T(8,128)(2,1)}, u32[]{:S(2)}, u32[]{:S(2)}) collective-permute-start(bf16[2,128,2304]{2,1,0:T(8,128)(2,1)} %carry_cotangent.1.car0), channel_id=1, source_target_pairs={{0,14},{1,15},{2,0},{3,1},{4,2},{5,3},{6,4},{7,5},{8,6},{9,7},{10,... | collective-permute-start | bytes 3538952 | tf_op jit(solution)/shard_map/ppermute | solution.py:28
  20.5 1.7 %collective-permute-start.2 = (bf16[2,144,512]{2,1,0:T(8,128)(2,1)S(1)}, bf16[2,144,512]{2,1,0:T(8,128)(2,1)}, u32[]{:S(2)}, u32[]{:S(2)}) collective-permute-start(bf16[2,144,512]{2,1,0:T(8,128)(2,1)S(1)} %collective-permute-done.pack1), channel_id=1, source_target_pairs={{0,1},{1,0},{2,3},{3,2},{4,5},{5,4},{6,7},{7,6},{8,9},{9,8},{10,11... | collective-permute-start | bytes 884744 | tf_op jit(solution)/shard_map/ppermute | solution.py:122
  22.2 1.2 %copy-start.9 = (bf16[2,128,2048]{2,1,0:T(8,128)(2,1)S(1)}, bf16[2,128,2048]{2,1,0:T(8,128)(2,1)}, u32[]{:S(2)}) copy-start(bf16[2,128,2048]{2,1,0:T(8,128)(2,1)} %inputs.1) | copy-start | bytes 3145732
  23.5 0.9 copy-start.13
  24.4 0.8 copy-start.14
  25.1 19.9 %copy-start.7 = (bf16[2,128,4096]{2,1,0:T(8,128)(2,1)S(1)}, bf16[2,128,4096]{2,1,0:T(8,128)(2,1)}, u32[]{:S(2)}) copy-start(bf16[2,128,4096]{2,1,0:T(8,128)(2,1)} %queries.1) | copy-start | bytes 6291460
  25.1 19.9 %copy-start.8 = (bf16[2,128,4096]{2,1,0:T(8,128)(2,1)S(1)}, bf16[2,128,4096]{2,1,0:T(8,128)(2,1)}, u32[]{:S(2)}) copy-start(bf16[2,128,4096]{2,1,0:T(8,128)(2,1)} %cotangent.5) | copy-start | bytes 6291460
  25.1 19.9 %copy-start.11 = (bf16[2,128,512]{2,1,0:T(8,128)(2,1)S(1)}, bf16[2,128,512]{2,1,0:T(8,128)(2,1)}, u32[]{:S(2)}) copy-start(bf16[2,128,512]{2,1,0:T(8,128)(2,1)} %own_keys.1) | copy-start | bytes 786436
  25.1 19.9 %copy-start.12 = (bf16[2,128,512]{2,1,0:T(8,128)(2,1)S(1)}, bf16[2,128,512]{2,1,0:T(8,128)(2,1)}, u32[]{:S(2)}) copy-start(bf16[2,128,512]{2,1,0:T(8,128)(2,1)} %own_values.1) | copy-start | bytes 786436
  25.1 19.9 %copy-start.16 = (s32[16]{0:T(128)S(1)}, s32[16]{0:T(128)}, u32[]{:S(2)}) copy-start(s32[16]{0:T(128)} %prefix_length.1) | copy-start | bytes 196
  45.1 35.6 %copy-start = (bf16[2,128,2304]{2,1,0:T(8,128)(2,1)S(1)}, bf16[2,128,2304]{2,1,0:T(8,128)(2,1)}, u32[]{:S(2)}) copy-start(bf16[2,128,2304]{2,1,0:T(8,128)(2,1)} %carry_cotangent.1.car0) | copy-start | bytes 3538948
  45.1 35.6 %copy-start.10 = (bf16[1,32,64,256]{3,2,1,0:T(8,128)(2,1)S(1)}, bf16[1,32,64,256]{3,2,1,0:T(8,128)(2,1)}, u32[]{:S(2)}) copy-start(bf16[1,32,64,256]{3,2,1,0:T(8,128)(2,1)} %param.31) | copy-start | bytes 3145732
  63.2 0.8 copy-start.2
  64.0 16.6 %collective-permute-start.5 = (bf16[2,128,2304]{2,1,0:T(8,128)(2,1)}, bf16[2,128,2304]{2,1,0:T(8,128)(2,1)S(1)}, u32[]{:S(2)}, u32[]{:S(2)}) collective-permute-start(bf16[2,128,2304]{2,1,0:T(8,128)(2,1)} %collective-permute-done.3.car1), channel_id=1, source_target_pairs={{0,1},{1,0},{2,3},{3,2},{4,5},{5,4},{6,7},{7,6},{8,9},{9,8},{10,11... | collective-permute-start | bytes 3538952 | tf_op jit(solution)/shard_map/ppermute | solution.py:122
  64.4 26.2 %collective-permute-start.10 = (bf16[2,144,512]{2,1,0:T(8,128)(2,1)S(1)}, bf16[2,144,512]{2,1,0:T(8,128)(2,1)S(1)}, u32[]{:S(2)}, u32[]{:S(2)}) collective-permute-start(bf16[2,144,512]{2,1,0:T(8,128)(2,1)S(1)} %get-tuple-element.49), channel_id=1, source_target_pairs={{0,14},{1,15},{2,0},{3,1},{4,2},{5,3},{6,4},{7,5},{8,6},{9,7},{10,... | collective-permute-start | bytes 884744 | tf_op jit(solution)/shard_map/ppermute | solution.py:28
  64.4 2.5 %collective-permute-start.12 = (f32[4,2048]{1,0:T(4,128)S(1)}, f32[4,2048]{1,0:T(4,128)S(1)}, u32[]{:S(2)}, u32[]{:S(2)}) collective-permute-start(f32[4,2048]{1,0:T(4,128)S(1)} %get-tuple-element.54), channel_id=1, source_target_pairs={{0,1},{1,0},{2,3},{3,2},{4,5},{5,4},{6,7},{7,6},{8,9},{9,8},{10,11... | collective-permute-start | bytes 98312 | tf_op jit(solution)/shard_map/ppermute | solution.py:122
  66.9 7.2 %collective-permute-start.13 = (f32[4,2048]{1,0:T(4,128)S(1)}, f32[4,2048]{1,0:T(4,128)S(1)}, u32[]{:S(2)}, u32[]{:S(2)}) collective-permute-start(f32[4,2048]{1,0:T(4,128)S(1)} %add.28), channel_id=1, source_target_pairs={{0,2},{1,3},{2,0},{3,1},{4,6},{5,7},{6,4},{7,5},{8,10},{9,11},{10,... | collective-permute-start | bytes 98312 | tf_op jit(solution)/shard_map/ppermute | solution.py:122
  74.2 4.1 %collective-permute-start.14 = (f32[4,2048]{1,0:T(4,128)S(1)}, f32[4,2048]{1,0:T(4,128)S(1)}, u32[]{:S(2)}, u32[]{:S(2)}) collective-permute-start(f32[4,2048]{1,0:T(4,128)S(1)} %add.29), channel_id=1, source_target_pairs={{0,4},{1,5},{2,6},{3,7},{4,0},{5,1},{6,2},{7,3},{8,12},{9,13},{10,... | collective-permute-start | bytes 98312 | tf_op jit(solution)/shard_map/ppermute | solution.py:122
  75.7 15.6 %collective-permute-start.9 = (bf16[2,144,512]{2,1,0:T(8,128)(2,1)S(1)}, bf16[2,144,512]{2,1,0:T(8,128)(2,1)S(1)}, u32[]{:S(2)}, u32[]{:S(2)}) collective-permute-start(bf16[2,144,512]{2,1,0:T(8,128)(2,1)S(1)} %get-tuple-element.40), channel_id=1, source_target_pairs={{0,15},{1,0},{2,1},{3,2},{4,3},{5,4},{6,5},{7,6},{8,7},{9,8},{10,9... | collective-permute-start | bytes 884744 | tf_op jit(solution)/shard_map/ppermute | solution.py:28
  78.3 13.0 %collective-permute-start.11 = (bf16[2,144,512]{2,1,0:T(8,128)(2,1)S(1)}, bf16[2,144,512]{2,1,0:T(8,128)(2,1)S(1)}, u32[]{:S(2)}, u32[]{:S(2)}) collective-permute-start(bf16[2,144,512]{2,1,0:T(8,128)(2,1)S(1)} %get-tuple-element.50), channel_id=1, source_target_pairs={{0,13},{1,14},{2,15},{3,0},{4,1},{5,2},{6,3},{7,4},{8,5},{9,6},{10... | collective-permute-start | bytes 884744 | tf_op jit(solution)/shard_map/ppermute | solution.py:28
  78.3 12.2 %collective-permute-start.15 = (f32[4,2048]{1,0:T(4,128)S(1)}, f32[4,2048]{1,0:T(4,128)S(1)}, u32[]{:S(2)}, u32[]{:S(2)}) collective-permute-start(f32[4,2048]{1,0:T(4,128)S(1)} %add.30), channel_id=1, source_target_pairs={{0,8},{1,9},{2,10},{3,11},{4,12},{5,13},{6,14},{7,15},{8,0},{9,1},... | collective-permute-start | bytes 98312 | tf_op jit(solution)/shard_map/ppermute | solution.py:122
  85.9 8.4 %collective-permute-start.6 = (bf16[2,128,256]{2,1,0:T(8,128)(2,1)S(1)}, bf16[2,128,256]{2,1,0:T(8,128)(2,1)S(1)}, u32[]{:S(2)}, u32[]{:S(2)}) collective-permute-start(bf16[2,128,256]{2,1,0:T(8,128)(2,1)S(1)} %get-tuple-element.43), channel_id=1, source_target_pairs={{0,1},{1,2},{2,3},{3,4},{4,5},{5,6},{6,7},{7,8},{8,9},{9,10},{10,1... | collective-permute-start | bytes 393224 | tf_op jit(solution)/shard_map/ppermute | solution.py:28
  90.5 8.8 %collective-permute-start.7 = (bf16[2,128,256]{2,1,0:T(8,128)(2,1)S(1)}, bf16[2,128,256]{2,1,0:T(8,128)(2,1)S(1)}, u32[]{:S(2)}, u32[]{:S(2)}) collective-permute-start(bf16[2,128,256]{2,1,0:T(8,128)(2,1)S(1)} %get-tuple-element.44), channel_id=1, source_target_pairs={{0,2},{1,3},{2,4},{3,5},{4,6},{5,7},{6,8},{7,9},{8,10},{9,11},{10,... | collective-permute-start | bytes 393224 | tf_op jit(solution)/shard_map/ppermute | solution.py:28
  90.6 0.7 copy-start.18
  90.6 8.8 %collective-permute-start.8 = (bf16[2,128,256]{2,1,0:T(8,128)(2,1)S(1)}, bf16[2,128,256]{2,1,0:T(8,128)(2,1)S(1)}, u32[]{:S(2)}, u32[]{:S(2)}) collective-permute-start(bf16[2,128,256]{2,1,0:T(8,128)(2,1)S(1)} %get-tuple-element.45), channel_id=1, source_target_pairs={{0,3},{1,4},{2,5},{3,6},{4,7},{5,8},{6,9},{7,10},{8,11},{9,12},{10... | collective-permute-start | bytes 393224 | tf_op jit(solution)/shard_map/ppermute | solution.py:28
  91.3 0.7 copy-start.20
  91.3 0.8 copy-start.19

commit v4 on v2

--- a/solution.py
+++ b/solution.py
@@ -104,20 +104,12 @@
     )(resp_length, log_decay, out_cotangent, state_out)
 
 
-def relayed(rank):
-    even = rank % 2 == 0
-    return 0, 2, jnp.where(even, 1, 3), jnp.where(even, 3, 1)
-
-
-def gather(value, sign):
-    length = lax.axis_size("dp")
-    two = shift(value, 2 * sign)
-    if sign > 0:
-        pairs = [(i, (i + (3 if i % 2 else 1)) % length) for i in range(length)]
-    else:
-        pairs = [(i, (i - (1 if i % 2 else 3)) % length) for i in range(length)]
-    last = lax.ppermute(value, "dp", pairs)
-    return [value, two, lax.ppermute(two, "dp", [(i, i ^ 1) for i in range(length)]), last]
+def swap(value, by):
+    return lax.ppermute(value, "dp", [(i, i ^ by) for i in range(lax.axis_size("dp"))])
+
+
+def after(value, *others):
+    return lax.optimization_barrier((value,) + others)[0]
 
 
 def distance_to(rank, owner, devices):
@@ -209,6 +201,7 @@
         ]
         rows = jnp.concatenate(rows, axis=0)
 
+
         @pl.when(resp == 0)
         def _(rows=rows, lanes=lanes):
             g_conv[:, lanes] = rows
@@ -301,7 +294,7 @@
     live_to = resp_length[resp]
     scale = 1.0 / math.sqrt(ATT_DIM)
     gap = distance_to(rank, prefix, devices)
-    for step, packed in zip(relayed(rank), (pack0, pack1, pack2, pack3)):
+    for step, packed in enumerate((pack0, pack1, pack2, pack3)):
 
         @pl.when(gap == step)
         def _(packed=packed):
@@ -326,19 +319,21 @@
         d_out = jnp.concatenate(
             [jnp.where(live, cotangent[0, :, span].astype(F32), 0.0).astype(BF16) for span in spans], axis=0
         )
-        scores = nt(all_keys, query) * scale + bias
+        scores = nt(all_keys, query) * (scale * math.log2(math.e)) + bias
         top = jnp.max(scores, axis=0, keepdims=True)
-        raised = jnp.exp(scores - top)
+        raised = jnp.exp2(scores - top)
         probs = raised * (1.0 / jnp.sum(raised, axis=0, keepdims=True))
         probs_low = probs.astype(BF16)
         d_probs = nt(all_values, d_out)
-        delta = jnp.sum(probs_low.astype(F32) * d_probs, axis=0, keepdims=True)
-        d_scores = (probs * ((d_probs - delta) * scale)).astype(BF16)
-        g_query = tn(d_scores, all_keys)
+        delta = jnp.sum(probs * d_probs, axis=0, keepdims=True)
+        d_scores = (probs * (d_probs - delta)).astype(BF16)
+        g_query = tn(d_scores, all_keys) * scale
         for i, span in enumerate(spans):
             g_queries[0, :, span] = g_query[i * length : (i + 1) * length].astype(BF16)
         g_keys = g_keys + nn(d_scores[0:rows], query)
         g_values = g_values + nn(probs_low[0:rows], d_out)
+
+    g_keys = g_keys * scale
 
     @pl.when(resp == 0)
     def _():
@@ -354,9 +349,8 @@
             back[0, 0:rows, :] = (kept[0] * one + g_keys * two).astype(back.dtype)
             back[1, 0:rows, :] = (kept[1] * one + g_values * two).astype(back.dtype)
             for half in range(2):
-                upper = g_tail[0, 2 * half] * one + g_tail[1, 2 * half] * two
-                lower = g_tail[0, 2 * half + 1] * one + g_tail[1, 2 * half + 1] * two
-                back[half, rows : rows + 16, :] = jnp.concatenate([upper, lower], axis=0).astype(back.dtype)
+                tiles = [g_tail[0, part] * one + g_tail[1, part] * two for part in (2 * half, 2 * half + 1)]
+                back[half, rows : rows + 16, :] = jnp.concatenate(tiles, axis=0).astype(back.dtype)
 
 
 def attention(rank, resp_prefix, resp_length, prefix_length, queries, cotangent, own_keys, own_values, packs, g_tail, devices):
@@ -478,7 +472,7 @@
         out[0] = total[0:rows]
         for part in range(2):
             lo = half * 1024 + part * 512
-            g_tail[0, :, lo : lo + 512] = total[rows + 8 * part : rows + 8 * part + 3]
+            g_tail[:, 0, lo : lo + 512] = total[rows + 8 * part : rows + 8 * part + 3]
 
 
 def sum_back(backs, tail_shape):
@@ -489,23 +483,12 @@
         out_shape=[
             jax.ShapeDtypeStruct((1, rows, width), F32),
             jax.ShapeDtypeStruct((1, rows, width), F32),
-            jax.ShapeDtypeStruct(tail_shape, F32),
+            jax.ShapeDtypeStruct((tail_shape[1], 1, tail_shape[2]), F32),
         ],
         in_specs=[VMEM] * 4,
         out_specs=[VMEM] * 3,
         name="sum_prefix",
     )(*backs)
-
-
-def all_sum(value):
-    length = lax.axis_size("dp")
-    if length & (length - 1):
-        return lax.psum(value, "dp")
-    by = 1
-    while by < length:
-        value = value + lax.ppermute(value, "dp", [(i, i ^ by) for i in range(length)])
-        by *= 2
-    return value
 
 
 def on_device(
@@ -537,28 +520,57 @@
     state = prefix_state.reshape(-1, states)
 
     decay = jnp.swapaxes(log_decay, 1, 2)
-    carries = gather(carry(resp_length, decay, out_cotangent, read), -1)
     tails = [prefix_tail] + [shift(prefix_tail, by) for by in range(1, SPAN)]
-    packs = gather(pack(prefix_keys, prefix_values), 1)
-    g_inputs, g_tail, g_conv, g_read = mamba(
-        rank, resp_prefix, resp_length, skip_gain, token_inputs, tails, conv_weight, write, read, decay, out_cotangent, devices
+    packed = pack(prefix_keys, prefix_values)
+    packs = [packed] + [shift(packed, by) for by in range(1, SPAN)]
+    carried = carry(after(resp_length, packed, *tails), decay, out_cotangent, read)
+    carry_two = shift(carried, -2)
+    carry_last = lax.ppermute(carried, "dp", [(i, (i - (1 if i % 2 else 3)) % devices) for i in range(devices)])
+    g_inputs, g_tail, conv, g_read = mamba(
+        rank, resp_prefix, after(resp_length, carried), skip_gain, token_inputs, tails, conv_weight, write, read, decay, out_cotangent, devices
     )
+    steps = [by for by in (4, 8, 1, 2) if by < devices]
+    while 2 * max(steps) < devices:
+        steps.append(2 * max(steps))
+    whole = devices & (devices - 1) == 0
+    swaps = iter(steps if whole else [])
+
+    def next_step():
+        by = next(swaps, None)
+        return jnp.zeros_like(conv) if by is None else swap(conv, by)
+
+    moved = next_step()
     g_queries, *backs = attention(
         rank, resp_prefix, resp_length, prefix_length, queries, attn_cotangent, own_keys, own_values, packs, g_tail, devices
     )
+    *backs, moved, carry_two = lax.optimization_barrier((*backs, moved, carry_two))
+    conv = conv + moved
+    moved = next_step()
+    carry_relay = swap(carry_two, 1)
     backs = [backs[0]] + [shift(backs[by], -by) for by in range(1, SPAN)]
-    g_state, *reads = owner(rank, resp_prefix, state, carries, devices)
-    for by in range(SPAN):
-        g_read = g_read + (reads[by] if by == 0 else shift(reads[by], by).astype(F32))
-    g_prefix_keys, g_prefix_values, g_prefix_tail = sum_back(backs, prefix_tail.shape)
+    g_state, *reads = owner(rank, resp_prefix, state, [carried, carry_two, carry_relay, carry_last], devices)
+    *reads, moved = lax.optimization_barrier((*reads, moved))
+    conv = conv + moved
+    moved = next_step()
+    reads = [reads[0]] + [shift(reads[by], by) for by in range(1, SPAN)]
+    sums = sum_back(backs, prefix_tail.shape)
+    *sums, moved, r0, r1, r2, r3 = lax.optimization_barrier((*sums, moved, *reads))
+    g_prefix_keys, g_prefix_values, g_prefix_tail = sums
+    conv = conv + moved
+    for by in swaps:
+        conv = conv + swap(conv, by)
+    if not whole:
+        conv = lax.psum(conv, "dp")
+    for part in (r0, r1, r2, r3):
+        g_read = g_read + part.astype(F32)
     token_total = count * length * devices
-    grad_conv = all_sum(g_conv) * (1.0 / math.sqrt(token_total))
+    grad_conv = conv * (1.0 / math.sqrt(token_total))
     return (
         g_inputs,
         g_read.astype(BF16).reshape(state_out.shape),
         g_queries,
         g_state.reshape(prefix_state.shape),
-        g_prefix_tail,
+        jnp.swapaxes(g_prefix_tail, 0, 1),
         g_prefix_keys,
         g_prefix_values,
         grad_conv,

time: 131 us -> 108 us (0.82)
  waiting for transfers between devices: 68.3 us -> 36.1 us
  starting transfers between devices: 13.3 us -> 25.1 us
    ppermute x11 -> x13, waiting for transfers between devices: 59.3 us -> 21.7 us  [shift(): lax.ppermute(value, 'dp', [(i, (i + by) % length) for i in range(length)])]
    ppermute x8 -> x6, starting transfers between devices: 1 us -> 8.26 us  [the longest x5 4.98 us: swap(): lax.ppermute(value, 'dp', [(i, i ^ by) for i in range(lax.axis_size('dp'))])]
    ppermute x8 -> x6, waiting for transfers between devices: 8.93 us -> 14.4 us  [the longest x5 14.4 us: swap(): lax.ppermute(value, 'dp', [(i, i ^ by) for i in range(lax.axis_size('dp'))])]
    ppermute x11 -> x13, starting transfers between devices: 12.3 us -> 16.8 us  [shift(): lax.ppermute(value, 'dp', [(i, (i + by) % length) for i in range(length)])]
    unnamed x45 -> x44, local copies, waits for them, and re-layouts: 5.14 us -> 4.33 us
  transfers between devices with their start and end apart: 19 -> 19, of which waited for: 9 -> 8; matrix products, arithmetic and copies ran while one was open for 2% -> 1% of each run, Pallas kernels for 29% -> 34%
where the time goes in v4:
time: 108 us
  Pallas kernels  40.5 us (38%)
  waiting for transfers between devices  36.1 us (33%)
  starting transfers between devices  25.1 us (23%)
  local copies, waits for them, and re-layouts  4.33 us (4%)
  other arithmetic  1.38 us (1%)
    ppermute x13, waiting for transfers between devices, shift(): lax.ppermute(value, 'dp', [(i, (i + by) % length) for i in range(length)])  21.7 us
    pallas_call x1, Pallas kernels, attention(): pl.pallas_call(functools.partial(attention_kernel, devices), grid=(KV_HEA...  17.6 us
    ppermute x13, starting transfers between devices, shift(): lax.ppermute(value, 'dp', [(i, (i + by) % length) for i in range(length)])  16.8 us
    ppermute x5, waiting for transfers between devices, swap(): lax.ppermute(value, 'dp', [(i, i ^ by) for i in range(lax.axis_size('dp'))])  14.4 us
    pallas_call x1, Pallas kernels, mamba(): pl.pallas_call(functools.partial(mamba_kernel, devices), grid=(count,), o...  11.7 us
    ppermute x5, starting transfers between devices, swap(): lax.ppermute(value, 'dp', [(i, i ^ by) for i in range(lax.axis_size('dp'))])  4.98 us
    unnamed x44, local copies, waits for them, and re-layouts  4.33 us
    pallas_call x1, Pallas kernels, carry(): pl.pallas_call(carry_kernel, grid=(count,), out_shape=jax.ShapeDtypeStruc...  4 us
  transfers between devices with their start and end apart: 19, of which 8 were waited for; matrix products, arithmetic and copies ran while one was open for 1% of the time, Pallas kernels for 34%

profile of v4, /device:TPU:0, one launch (start us, length us, event | category | flops | bytes accessed | tf_op | source)
XLA Modules:
  0.0 108.2 jit_solution(1430356657231854028)
XLA Ops:
  0.6 0.5 collective-permute-start
  1.1 2.6 %collective-permute-start.1 = (bf16[1,3,2048]{2,1,0:T(4,128)(2,1)}, bf16[1,3,2048]{2,1,0:T(4,128)(2,1)S(1)}, u32[]{:S(2)}, u32[]{:S(2)}) collective-permute-start(bf16[1,3,2048]{2,1,0:T(4,128)(2,1)} %tail0.1), channel_id=1, source_target_pairs={{0,2},{1,3},{2,4},{3,5},{4,6},{5,7},{6,8},{7,9},{8,10},{9,11},{10,... | collective-permute-start | bytes 36872 | tf_op jit(solution)/shard_map/ppermute | solution.py:28
  3.7 2.4 %collective-permute-start.2 = (bf16[1,3,2048]{2,1,0:T(4,128)(2,1)}, bf16[1,3,2048]{2,1,0:T(4,128)(2,1)S(1)}, u32[]{:S(2)}, u32[]{:S(2)}) collective-permute-start(bf16[1,3,2048]{2,1,0:T(4,128)(2,1)} %tail0.1), channel_id=1, source_target_pairs={{0,3},{1,4},{2,5},{3,6},{4,7},{5,8},{6,9},{7,10},{8,11},{9,12},{10... | collective-permute-start | bytes 36872 | tf_op jit(solution)/shard_map/ppermute | solution.py:28
  6.1 1.7 %pack_prefix.1.pack0 = bf16[2,128,512]{2,1,0:T(8,128)(2,1)} custom-call(bf16[1,128,512]{2,1,0:T(8,128)(2,1)} %keys.1, bf16[1,128,512]{2,1,0:T(8,128)(2,1)} %values.1), custom_call_target="tpu_custom_call" | custom-call | tf_op jit(solution)/shard_map/pack_prefix/pallas_call | solution.py:49
  7.8 0.9 collective-permute-done.1.tail2
  8.7 0.2 collective-permute-done.2.tail3
  8.9 0.0 copy-start.6
  8.9 0.0 copy-start.14
  8.9 0.0 copy-start.15
  8.9 0.0 copy-start.16
  9.0 0.0 copy-start.18
  9.0 4.0 %carry_cotangent.1.car0 = bf16[2,128,2304]{2,1,0:T(8,128)(2,1)} custom-call(s32[2]{0:T(128)} %resp_length.3, f32[2,32,128]{2,1,0:T(8,128)} %bitcast.13, bf16[2,128,2048]{2,1,0:T(8,128)(2,1)} %cotangent.4, bf16[2,128,256]{2,1,0:T(8,128)(2,1)} %bitcast.11), custom_call_target="tpu_custom_call" | custom-call | tf_op jit(solution)/shard_map/carry_cotangent/pallas_call | solution.py:92
  13.0 2.5 %collective-permute-start.7 = (bf16[2,128,2304]{2,1,0:T(8,128)(2,1)}, bf16[2,128,2304]{2,1,0:T(8,128)(2,1)S(1)}, u32[]{:S(2)}, u32[]{:S(2)}) collective-permute-start(bf16[2,128,2304]{2,1,0:T(8,128)(2,1)} %carry_cotangent.1.car0), channel_id=1, source_target_pairs={{0,14},{1,15},{2,0},{3,1},{4,2},{5,3},{6,4},{7,5},{8,6},{9,7},{10,... | collective-permute-start | bytes 3538952 | tf_op jit(solution)/shard_map/ppermute | solution.py:28
  15.5 1.4 %collective-permute-start.4 = (bf16[2,128,512]{2,1,0:T(8,128)(2,1)S(1)}, bf16[2,128,512]{2,1,0:T(8,128)(2,1)S(1)}, u32[]{:S(2)}, u32[]{:S(2)}) collective-permute-start(bf16[2,128,512]{2,1,0:T(8,128)(2,1)S(1)} %copy-done.3), channel_id=1, source_target_pairs={{0,2},{1,3},{2,4},{3,5},{4,6},{5,7},{6,8},{7,9},{8,10},{9,11},{10,... | collective-permute-start | bytes 786440 | tf_op jit(solution)/shard_map/ppermute | solution.py:28
  16.9 0.3 collective-permute-start.5
  17.2 3.3 %collective-permute-start.12 = (bf16[2,128,2304]{2,1,0:T(8,128)(2,1)}, bf16[2,128,2304]{2,1,0:T(8,128)(2,1)S(1)}, u32[]{:S(2)}, u32[]{:S(2)}) collective-permute-start(bf16[2,128,2304]{2,1,0:T(8,128)(2,1)} %carry_cotangent.1.car0), channel_id=1, source_target_pairs={{0,13},{1,0},{2,15},{3,2},{4,1},{5,4},{6,3},{7,6},{8,5},{9,8},{10,... | collective-permute-start | bytes 3538952 | tf_op jit(solution)/shard_map/ppermute | solution.py:528
  20.5 0.0 copy-start.9
  20.5 1.2 %copy-done.9 = bf16[2,128,2048]{2,1,0:T(8,128)(2,1)S(1)} copy-done((bf16[2,128,2048]{2,1,0:T(8,128)(2,1)S(1)}, bf16[2,128,2048]{2,1,0:T(8,128)(2,1)}, u32[]{:S(2)}) %copy-start.9) | copy-done | bytes 1048600
  21.7 0.9 copy-done.13
  22.6 0.0 copy-start.17
  22.7 11.7 %mamba_grads.1 = (bf16[2,128,2048]{2,1,0:T(8,128)(2,1)}, f32[2,4,8,512]{3,2,1,0:T(8,128)S(1)}, f32[4,2048]{1,0:T(4,128)S(1)}, f32[2,128,256]{2,1,0:T(8,128)S(1)}) custom-call(s32[1]{0:T(128)} %bitcast.rank_ref, s32[32]{0:T(128)S(1)} %copy-done.18, s32[2]{0:T(128)S(1)} %copy-done.6, f32[32]{0:T(128)S(1)} %copy-done.16, bf16[2,128,2048]{2,1,0:T(8,128)(2,1)S(1)} %copy-done.9, ...), custom_call_target="tpu_custom_call" | custom-call | flops 2000000000 | bytes 8388608 | tf_op jit(solution)/shard_map/mamba_grads/pallas_call | solution.py:222
  34.3 12.2 %collective-permute-done.4.pack2 = bf16[2,128,512]{2,1,0:T(8,128)(2,1)S(1)} collective-permute-done((bf16[2,128,512]{2,1,0:T(8,128)(2,1)S(1)}, bf16[2,128,512]{2,1,0:T(8,128)(2,1)S(1)}, u32[]{:S(2)}, u32[]{:S(2)}) %collective-permute-start.4) | collective-permute-done | bytes 262176 | tf_op jit(solution)/shard_map/ppermute | solution.py:28
  46.5 5.5 %collective-permute-done.5.pack3 = bf16[2,128,512]{2,1,0:T(8,128)(2,1)} collective-permute-done((bf16[2,128,512]{2,1,0:T(8,128)(2,1)S(1)}, bf16[2,128,512]{2,1,0:T(8,128)(2,1)}, u32[]{:S(2)}, u32[]{:S(2)}) %collective-permute-start.5) | collective-permute-done | bytes 262176 | tf_op jit(solution)/shard_map/ppermute | solution.py:28
  52.0 0.0 copy-start.10
  52.1 17.6 %attention_grads.1 = (bf16[2,128,4096]{2,1,0:T(8,128)(2,1)}, f32[2,144,512]{2,1,0:T(8,128)S(1)}, bf16[2,144,512]{2,1,0:T(8,128)(2,1)S(1)}, bf16[2,144,512]{2,1,0:T(8,128)(2,1)S(1)}, bf16[2,144,512]{2,1,0:T(8,128)(2,1)S(1)}) custom-call(s32[1]{0:T(128)} %bitcast.rank_ref, s32[32]{0:T(128)S(1)} %copy-done.18, s32[2]{0:T(128)S(1)} %copy-done.6, ...), custom_call_target="tpu_custom_call" | custom-call | flops 4000000000 | bytes 8388608 | tf_op jit(solution)/shard_map/attention_grads/pallas_call | solution.py:363
  69.7 0.8 copy-done.2
  70.5 0.0 collective-permute-done.6
  70.5 0.0 collective-permute-start.11
  70.6 3.6 %collective-permute-start.8 = (bf16[2,144,512]{2,1,0:T(8,128)(2,1)S(1)}, bf16[2,144,512]{2,1,0:T(8,128)(2,1)S(1)}, u32[]{:S(2)}, u32[]{:S(2)}) collective-permute-start(bf16[2,144,512]{2,1,0:T(8,128)(2,1)S(1)} %get-tuple-element.57), channel_id=1, source_target_pairs={{0,15},{1,0},{2,1},{3,2},{4,3},{5,4},{6,5},{7,6},{8,7},{9,8},{10,9... | collective-permute-start | bytes 884744 | tf_op jit(solution)/shard_map/ppermute | solution.py:28
  74.1 0.3 collective-permute-start.9
  74.5 0.8 collective-permute-start.10
  75.3 0.0 collective-permute-done.12.car3
  75.3 0.5 collective-permute-start.13
  75.8 3.3 %owner_state.1 = (bf16[2048,256]{1,0:T(8,128)(2,1)}, f32[2,128,256]{2,1,0:T(8,128)S(1)}, bf16[2,128,256]{2,1,0:T(8,128)(2,1)S(1)}, bf16[2,128,256]{2,1,0:T(8,128)(2,1)S(1)}, bf16[2,128,256]{2,1,0:T(8,128)(2,1)S(1)}) custom-call(s32[1]{0:T(128)} %bitcast.rank_ref, s32[32]{0:T(128)S(1)} %copy-done.18, bf16[2048,256]{1,0:T(8,128)(2,1)S(1)} %bitcast.15, ...), custom_call_target="tpu_custom_call" | custom-call | flops 2000000000 | bytes 8388608 | tf_op jit(solution)/shard_map/owner_state/pallas_call | solution.py:453
  79.1 13.2 %collective-permute-done.13 = f32[4,2048]{1,0:T(4,128)S(1)} collective-permute-done((f32[4,2048]{1,0:T(4,128)S(1)}, f32[4,2048]{1,0:T(4,128)S(1)}, u32[]{:S(2)}, u32[]{:S(2)}) %collective-permute-start.13) | collective-permute-done | bytes 32800 | tf_op jit(solution)/shard_map/ppermute | solution.py:108
  92.3 0.0 collective-permute-start.15
  92.3 0.0 collective-permute-start.16
  92.4 2.5 %collective-permute-start.17 = (bf16[2,128,256]{2,1,0:T(8,128)(2,1)S(1)}, bf16[2,128,256]{2,1,0:T(8,128)(2,1)S(1)}, u32[]{:S(2)}, u32[]{:S(2)}) collective-permute-start(bf16[2,128,256]{2,1,0:T(8,128)(2,1)S(1)} %get-tuple-element.73), channel_id=1, source_target_pairs={{0,3},{1,4},{2,5},{3,6},{4,7},{5,8},{6,9},{7,10},{8,11},{9,12},{10... | collective-permute-start | bytes 393224 | tf_op jit(solution)/shard_map/ppermute | solution.py:28
  94.8 0.1 collective-permute-start.14
  95.0 0.6 copy-done.20
  95.6 0.7 copy-done.21
  96.3 2.2 %sum_prefix.1 = (f32[1,128,512]{2,1,0:T(8,128)}, f32[1,128,512]{2,1,0:T(8,128)}, f32[3,1,2048]{2,1,0:T(1,128)}) custom-call(f32[2,144,512]{2,1,0:T(8,128)} %copy-done.2, bf16[2,144,512]{2,1,0:T(8,128)(2,1)} %copy-done.19, bf16[2,144,512]{2,1,0:T(8,128)(2,1)} %copy-done.20, bf16[2,144,512]{2,1,0:T(8,128)(2,1)} %copy-done.21), custom_call_target="tpu_custom_call" | custom-call | tf_op jit(solution)/shard_map/sum_prefix/pallas_call | solution.py:481
  98.5 1.8 %collective-permute-done.15 = bf16[2,128,256]{2,1,0:T(8,128)(2,1)S(1)} collective-permute-done((bf16[2,128,256]{2,1,0:T(8,128)(2,1)S(1)}, bf16[2,128,256]{2,1,0:T(8,128)(2,1)S(1)}, u32[]{:S(2)}, u32[]{:S(2)}) %collective-permute-start.15) | collective-permute-done | bytes 131104 | tf_op jit(solution)/shard_map/ppermute | solution.py:28
  100.3 1.1 %collective-permute-done.16 = bf16[2,128,256]{2,1,0:T(8,128)(2,1)S(1)} collective-permute-done((bf16[2,128,256]{2,1,0:T(8,128)(2,1)S(1)}, bf16[2,128,256]{2,1,0:T(8,128)(2,1)S(1)}, u32[]{:S(2)}, u32[]{:S(2)}) %collective-permute-start.16) | collective-permute-done | bytes 131104 | tf_op jit(solution)/shard_map/ppermute | solution.py:28
  101.4 4.3 %collective-permute-start.18 = (f32[4,2048]{1,0:T(4,128)S(1)}, f32[4,2048]{1,0:T(4,128)S(1)}, u32[]{:S(2)}, u32[]{:S(2)}) collective-permute-start(f32[4,2048]{1,0:T(4,128)S(1)} %add.30), channel_id=1, source_target_pairs={{0,2},{1,3},{2,0},{3,1},{4,6},{5,7},{6,4},{7,5},{8,10},{9,11},{10,... | collective-permute-start | bytes 98312 | tf_op jit(solution)/shard_map/ppermute | solution.py:108
  105.7 0.7 fusion
  106.4 1.2 %collective-permute-done.18 = f32[4,2048]{1,0:T(4,128)S(1)} collective-permute-done((f32[4,2048]{1,0:T(4,128)S(1)}, f32[4,2048]{1,0:T(4,128)S(1)}, u32[]{:S(2)}, u32[]{:S(2)}) %collective-permute-start.18) | collective-permute-done | bytes 32800 | tf_op jit(solution)/shard_map/ppermute | solution.py:108
  107.6 0.6 add_multiply_fusion
  (45 shorter events, 0.1 us)
Async XLA Ops:
  0.6 7.2 %collective-permute-start = (bf16[1,3,2048]{2,1,0:T(4,128)(2,1)}, bf16[1,3,2048]{2,1,0:T(4,128)(2,1)S(1)}, u32[]{:S(2)}, u32[]{:S(2)}) collective-permute-start(bf16[1,3,2048]{2,1,0:T(4,128)(2,1)} %tail0.1), channel_id=1, source_target_pairs={{0,1},{1,2},{2,3},{3,4},{4,5},{5,6},{6,7},{7,8},{8,9},{9,10},{10,1... | collective-permute-start | bytes 36872 | tf_op jit(solution)/shard_map/ppermute | solution.py:28
  1.1 7.6 %collective-permute-start.1 = (bf16[1,3,2048]{2,1,0:T(4,128)(2,1)}, bf16[1,3,2048]{2,1,0:T(4,128)(2,1)S(1)}, u32[]{:S(2)}, u32[]{:S(2)}) collective-permute-start(bf16[1,3,2048]{2,1,0:T(4,128)(2,1)} %tail0.1), channel_id=1, source_target_pairs={{0,2},{1,3},{2,4},{3,5},{4,6},{5,7},{6,8},{7,9},{8,10},{9,11},{10,... | collective-permute-start | bytes 36872 | tf_op jit(solution)/shard_map/ppermute | solution.py:28
  3.7 5.2 %collective-permute-start.2 = (bf16[1,3,2048]{2,1,0:T(4,128)(2,1)}, bf16[1,3,2048]{2,1,0:T(4,128)(2,1)S(1)}, u32[]{:S(2)}, u32[]{:S(2)}) collective-permute-start(bf16[1,3,2048]{2,1,0:T(4,128)(2,1)} %tail0.1), channel_id=1, source_target_pairs={{0,3},{1,4},{2,5},{3,6},{4,7},{5,8},{6,9},{7,10},{8,11},{9,12},{10... | collective-permute-start | bytes 36872 | tf_op jit(solution)/shard_map/ppermute | solution.py:28
  8.9 6.6 %copy-start.3 = (bf16[2,128,512]{2,1,0:T(8,128)(2,1)S(1)}, bf16[2,128,512]{2,1,0:T(8,128)(2,1)}, u32[]{:S(2)}) copy-start(bf16[2,128,512]{2,1,0:T(8,128)(2,1)} %pack_prefix.1.pack0) | copy-start | bytes 786436
  8.9 11.6 %copy-start.1 = (bf16[2,128,2048]{2,1,0:T(8,128)(2,1)S(1)}, bf16[2,128,2048]{2,1,0:T(8,128)(2,1)}, u32[]{:S(2)}) copy-start(bf16[2,128,2048]{2,1,0:T(8,128)(2,1)} %cotangent.4) | copy-start | bytes 3145732
  8.9 11.6 %copy-start.4 = (bf16[2,128,1,256]{3,1,2,0:T(8,128)(2,1)S(1)}, bf16[2,128,1,256]{3,1,2,0:T(8,128)(2,1)}, u32[]{:S(2)}) copy-start(bf16[2,128,1,256]{3,1,2,0:T(8,128)(2,1)} %param.20) | copy-start | bytes 393220
  8.9 11.6 %copy-start.5 = (f32[2,128,32]{1,2,0:T(8,128)S(1)}, f32[2,128,32]{1,2,0:T(8,128)}, u32[]{:S(2)}) copy-start(f32[2,128,32]{1,2,0:T(8,128)} %param.21) | copy-start | bytes 98308
  8.9 11.6 %copy-start.6 = (s32[2]{0:T(128)S(1)}, s32[2]{0:T(128)}, u32[]{:S(2)}) copy-start(s32[2]{0:T(128)} %resp_length.3) | copy-start | bytes 28
  8.9 11.5 %copy-start.14 = (f32[4,2048]{1,0:T(4,128)S(1)}, f32[4,2048]{1,0:T(4,128)}, u32[]{:S(2)}) copy-start(f32[4,2048]{1,0:T(4,128)} %conv_weight.1) | copy-start | bytes 98308
  8.9 11.5 %copy-start.15 = (bf16[1,3,2048]{2,1,0:T(4,128)(2,1)S(1)}, bf16[1,3,2048]{2,1,0:T(4,128)(2,1)}, u32[]{:S(2)}) copy-start(bf16[1,3,2048]{2,1,0:T(4,128)(2,1)} %tail0.1) | copy-start | bytes 36868
  8.9 11.5 %copy-start.16 = (f32[32]{0:T(128)S(1)}, f32[32]{0:T(128)}, u32[]{:S(2)}) copy-start(f32[32]{0:T(128)} %skip_gain.1) | copy-start | bytes 388
  9.0 11.5 %copy-start.18 = (s32[32]{0:T(128)S(1)}, s32[32]{0:T(128)}, u32[]{:S(2)}) copy-start(s32[32]{0:T(128)} %resp_prefix.5) | copy-start | bytes 388
  13.0 57.6 %collective-permute-start.7 = (bf16[2,128,2304]{2,1,0:T(8,128)(2,1)}, bf16[2,128,2304]{2,1,0:T(8,128)(2,1)S(1)}, u32[]{:S(2)}, u32[]{:S(2)}) collective-permute-start(bf16[2,128,2304]{2,1,0:T(8,128)(2,1)} %carry_cotangent.1.car0), channel_id=1, source_target_pairs={{0,14},{1,15},{2,0},{3,1},{4,2},{5,3},{6,4},{7,5},{8,6},{9,7},{10,... | collective-permute-start | bytes 3538952 | tf_op jit(solution)/shard_map/ppermute | solution.py:28
  15.5 18.8 %collective-permute-start.3 = (bf16[2,128,512]{2,1,0:T(8,128)(2,1)S(1)}, bf16[2,128,512]{2,1,0:T(8,128)(2,1)S(1)}, u32[]{:S(2)}, u32[]{:S(2)}) collective-permute-start(bf16[2,128,512]{2,1,0:T(8,128)(2,1)S(1)} %copy-done.3), channel_id=1, source_target_pairs={{0,1},{1,2},{2,3},{3,4},{4,5},{5,6},{6,7},{7,8},{8,9},{9,10},{10,1... | collective-permute-start | bytes 786440 | tf_op jit(solution)/shard_map/ppermute | solution.py:28
  15.5 31.0 %collective-permute-start.4 = (bf16[2,128,512]{2,1,0:T(8,128)(2,1)S(1)}, bf16[2,128,512]{2,1,0:T(8,128)(2,1)S(1)}, u32[]{:S(2)}, u32[]{:S(2)}) collective-permute-start(bf16[2,128,512]{2,1,0:T(8,128)(2,1)S(1)} %copy-done.3), channel_id=1, source_target_pairs={{0,2},{1,3},{2,4},{3,5},{4,6},{5,7},{6,8},{7,9},{8,10},{9,11},{10,... | collective-permute-start | bytes 786440 | tf_op jit(solution)/shard_map/ppermute | solution.py:28
  16.9 35.1 %collective-permute-start.5 = (bf16[2,128,512]{2,1,0:T(8,128)(2,1)S(1)}, bf16[2,128,512]{2,1,0:T(8,128)(2,1)}, u32[]{:S(2)}, u32[]{:S(2)}) collective-permute-start(bf16[2,128,512]{2,1,0:T(8,128)(2,1)S(1)} %copy-done.3), channel_id=1, source_target_pairs={{0,3},{1,4},{2,5},{3,6},{4,7},{5,8},{6,9},{7,10},{8,11},{9,12},{10... | collective-permute-start | bytes 786440 | tf_op jit(solution)/shard_map/ppermute | solution.py:28
  17.2 58.1 %collective-permute-start.12 = (bf16[2,128,2304]{2,1,0:T(8,128)(2,1)}, bf16[2,128,2304]{2,1,0:T(8,128)(2,1)S(1)}, u32[]{:S(2)}, u32[]{:S(2)}) collective-permute-start(bf16[2,128,2304]{2,1,0:T(8,128)(2,1)} %carry_cotangent.1.car0), channel_id=1, source_target_pairs={{0,13},{1,0},{2,15},{3,2},{4,1},{5,4},{6,3},{7,6},{8,5},{9,8},{10,... | collective-permute-start | bytes 3538952 | tf_op jit(solution)/shard_map/ppermute | solution.py:528
  20.5 1.2 %copy-start.9 = (bf16[2,128,2048]{2,1,0:T(8,128)(2,1)S(1)}, bf16[2,128,2048]{2,1,0:T(8,128)(2,1)}, u32[]{:S(2)}) copy-start(bf16[2,128,2048]{2,1,0:T(8,128)(2,1)} %inputs.1) | copy-start | bytes 3145732
  21.7 0.9 copy-start.13
  22.6 29.4 %copy-start.7 = (bf16[2,128,4096]{2,1,0:T(8,128)(2,1)S(1)}, bf16[2,128,4096]{2,1,0:T(8,128)(2,1)}, u32[]{:S(2)}) copy-start(bf16[2,128,4096]{2,1,0:T(8,128)(2,1)} %queries.1) | copy-start | bytes 6291460
  22.6 29.4 %copy-start.8 = (bf16[2,128,4096]{2,1,0:T(8,128)(2,1)S(1)}, bf16[2,128,4096]{2,1,0:T(8,128)(2,1)}, u32[]{:S(2)}) copy-start(bf16[2,128,4096]{2,1,0:T(8,128)(2,1)} %cotangent.5) | copy-start | bytes 6291460
  22.6 29.4 %copy-start.11 = (bf16[2,128,512]{2,1,0:T(8,128)(2,1)S(1)}, bf16[2,128,512]{2,1,0:T(8,128)(2,1)}, u32[]{:S(2)}) copy-start(bf16[2,128,512]{2,1,0:T(8,128)(2,1)} %own_keys.1) | copy-start | bytes 786436
  22.6 29.4 %copy-start.12 = (bf16[2,128,512]{2,1,0:T(8,128)(2,1)S(1)}, bf16[2,128,512]{2,1,0:T(8,128)(2,1)}, u32[]{:S(2)}) copy-start(bf16[2,128,512]{2,1,0:T(8,128)(2,1)} %own_values.1) | copy-start | bytes 786436
  22.6 29.4 %copy-start.17 = (s32[16]{0:T(128)S(1)}, s32[16]{0:T(128)}, u32[]{:S(2)}) copy-start(s32[16]{0:T(128)} %prefix_length.1) | copy-start | bytes 196
  34.3 36.2 %collective-permute-start.6 = (f32[4,2048]{1,0:T(4,128)S(1)}, f32[4,2048]{1,0:T(4,128)S(1)}, u32[]{:S(2)}, u32[]{:S(2)}) collective-permute-start(f32[4,2048]{1,0:T(4,128)S(1)} %get-tuple-element.55), channel_id=1, source_target_pairs={{0,4},{1,5},{2,6},{3,7},{4,0},{5,1},{6,2},{7,3},{8,12},{9,13},{10,... | collective-permute-start | bytes 98312 | tf_op jit(solution)/shard_map/ppermute | solution.py:108
  52.0 23.8 %copy-start = (bf16[2,128,2304]{2,1,0:T(8,128)(2,1)S(1)}, bf16[2,128,2304]{2,1,0:T(8,128)(2,1)}, u32[]{:S(2)}) copy-start(bf16[2,128,2304]{2,1,0:T(8,128)(2,1)} %carry_cotangent.1.car0) | copy-start | bytes 3538948
  52.0 23.8 %copy-start.10 = (bf16[1,32,64,256]{3,2,1,0:T(8,128)(2,1)S(1)}, bf16[1,32,64,256]{3,2,1,0:T(8,128)(2,1)}, u32[]{:S(2)}) copy-start(bf16[1,32,64,256]{3,2,1,0:T(8,128)(2,1)} %param.31) | copy-start | bytes 3145732
  69.7 0.8 copy-start.2
  70.5 5.3 %collective-permute-start.11 = (bf16[2,128,2304]{2,1,0:T(8,128)(2,1)S(1)}, bf16[2,128,2304]{2,1,0:T(8,128)(2,1)S(1)}, u32[]{:S(2)}, u32[]{:S(2)}) collective-permute-start(bf16[2,128,2304]{2,1,0:T(8,128)(2,1)S(1)} %collective-permute-done.7.car1), channel_id=1, source_target_pairs={{0,1},{1,0},{2,3},{3,2},{4,5},{5,4},{6,7},{7,6},{8,9},{9,8},{10,11... | collective-permute-start | bytes 3538952 | tf_op jit(solution)/shard_map/ppermute | solution.py:108
  70.6 21.8 %collective-permute-start.8 = (bf16[2,144,512]{2,1,0:T(8,128)(2,1)S(1)}, bf16[2,144,512]{2,1,0:T(8,128)(2,1)S(1)}, u32[]{:S(2)}, u32[]{:S(2)}) collective-permute-start(bf16[2,144,512]{2,1,0:T(8,128)(2,1)S(1)} %get-tuple-element.57), channel_id=1, source_target_pairs={{0,15},{1,0},{2,1},{3,2},{4,3},{5,4},{6,5},{7,6},{8,7},{9,8},{10,9... | collective-permute-start | bytes 884744 | tf_op jit(solution)/shard_map/ppermute | solution.py:28
  74.1 20.7 %collective-permute-start.9 = (bf16[2,144,512]{2,1,0:T(8,128)(2,1)S(1)}, bf16[2,144,512]{2,1,0:T(8,128)(2,1)S(1)}, u32[]{:S(2)}, u32[]{:S(2)}) collective-permute-start(bf16[2,144,512]{2,1,0:T(8,128)(2,1)S(1)} %get-tuple-element.58), channel_id=1, source_target_pairs={{0,14},{1,15},{2,0},{3,1},{4,2},{5,3},{6,4},{7,5},{8,6},{9,7},{10,... | collective-permute-start | bytes 884744 | tf_op jit(solution)/shard_map/ppermute | solution.py:28
  74.5 20.5 %collective-permute-start.10 = (bf16[2,144,512]{2,1,0:T(8,128)(2,1)S(1)}, bf16[2,144,512]{2,1,0:T(8,128)(2,1)S(1)}, u32[]{:S(2)}, u32[]{:S(2)}) collective-permute-start(bf16[2,144,512]{2,1,0:T(8,128)(2,1)S(1)} %get-tuple-element.59), channel_id=1, source_target_pairs={{0,13},{1,14},{2,15},{3,0},{4,1},{5,2},{6,3},{7,4},{8,5},{9,6},{10... | collective-permute-start | bytes 884744 | tf_op jit(solution)/shard_map/ppermute | solution.py:28
  75.3 17.1 %collective-permute-start.13 = (f32[4,2048]{1,0:T(4,128)S(1)}, f32[4,2048]{1,0:T(4,128)S(1)}, u32[]{:S(2)}, u32[]{:S(2)}) collective-permute-start(f32[4,2048]{1,0:T(4,128)S(1)} %add.24), channel_id=1, source_target_pairs={{0,8},{1,9},{2,10},{3,11},{4,12},{5,13},{6,14},{7,15},{8,0},{9,1},... | collective-permute-start | bytes 98312 | tf_op jit(solution)/shard_map/ppermute | solution.py:108
  92.3 7.9 %collective-permute-start.15 = (bf16[2,128,256]{2,1,0:T(8,128)(2,1)S(1)}, bf16[2,128,256]{2,1,0:T(8,128)(2,1)S(1)}, u32[]{:S(2)}, u32[]{:S(2)}) collective-permute-start(bf16[2,128,256]{2,1,0:T(8,128)(2,1)S(1)} %get-tuple-element.71), channel_id=1, source_target_pairs={{0,1},{1,2},{2,3},{3,4},{4,5},{5,6},{6,7},{7,8},{8,9},{9,10},{10,1... | collective-permute-start | bytes 393224 | tf_op jit(solution)/shard_map/ppermute | solution.py:28
  92.3 9.0 %collective-permute-start.16 = (bf16[2,128,256]{2,1,0:T(8,128)(2,1)S(1)}, bf16[2,128,256]{2,1,0:T(8,128)(2,1)S(1)}, u32[]{:S(2)}, u32[]{:S(2)}) collective-permute-start(bf16[2,128,256]{2,1,0:T(8,128)(2,1)S(1)} %get-tuple-element.72), channel_id=1, source_target_pairs={{0,2},{1,3},{2,4},{3,5},{4,6},{5,7},{6,8},{7,9},{8,10},{9,11},{10,... | collective-permute-start | bytes 393224 | tf_op jit(solution)/shard_map/ppermute | solution.py:28
  92.3 2.6 %copy-start.19 = (bf16[2,144,512]{2,1,0:T(8,128)(2,1)}, bf16[2,144,512]{2,1,0:T(8,128)(2,1)S(1)}, u32[]{:S(2)}) copy-start(bf16[2,144,512]{2,1,0:T(8,128)(2,1)S(1)} %collective-permute-done.8.back1) | copy-start | bytes 884740
  92.4 9.0 %collective-permute-start.17 = (bf16[2,128,256]{2,1,0:T(8,128)(2,1)S(1)}, bf16[2,128,256]{2,1,0:T(8,128)(2,1)S(1)}, u32[]{:S(2)}, u32[]{:S(2)}) collective-permute-start(bf16[2,128,256]{2,1,0:T(8,128)(2,1)S(1)} %get-tuple-element.73), channel_id=1, source_target_pairs={{0,3},{1,4},{2,5},{3,6},{4,7},{5,8},{6,9},{7,10},{8,11},{9,12},{10... | collective-permute-start | bytes 393224 | tf_op jit(solution)/shard_map/ppermute | solution.py:28
  94.8 0.7 copy-start.20
  94.8 3.6 %collective-permute-start.14 = (f32[4,2048]{1,0:T(4,128)S(1)}, f32[4,2048]{1,0:T(4,128)S(1)}, u32[]{:S(2)}, u32[]{:S(2)}) collective-permute-start(f32[4,2048]{1,0:T(4,128)S(1)} %add.25), channel_id=1, source_target_pairs={{0,1},{1,0},{2,3},{3,2},{4,5},{5,4},{6,7},{7,6},{8,9},{9,8},{10,11... | collective-permute-start | bytes 98312 | tf_op jit(solution)/shard_map/ppermute | solution.py:108
  95.6 0.7 copy-start.21
  101.4 6.2 %collective-permute-start.18 = (f32[4,2048]{1,0:T(4,128)S(1)}, f32[4,2048]{1,0:T(4,128)S(1)}, u32[]{:S(2)}, u32[]{:S(2)}) collective-permute-start(f32[4,2048]{1,0:T(4,128)S(1)} %add.30), channel_id=1, source_target_pairs={{0,2},{1,3},{2,0},{3,1},{4,6},{5,7},{6,4},{7,5},{8,10},{9,11},{10,... | collective-permute-start | bytes 98312 | tf_op jit(solution)/shard_map/ppermute | solution.py:108

commit v5 on v3

--- a/solution.py
+++ b/solution.py
@@ -228,6 +228,7 @@
         ]
         rows = jnp.concatenate(rows, axis=0)
 
+
         @pl.when(resp == 0)
         def _(rows=rows, lanes=lanes):
             g_conv[:, lanes] = rows
@@ -281,7 +282,7 @@
             pltpu.VMEM((length + 16, width), F32),
             pltpu.VMEM((length, length), F32),
         ],
-        compiler_params=pltpu.CompilerParams(vmem_limit_bytes=32 * 2**20),
+        compiler_params=pltpu.CompilerParams(vmem_limit_bytes=58 * 2**20),
         cost_estimate=pl.CostEstimate(flops=2 * 10**9, bytes_accessed=8 * 2**20, transcendentals=10**6),
         name="mamba_grads",
     )(rank, resp_prefix, resp_length, skip_gain, inputs, *packs, conv_weight, write, read, log_decay, cotangent)
@@ -345,19 +346,21 @@
         d_out = jnp.concatenate(
             [jnp.where(live, cotangent[0, :, span].astype(F32), 0.0).astype(BF16) for span in spans], axis=0
         )
-        scores = nt(all_keys, query) * scale + bias
+        scores = nt(all_keys, query) * (scale * math.log2(math.e)) + bias
         top = jnp.max(scores, axis=0, keepdims=True)
-        raised = jnp.exp(scores - top)
+        raised = jnp.exp2(scores - top)
         probs = raised * (1.0 / jnp.sum(raised, axis=0, keepdims=True))
         probs_low = probs.astype(BF16)
         d_probs = nt(all_values, d_out)
-        delta = jnp.sum(probs_low.astype(F32) * d_probs, axis=0, keepdims=True)
-        d_scores = (probs * ((d_probs - delta) * scale)).astype(BF16)
-        g_query = tn(d_scores, all_keys)
+        delta = jnp.sum(probs * d_probs, axis=0, keepdims=True)
+        d_scores = (probs * (d_probs - delta)).astype(BF16)
+        g_query = tn(d_scores, all_keys) * scale
         for i, span in enumerate(spans):
             g_queries[0, :, span] = g_query[i * length : (i + 1) * length].astype(BF16)
         g_keys = g_keys + nn(d_scores[0:rows], query)
         g_values = g_values + nn(probs_low[0:rows], d_out)
+
+    g_keys = g_keys * scale
 
     @pl.when(resp == 0)
     def _():
@@ -373,9 +376,8 @@
             back[0, 0:rows, :] = (kept[0] * one + g_keys * two).astype(back.dtype)
             back[1, 0:rows, :] = (kept[1] * one + g_values * two).astype(back.dtype)
             for half in range(2):
-                upper = g_tail[0, 2 * half] * one + g_tail[1, 2 * half] * two
-                lower = g_tail[0, 2 * half + 1] * one + g_tail[1, 2 * half + 1] * two
-                back[half, rows : rows + 16, :] = jnp.concatenate([upper, lower], axis=0).astype(back.dtype)
+                tiles = [g_tail[0, part] * one + g_tail[1, part] * two for part in (2 * half, 2 * half + 1)]
+                back[half, rows : rows + 16, :] = jnp.concatenate(tiles, axis=0).astype(back.dtype)
 
 
 def attention(rank, resp_prefix, resp_length, prefix_length, queries, cotangent, own_keys, own_values, packs, g_tail, devices):
@@ -422,7 +424,7 @@
             pltpu.VMEM((rows + length, ATT_DIM), BF16),
             pltpu.VMEM((2, rows, ATT_DIM), F32),
         ],
-        compiler_params=pltpu.CompilerParams(vmem_limit_bytes=32 * 2**20),
+        compiler_params=pltpu.CompilerParams(vmem_limit_bytes=58 * 2**20),
         cost_estimate=pl.CostEstimate(flops=4 * 10**9, bytes_accessed=8 * 2**20, transcendentals=2 * 10**6),
         name="attention_grads",
     )(rank, resp_prefix, resp_length, prefix_length, queries, cotangent, own_keys, own_values, *packs, g_tail)
@@ -482,7 +484,7 @@
         in_specs=[SMEM, SMEM] + [VMEM] * 5,
         out_specs=[VMEM] * 5,
         scratch_shapes=[pltpu.VMEM((width, states), F32), pltpu.VMEM((SPAN, count, length, states), F32)],
-        compiler_params=pltpu.CompilerParams(vmem_limit_bytes=32 * 2**20),
+        compiler_params=pltpu.CompilerParams(vmem_limit_bytes=24 * 2**20),
         cost_estimate=pl.CostEstimate(flops=2 * 10**9, bytes_accessed=8 * 2**20, transcendentals=0),
         name="owner_state",
     )(rank, resp_prefix, state, *carried)
@@ -550,28 +552,43 @@
     carried = carry(after(resp_length, packed), decay, out_cotangent, read)
     pack_two, pack_last, carried = lax.optimization_barrier((pack_two, pack_last, carried))
     carry_two, carry_last = two_and_last(carried, -1)
-    pack_relay = swap(pack_two, 1)
-    packs = [packed, pack_two, pack_relay, pack_last]
-    g_inputs, g_tail, g_conv, g_read = mamba(
+    packs = [packed, pack_two, swap(pack_two, 1), pack_last]
+    g_inputs, g_tail, conv, g_read = mamba(
         rank, resp_prefix, resp_length, skip_gain, token_inputs, packs, conv_weight, write, read, decay, out_cotangent, devices
     )
-    conv = g_conv + swap(g_conv, 1)
+    steps = [by for by in (2, 1, 4, 8) if by < devices]
+    while 2 * max(steps) < devices:
+        steps.append(2 * max(steps))
+    whole = devices & (devices - 1) == 0
+    swaps = iter(steps if whole else [])
+
+    def next_step():
+        by = next(swaps, None)
+        return jnp.zeros_like(conv) if by is None else swap(conv, by)
+
+    moved = next_step()
     g_queries, *backs = attention(
-        rank, resp_prefix, after(resp_length, carry_last), prefix_length, queries, attn_cotangent, own_keys, own_values, packs, g_tail, devices
+        rank, resp_prefix, resp_length, prefix_length, queries, attn_cotangent, own_keys, own_values, packs, g_tail, devices
     )
-    carry_two = after(carry_two, backs[1])
+    *backs, moved, carry_two = lax.optimization_barrier((*backs, moved, carry_two))
+    conv = conv + moved
+    moved = next_step()
     carry_relay = swap(carry_two, 1)
-    conv = after(conv, carry_two)
-    conv = conv + swap(conv, 2)
     backs = [backs[0]] + [shift(backs[by], -by) for by in range(1, SPAN)]
-    g_state, *reads = owner(rank, resp_prefix, state, [carried, carry_two, carry_relay, carry_last], devices)
-    by = 4
-    while by < devices:
-        conv = conv + (swap(conv, by) if devices & (devices - 1) == 0 else 0)
-        by *= 2
-    for by in range(SPAN):
-        g_read = g_read + (reads[by] if by == 0 else shift(reads[by], by).astype(F32))
-    g_prefix_keys, g_prefix_values, g_prefix_tail = sum_back(backs, prefix_tail.shape)
+    g_state, *reads = owner(rank, after(resp_prefix, moved), state, [carried, carry_two, carry_relay, carry_last], devices)
+    conv = conv + moved
+    moved = next_step()
+    reads = [reads[0]] + [shift(reads[by], by) for by in range(1, SPAN)]
+    sums = sum_back(backs, prefix_tail.shape)
+    *sums, moved, r0, r1, r2, r3 = lax.optimization_barrier((*sums, moved, *reads))
+    g_prefix_keys, g_prefix_values, g_prefix_tail = sums
+    conv = conv + moved
+    for by in swaps:
+        conv = conv + swap(conv, by)
+    if not whole:
+        conv = lax.psum(conv, "dp")
+    for part in (r0, r1, r2, r3):
+        g_read = g_read + part.astype(F32)
     token_total = count * length * devices
     grad_conv = conv * (1.0 / math.sqrt(token_total))
     return (

time: 101 us -> 84.1 us (0.83)
  waiting for transfers between devices: 35.1 us -> 23 us
  local copies, waits for them, and re-layouts: 4.57 us -> 0.75 us
  Pallas kernels: 43.3 us -> 41.8 us
  starting transfers between devices: 14.9 us -> 16.3 us
    ppermute x6, waiting for transfers between devices: 15.2 us -> 3.59 us  [swap(): lax.ppermute(value, 'dp', [(i, i ^ by) for i in range(lax.axis_size('dp'))])]
    ppermute x2, waiting for transfers between devices: 9.92 us -> 2.26 us  [two_and_last(): return (shift(value, 2 * sign), lax.ppermute(value, 'dp', pairs))]
    ppermute x8, waiting for transfers between devices: 9.96 us -> 17.1 us  [shift(): lax.ppermute(value, 'dp', [(i, (i + by) % length) for i in range(length)])]
    ppermute x8, starting transfers between devices: 5.2 us -> 9.89 us  [shift(): lax.ppermute(value, 'dp', [(i, (i + by) % length) for i in range(length)])]
    unnamed x42 -> x20, local copies, waits for them, and re-layouts: 4.57 us -> 0.75 us
    ppermute x2, starting transfers between devices: 4.58 us -> 1.92 us  [two_and_last(): return (shift(value, 2 * sign), lax.ppermute(value, 'dp', pairs))]
    pallas_call x1, Pallas kernels: 5.23 us -> 3.94 us  [owner(): pl.pallas_call(functools.partial(owner_kernel, devices), out_shape=[jax.S...]
  transfers between devices with their start and end apart: 16 -> 16, of which waited for: 8 -> 7; matrix products, arithmetic and copies ran while one was open for 1% -> 1% of each run, Pallas kernels for 42% -> 48%
where the time goes in v5:
time: 84.1 us; the launch traced here: 83.9 us
  Pallas kernels  41.8 us (50%)
  waiting for transfers between devices  23 us (27%)
  starting transfers between devices  16.3 us (19%)
  other arithmetic  1.38 us (2%)
    pallas_call x1, Pallas kernels, attention(): pl.pallas_call(functools.partial(attention_kernel, devices), grid=(KV_HEA...  17.6 us
    ppermute x8, waiting for transfers between devices, shift(): lax.ppermute(value, 'dp', [(i, (i + by) % length) for i in range(length)])  17.1 us
    pallas_call x1, Pallas kernels, mamba(): pl.pallas_call(functools.partial(mamba_kernel, devices), grid=(count,), o...  12.5 us
    ppermute x8, starting transfers between devices, shift(): lax.ppermute(value, 'dp', [(i, (i + by) % length) for i in range(length)])  9.89 us
    ppermute x6, starting transfers between devices, swap(): lax.ppermute(value, 'dp', [(i, i ^ by) for i in range(lax.axis_size('dp'))])  4.49 us
    pallas_call x1, Pallas kernels, owner(): pl.pallas_call(functools.partial(owner_kernel, devices), out_shape=[jax.S...  3.94 us
    pallas_call x1, Pallas kernels, carry(): pl.pallas_call(carry_kernel, grid=(count,), out_shape=jax.ShapeDtypeStruc...  3.88 us
    ppermute x6, waiting for transfers between devices, swap(): lax.ppermute(value, 'dp', [(i, i ^ by) for i in range(lax.axis_size('dp'))])  3.59 us
  transfers between devices with their start and end apart: 16, of which 7 were waited for; matrix products, arithmetic and copies ran while one was open for 1% of the time, Pallas kernels for 48%

profile of v5, /device:TPU:0, one launch (start us, length us, event | category | flops | bytes accessed | tf_op | source)
XLA Modules:
  0.0 83.9 jit_solution(8647292671643296023)
XLA Ops:
  0.6 1.7 %pack_prefix.1.pack0 = bf16[2,144,512]{2,1,0:T(8,128)(2,1)} custom-call(bf16[1,128,512]{2,1,0:T(8,128)(2,1)} %keys.1, bf16[1,128,512]{2,1,0:T(8,128)(2,1)} %values.1, bf16[1,3,2048]{2,1,0:T(4,128)(2,1)} %tail.1), custom_call_target="tpu_custom_call" | custom-call | tf_op jit(solution)/shard_map/pack_prefix/pallas_call | solution.py:57
  2.4 0.5 collective-permute-start.1
  2.8 2.5 %collective-permute-start = (bf16[2,144,512]{2,1,0:T(8,128)(2,1)}, bf16[2,144,512]{2,1,0:T(8,128)(2,1)S(1)}, u32[]{:S(2)}, u32[]{:S(2)}) collective-permute-start(bf16[2,144,512]{2,1,0:T(8,128)(2,1)} %pack_prefix.1.pack0), channel_id=1, source_target_pairs={{0,2},{1,3},{2,4},{3,5},{4,6},{5,7},{6,8},{7,9},{8,10},{9,11},{10,... | collective-permute-start | bytes 884744 | tf_op jit(solution)/shard_map/ppermute | solution.py:28
  5.3 3.9 %carry_cotangent.1.car0 = bf16[2,128,2304]{2,1,0:T(8,128)(2,1)} custom-call(s32[2]{0:T(128)} %resp_length.4, f32[2,32,128]{2,1,0:T(8,128)} %bitcast.14, bf16[2,128,2048]{2,1,0:T(8,128)(2,1)} %cotangent.4, bf16[2,128,256]{2,1,0:T(8,128)(2,1)} %bitcast.12), custom_call_target="tpu_custom_call" | custom-call | tf_op jit(solution)/shard_map/carry_cotangent/pallas_call | solution.py:101
  9.2 2.3 %collective-permute-done.1.pack3 = bf16[2,144,512]{2,1,0:T(8,128)(2,1)S(1)} collective-permute-done((bf16[2,144,512]{2,1,0:T(8,128)(2,1)}, bf16[2,144,512]{2,1,0:T(8,128)(2,1)S(1)}, u32[]{:S(2)}, u32[]{:S(2)}) %collective-permute-start.1) | collective-permute-done | bytes 294944 | tf_op jit(solution)/shard_map/ppermute | solution.py:131
  11.5 4.9 %collective-permute-done.pack1 = bf16[2,144,512]{2,1,0:T(8,128)(2,1)S(1)} collective-permute-done((bf16[2,144,512]{2,1,0:T(8,128)(2,1)}, bf16[2,144,512]{2,1,0:T(8,128)(2,1)S(1)}, u32[]{:S(2)}, u32[]{:S(2)}) %collective-permute-start) | collective-permute-done | bytes 294944 | tf_op jit(solution)/shard_map/ppermute | solution.py:28
  16.3 1.5 %collective-permute-start.4 = (bf16[2,128,2304]{2,1,0:T(8,128)(2,1)}, bf16[2,128,2304]{2,1,0:T(8,128)(2,1)S(1)}, u32[]{:S(2)}, u32[]{:S(2)}) collective-permute-start(bf16[2,128,2304]{2,1,0:T(8,128)(2,1)} %carry_cotangent.1.car0), channel_id=1, source_target_pairs={{0,14},{1,15},{2,0},{3,1},{4,2},{5,3},{6,4},{7,5},{8,6},{9,7},{10,... | collective-permute-start | bytes 3538952 | tf_op jit(solution)/shard_map/ppermute | solution.py:28
  17.8 1.2 %collective-permute-start.2 = (bf16[2,144,512]{2,1,0:T(8,128)(2,1)S(1)}, bf16[2,144,512]{2,1,0:T(8,128)(2,1)S(1)}, u32[]{:S(2)}, u32[]{:S(2)}) collective-permute-start(bf16[2,144,512]{2,1,0:T(8,128)(2,1)S(1)} %collective-permute-done.pack1), channel_id=1, source_target_pairs={{0,1},{1,0},{2,3},{3,2},{4,5},{5,4},{6,7},{7,6},{8,9},{9,8},{10,11... | collective-permute-start | bytes 884744 | tf_op jit(solution)/shard_map/ppermute | solution.py:122
  19.1 1.5 %collective-permute-start.11 = (bf16[2,128,2304]{2,1,0:T(8,128)(2,1)}, bf16[2,128,2304]{2,1,0:T(8,128)(2,1)S(1)}, u32[]{:S(2)}, u32[]{:S(2)}) collective-permute-start(bf16[2,128,2304]{2,1,0:T(8,128)(2,1)} %carry_cotangent.1.car0), channel_id=1, source_target_pairs={{0,13},{1,0},{2,15},{3,2},{4,1},{5,4},{6,3},{7,6},{8,5},{9,8},{10,... | collective-permute-start | bytes 3538952 | tf_op jit(solution)/shard_map/ppermute | solution.py:131
  20.5 0.0 collective-permute-done.2.pack2
  20.5 0.0 copy-done.7
  20.5 0.0 copy-done.8
  20.5 0.7 copy-done.9
  21.3 12.5 %mamba_grads.1 = (bf16[2,128,2048]{2,1,0:T(8,128)(2,1)}, f32[2,4,8,512]{3,2,1,0:T(8,128)}, f32[4,2048]{1,0:T(4,128)}, f32[2,128,256]{2,1,0:T(8,128)}) custom-call(s32[1]{0:T(128)} %bitcast.rank_ref, s32[32]{0:T(128)} %resp_prefix.4, s32[2]{0:T(128)} %resp_length.4, f32[32]{0:T(128)} %skip_gain.1, bf16[2,128,2048]{2,1,0:T(8,128)(2,1)} %inputs.1, ...), custom_call_target="tpu_custom_call" | custom-call | flops 2000000000 | bytes 8388608 | tf_op jit(solution)/shard_map/mamba_grads/pallas_call | solution.py:249
  33.8 1.7 %collective-permute-start.3 = (f32[4,2048]{1,0:T(4,128)}, f32[4,2048]{1,0:T(4,128)S(1)}, u32[]{:S(2)}, u32[]{:S(2)}) collective-permute-start(f32[4,2048]{1,0:T(4,128)} %get-tuple-element.54), channel_id=1, source_target_pairs={{0,2},{1,3},{2,0},{3,1},{4,6},{5,7},{6,4},{7,5},{8,10},{9,11},{10,... | collective-permute-start | bytes 98312 | tf_op jit(solution)/shard_map/ppermute | solution.py:122
  35.5 17.6 %attention_grads.1 = (bf16[2,128,4096]{2,1,0:T(8,128)(2,1)}, f32[2,144,512]{2,1,0:T(8,128)}, bf16[2,144,512]{2,1,0:T(8,128)(2,1)}, bf16[2,144,512]{2,1,0:T(8,128)(2,1)}, bf16[2,144,512]{2,1,0:T(8,128)(2,1)}) custom-call(s32[1]{0:T(128)} %bitcast.rank_ref, s32[32]{0:T(128)} %resp_prefix.4, s32[2]{0:T(128)} %resp_length.4, s32[16]{0:T(128)} %prefix_length.1, ...), custom_call_target="tpu_custom_call" | custom-call | flops 4000000000 | bytes 8388608 | tf_op jit(solution)/shard_map/attention_grads/pallas_call | solution.py:390
  53.1 0.0 collective-permute-done.3
  53.1 0.0 collective-permute-done.4.car1
  53.1 0.1 collective-permute-start.10
  53.2 1.4 %collective-permute-start.5 = (bf16[2,144,512]{2,1,0:T(8,128)(2,1)}, bf16[2,144,512]{2,1,0:T(8,128)(2,1)S(1)}, u32[]{:S(2)}, u32[]{:S(2)}) collective-permute-start(bf16[2,144,512]{2,1,0:T(8,128)(2,1)} %get-tuple-element.57), channel_id=1, source_target_pairs={{0,15},{1,0},{2,1},{3,2},{4,3},{5,4},{6,5},{7,6},{8,7},{9,8},{10,9... | collective-permute-start | bytes 884744 | tf_op jit(solution)/shard_map/ppermute | solution.py:28
  54.6 0.0 copy-done.6
  54.6 0.1 collective-permute-start.8
  54.7 1.8 %collective-permute-start.6 = (bf16[2,144,512]{2,1,0:T(8,128)(2,1)}, bf16[2,144,512]{2,1,0:T(8,128)(2,1)S(1)}, u32[]{:S(2)}, u32[]{:S(2)}) collective-permute-start(bf16[2,144,512]{2,1,0:T(8,128)(2,1)} %get-tuple-element.58), channel_id=1, source_target_pairs={{0,14},{1,15},{2,0},{3,1},{4,2},{5,3},{6,4},{7,5},{8,6},{9,7},{10,... | collective-permute-start | bytes 884744 | tf_op jit(solution)/shard_map/ppermute | solution.py:28
  56.5 0.0 collective-permute-done.8
  56.5 1.3 %collective-permute-start.7 = (bf16[2,144,512]{2,1,0:T(8,128)(2,1)}, bf16[2,144,512]{2,1,0:T(8,128)(2,1)}, u32[]{:S(2)}, u32[]{:S(2)}) collective-permute-start(bf16[2,144,512]{2,1,0:T(8,128)(2,1)} %get-tuple-element.59), channel_id=1, source_target_pairs={{0,13},{1,14},{2,15},{3,0},{4,1},{5,2},{6,3},{7,4},{8,5},{9,6},{10... | collective-permute-start | bytes 884744 | tf_op jit(solution)/shard_map/ppermute | solution.py:28
  57.9 0.0 collective-permute-done.11.car3
  57.9 0.0 collective-permute-done.10.car2
  57.9 0.0 copy-done
  57.9 0.0 copy-done.1
  57.9 0.0 copy-done.2
  57.9 3.9 %owner_state.1 = (bf16[2048,256]{1,0:T(8,128)(2,1)}, f32[2,128,256]{2,1,0:T(8,128)S(1)}, bf16[2,128,256]{2,1,0:T(8,128)(2,1)S(1)}, bf16[2,128,256]{2,1,0:T(8,128)(2,1)S(1)}, bf16[2,128,256]{2,1,0:T(8,128)(2,1)S(1)}) custom-call(s32[1]{0:T(128)} %bitcast.rank_ref, s32[32]{0:T(128)S(1)} %copy-done.2, bf16[2048,256]{1,0:T(8,128)(2,1)S(1)} %bitcast.11, ...), custom_call_target="tpu_custom_call" | custom-call | flops 2000000000 | bytes 8388608 | tf_op jit(solution)/shard_map/owner_state/pallas_call | solution.py:480
  61.8 0.0 collective-permute-start.12
  61.8 0.2 collective-permute-start.13
  62.0 1.1 %collective-permute-done.5.back1 = bf16[2,144,512]{2,1,0:T(8,128)(2,1)S(1)} collective-permute-done((bf16[2,144,512]{2,1,0:T(8,128)(2,1)}, bf16[2,144,512]{2,1,0:T(8,128)(2,1)S(1)}, u32[]{:S(2)}, u32[]{:S(2)}) %collective-permute-start.5) | collective-permute-done | bytes 294944 | tf_op jit(solution)/shard_map/ppermute | solution.py:28
  63.1 1.1 %collective-permute-start.14 = (bf16[2,128,256]{2,1,0:T(8,128)(2,1)S(1)}, bf16[2,128,256]{2,1,0:T(8,128)(2,1)S(1)}, u32[]{:S(2)}, u32[]{:S(2)}) collective-permute-start(bf16[2,128,256]{2,1,0:T(8,128)(2,1)S(1)} %get-tuple-element.69), channel_id=1, source_target_pairs={{0,3},{1,4},{2,5},{3,6},{4,7},{5,8},{6,9},{7,10},{8,11},{9,12},{10... | collective-permute-start | bytes 393224 | tf_op jit(solution)/shard_map/ppermute | solution.py:28
  64.3 10.1 %collective-permute-done.6.back2 = bf16[2,144,512]{2,1,0:T(8,128)(2,1)S(1)} collective-permute-done((bf16[2,144,512]{2,1,0:T(8,128)(2,1)}, bf16[2,144,512]{2,1,0:T(8,128)(2,1)S(1)}, u32[]{:S(2)}, u32[]{:S(2)}) %collective-permute-start.6) | collective-permute-done | bytes 294944 | tf_op jit(solution)/shard_map/ppermute | solution.py:28
  74.4 0.0 collective-permute-start.9
  74.4 1.0 %collective-permute-done.7.back3 = bf16[2,144,512]{2,1,0:T(8,128)(2,1)} collective-permute-done((bf16[2,144,512]{2,1,0:T(8,128)(2,1)}, bf16[2,144,512]{2,1,0:T(8,128)(2,1)}, u32[]{:S(2)}, u32[]{:S(2)}) %collective-permute-start.7) | collective-permute-done | bytes 294944 | tf_op jit(solution)/shard_map/ppermute | solution.py:28
  75.4 0.0 copy-done.3
  75.4 2.2 %sum_prefix.1 = (f32[1,128,512]{2,1,0:T(8,128)}, f32[1,128,512]{2,1,0:T(8,128)}, f32[3,1,2048]{2,1,0:T(1,128)}) custom-call(f32[2,144,512]{2,1,0:T(8,128)} %get-tuple-element.56.back0, bf16[2,144,512]{2,1,0:T(8,128)(2,1)} %copy-done.3, bf16[2,144,512]{2,1,0:T(8,128)(2,1)} %copy-done.4, bf16[2,144,512]{2,1,0:T(8,128)(2,1)} %collective-permute-done.7.back3), custom_call_target="tpu_custom_call" | custom-call | tf_op jit(solution)/shard_map/sum_prefix/pallas_call | solution.py:508
  77.6 0.7 collective-permute-done.9
  78.3 0.0 collective-permute-done.12
  78.3 0.0 collective-permute-done.13
  78.3 0.0 collective-permute-done.14
  78.3 1.4 %collective-permute-start.15 = (f32[4,2048]{1,0:T(4,128)S(1)}, f32[4,2048]{1,0:T(4,128)S(1)}, u32[]{:S(2)}, u32[]{:S(2)}) collective-permute-start(f32[4,2048]{1,0:T(4,128)S(1)} %add.30), channel_id=1, source_target_pairs={{0,8},{1,9},{2,10},{3,11},{4,12},{5,13},{6,14},{7,15},{8,0},{9,1},... | collective-permute-start | bytes 98312 | tf_op jit(solution)/shard_map/ppermute | solution.py:122
  79.7 0.7 fusion
  80.4 2.9 %collective-permute-done.15 = f32[4,2048]{1,0:T(4,128)S(1)} collective-permute-done((f32[4,2048]{1,0:T(4,128)S(1)}, f32[4,2048]{1,0:T(4,128)S(1)}, u32[]{:S(2)}, u32[]{:S(2)}) %collective-permute-start.15) | collective-permute-done | bytes 32800 | tf_op jit(solution)/shard_map/ppermute | solution.py:122
  83.3 0.6 add_multiply_fusion
  (15 shorter events, 0.1 us)
Async XLA Ops:
  2.4 9.1 %collective-permute-start.1 = (bf16[2,144,512]{2,1,0:T(8,128)(2,1)}, bf16[2,144,512]{2,1,0:T(8,128)(2,1)S(1)}, u32[]{:S(2)}, u32[]{:S(2)}) collective-permute-start(bf16[2,144,512]{2,1,0:T(8,128)(2,1)} %pack_prefix.1.pack0), channel_id=1, source_target_pairs={{0,1},{1,4},{2,3},{3,6},{4,5},{5,8},{6,7},{7,10},{8,9},{9,12},{10,... | collective-permute-start | bytes 884744 | tf_op jit(solution)/shard_map/ppermute | solution.py:131
  2.8 13.5 %collective-permute-start = (bf16[2,144,512]{2,1,0:T(8,128)(2,1)}, bf16[2,144,512]{2,1,0:T(8,128)(2,1)S(1)}, u32[]{:S(2)}, u32[]{:S(2)}) collective-permute-start(bf16[2,144,512]{2,1,0:T(8,128)(2,1)} %pack_prefix.1.pack0), channel_id=1, source_target_pairs={{0,2},{1,3},{2,4},{3,5},{4,6},{5,7},{6,8},{7,9},{8,10},{9,11},{10,... | collective-permute-start | bytes 884744 | tf_op jit(solution)/shard_map/ppermute | solution.py:28
  11.5 9.1 %copy-start.7 = (bf16[2,144,512]{2,1,0:T(8,128)(2,1)}, bf16[2,144,512]{2,1,0:T(8,128)(2,1)S(1)}, u32[]{:S(2)}) copy-start(bf16[2,144,512]{2,1,0:T(8,128)(2,1)S(1)} %collective-permute-done.1.pack3) | copy-start | bytes 884740
  16.3 4.2 %copy-start.8 = (bf16[2,144,512]{2,1,0:T(8,128)(2,1)}, bf16[2,144,512]{2,1,0:T(8,128)(2,1)S(1)}, u32[]{:S(2)}) copy-start(bf16[2,144,512]{2,1,0:T(8,128)(2,1)S(1)} %collective-permute-done.pack1) | copy-start | bytes 884740
  16.3 36.8 %collective-permute-start.4 = (bf16[2,128,2304]{2,1,0:T(8,128)(2,1)}, bf16[2,128,2304]{2,1,0:T(8,128)(2,1)S(1)}, u32[]{:S(2)}, u32[]{:S(2)}) collective-permute-start(bf16[2,128,2304]{2,1,0:T(8,128)(2,1)} %carry_cotangent.1.car0), channel_id=1, source_target_pairs={{0,14},{1,15},{2,0},{3,1},{4,2},{5,3},{6,4},{7,5},{8,6},{9,7},{10,... | collective-permute-start | bytes 3538952 | tf_op jit(solution)/shard_map/ppermute | solution.py:28
  17.8 2.7 %collective-permute-start.2 = (bf16[2,144,512]{2,1,0:T(8,128)(2,1)S(1)}, bf16[2,144,512]{2,1,0:T(8,128)(2,1)S(1)}, u32[]{:S(2)}, u32[]{:S(2)}) collective-permute-start(bf16[2,144,512]{2,1,0:T(8,128)(2,1)S(1)} %collective-permute-done.pack1), channel_id=1, source_target_pairs={{0,1},{1,0},{2,3},{3,2},{4,5},{5,4},{6,7},{7,6},{8,9},{9,8},{10,11... | collective-permute-start | bytes 884744 | tf_op jit(solution)/shard_map/ppermute | solution.py:122
  19.1 38.8 %collective-permute-start.11 = (bf16[2,128,2304]{2,1,0:T(8,128)(2,1)}, bf16[2,128,2304]{2,1,0:T(8,128)(2,1)S(1)}, u32[]{:S(2)}, u32[]{:S(2)}) collective-permute-start(bf16[2,128,2304]{2,1,0:T(8,128)(2,1)} %carry_cotangent.1.car0), channel_id=1, source_target_pairs={{0,13},{1,0},{2,15},{3,2},{4,1},{5,4},{6,3},{7,6},{8,5},{9,8},{10,... | collective-permute-start | bytes 3538952 | tf_op jit(solution)/shard_map/ppermute | solution.py:131
  20.5 0.7 copy-start.9
  33.8 19.3 %collective-permute-start.3 = (f32[4,2048]{1,0:T(4,128)}, f32[4,2048]{1,0:T(4,128)S(1)}, u32[]{:S(2)}, u32[]{:S(2)}) collective-permute-start(f32[4,2048]{1,0:T(4,128)} %get-tuple-element.54), channel_id=1, source_target_pairs={{0,2},{1,3},{2,0},{3,1},{4,6},{5,7},{6,4},{7,5},{8,10},{9,11},{10,... | collective-permute-start | bytes 98312 | tf_op jit(solution)/shard_map/ppermute | solution.py:122
  35.5 19.1 %copy-start.6 = (f32[4,2048]{1,0:T(4,128)S(1)}, f32[4,2048]{1,0:T(4,128)}, u32[]{:S(2)}) copy-start(f32[4,2048]{1,0:T(4,128)} %get-tuple-element.54) | copy-start | bytes 98308
  35.5 22.4 %copy-start = (bf16[2,128,2304]{2,1,0:T(8,128)(2,1)S(1)}, bf16[2,128,2304]{2,1,0:T(8,128)(2,1)}, u32[]{:S(2)}) copy-start(bf16[2,128,2304]{2,1,0:T(8,128)(2,1)} %carry_cotangent.1.car0) | copy-start | bytes 3538948
  35.5 22.4 %copy-start.1 = (bf16[1,32,64,256]{3,2,1,0:T(8,128)(2,1)S(1)}, bf16[1,32,64,256]{3,2,1,0:T(8,128)(2,1)}, u32[]{:S(2)}) copy-start(bf16[1,32,64,256]{3,2,1,0:T(8,128)(2,1)} %param.31) | copy-start | bytes 3145732
  35.5 22.4 %copy-start.2 = (s32[32]{0:T(128)S(1)}, s32[32]{0:T(128)}, u32[]{:S(2)}) copy-start(s32[32]{0:T(128)} %resp_prefix.4) | copy-start | bytes 388
  53.1 4.7 %collective-permute-start.10 = (bf16[2,128,2304]{2,1,0:T(8,128)(2,1)S(1)}, bf16[2,128,2304]{2,1,0:T(8,128)(2,1)S(1)}, u32[]{:S(2)}, u32[]{:S(2)}) collective-permute-start(bf16[2,128,2304]{2,1,0:T(8,128)(2,1)S(1)} %collective-permute-done.4.car1), channel_id=1, source_target_pairs={{0,1},{1,0},{2,3},{3,2},{4,5},{5,4},{6,7},{7,6},{8,9},{9,8},{10,11... | collective-permute-start | bytes 3538952 | tf_op jit(solution)/shard_map/ppermute | solution.py:122
  53.2 9.9 %collective-permute-start.5 = (bf16[2,144,512]{2,1,0:T(8,128)(2,1)}, bf16[2,144,512]{2,1,0:T(8,128)(2,1)S(1)}, u32[]{:S(2)}, u32[]{:S(2)}) collective-permute-start(bf16[2,144,512]{2,1,0:T(8,128)(2,1)} %get-tuple-element.57), channel_id=1, source_target_pairs={{0,15},{1,0},{2,1},{3,2},{4,3},{5,4},{6,5},{7,6},{8,7},{9,8},{10,9... | collective-permute-start | bytes 884744 | tf_op jit(solution)/shard_map/ppermute | solution.py:28
  54.6 1.9 %collective-permute-start.8 = (f32[4,2048]{1,0:T(4,128)S(1)}, f32[4,2048]{1,0:T(4,128)S(1)}, u32[]{:S(2)}, u32[]{:S(2)}) collective-permute-start(f32[4,2048]{1,0:T(4,128)S(1)} %add.24), channel_id=1, source_target_pairs={{0,1},{1,0},{2,3},{3,2},{4,5},{5,4},{6,7},{7,6},{8,9},{9,8},{10,11... | collective-permute-start | bytes 98312 | tf_op jit(solution)/shard_map/ppermute | solution.py:122
  54.7 19.7 %collective-permute-start.6 = (bf16[2,144,512]{2,1,0:T(8,128)(2,1)}, bf16[2,144,512]{2,1,0:T(8,128)(2,1)S(1)}, u32[]{:S(2)}, u32[]{:S(2)}) collective-permute-start(bf16[2,144,512]{2,1,0:T(8,128)(2,1)} %get-tuple-element.58), channel_id=1, source_target_pairs={{0,14},{1,15},{2,0},{3,1},{4,2},{5,3},{6,4},{7,5},{8,6},{9,7},{10,... | collective-permute-start | bytes 884744 | tf_op jit(solution)/shard_map/ppermute | solution.py:28
  56.5 18.9 %collective-permute-start.7 = (bf16[2,144,512]{2,1,0:T(8,128)(2,1)}, bf16[2,144,512]{2,1,0:T(8,128)(2,1)}, u32[]{:S(2)}, u32[]{:S(2)}) collective-permute-start(bf16[2,144,512]{2,1,0:T(8,128)(2,1)} %get-tuple-element.59), channel_id=1, source_target_pairs={{0,13},{1,14},{2,15},{3,0},{4,1},{5,2},{6,3},{7,4},{8,5},{9,6},{10... | collective-permute-start | bytes 884744 | tf_op jit(solution)/shard_map/ppermute | solution.py:28
  61.8 17.9 %copy-start.5 = (f32[2,128,256]{2,1,0:T(8,128)S(1)}, f32[2,128,256]{2,1,0:T(8,128)}, u32[]{:S(2)}) copy-start(f32[2,128,256]{2,1,0:T(8,128)} %get-tuple-element.48) | copy-start | bytes 786436
  61.8 16.5 %collective-permute-start.12 = (bf16[2,128,256]{2,1,0:T(8,128)(2,1)S(1)}, bf16[2,128,256]{2,1,0:T(8,128)(2,1)S(1)}, u32[]{:S(2)}, u32[]{:S(2)}) collective-permute-start(bf16[2,128,256]{2,1,0:T(8,128)(2,1)S(1)} %get-tuple-element.67), channel_id=1, source_target_pairs={{0,1},{1,2},{2,3},{3,4},{4,5},{5,6},{6,7},{7,8},{8,9},{9,10},{10,1... | collective-permute-start | bytes 393224 | tf_op jit(solution)/shard_map/ppermute | solution.py:28
  61.8 16.5 %collective-permute-start.13 = (bf16[2,128,256]{2,1,0:T(8,128)(2,1)S(1)}, bf16[2,128,256]{2,1,0:T(8,128)(2,1)S(1)}, u32[]{:S(2)}, u32[]{:S(2)}) collective-permute-start(bf16[2,128,256]{2,1,0:T(8,128)(2,1)S(1)} %get-tuple-element.68), channel_id=1, source_target_pairs={{0,2},{1,3},{2,4},{3,5},{4,6},{5,7},{6,8},{7,9},{8,10},{9,11},{10,... | collective-permute-start | bytes 393224 | tf_op jit(solution)/shard_map/ppermute | solution.py:28
  63.1 12.3 %copy-start.3 = (bf16[2,144,512]{2,1,0:T(8,128)(2,1)}, bf16[2,144,512]{2,1,0:T(8,128)(2,1)S(1)}, u32[]{:S(2)}) copy-start(bf16[2,144,512]{2,1,0:T(8,128)(2,1)S(1)} %collective-permute-done.5.back1) | copy-start | bytes 884740
  63.1 15.2 %collective-permute-start.14 = (bf16[2,128,256]{2,1,0:T(8,128)(2,1)S(1)}, bf16[2,128,256]{2,1,0:T(8,128)(2,1)S(1)}, u32[]{:S(2)}, u32[]{:S(2)}) collective-permute-start(bf16[2,128,256]{2,1,0:T(8,128)(2,1)S(1)} %get-tuple-element.69), channel_id=1, source_target_pairs={{0,3},{1,4},{2,5},{3,6},{4,7},{5,8},{6,9},{7,10},{8,11},{9,12},{10... | collective-permute-start | bytes 393224 | tf_op jit(solution)/shard_map/ppermute | solution.py:28
  74.4 1.0 %copy-start.4 = (bf16[2,144,512]{2,1,0:T(8,128)(2,1)}, bf16[2,144,512]{2,1,0:T(8,128)(2,1)S(1)}, u32[]{:S(2)}) copy-start(bf16[2,144,512]{2,1,0:T(8,128)(2,1)S(1)} %collective-permute-done.6.back2) | copy-start | bytes 884740
  74.4 3.9 %collective-permute-start.9 = (f32[4,2048]{1,0:T(4,128)S(1)}, f32[4,2048]{1,0:T(4,128)S(1)}, u32[]{:S(2)}, u32[]{:S(2)}) collective-permute-start(f32[4,2048]{1,0:T(4,128)S(1)} %add.25), channel_id=1, source_target_pairs={{0,4},{1,5},{2,6},{3,7},{4,0},{5,1},{6,2},{7,3},{8,12},{9,13},{10,... | collective-permute-start | bytes 98312 | tf_op jit(solution)/shard_map/ppermute | solution.py:122
  78.3 5.0 %collective-permute-start.15 = (f32[4,2048]{1,0:T(4,128)S(1)}, f32[4,2048]{1,0:T(4,128)S(1)}, u32[]{:S(2)}, u32[]{:S(2)}) collective-permute-start(f32[4,2048]{1,0:T(4,128)S(1)} %add.30), channel_id=1, source_target_pairs={{0,8},{1,9},{2,10},{3,11},{4,12},{5,13},{6,14},{7,15},{8,0},{9,1},... | collective-permute-start | bytes 98312 | tf_op jit(solution)/shard_map/ppermute | solution.py:122

commit v6 on v5

--- a/solution.py
+++ b/solution.py
@@ -15,6 +15,7 @@
 HEAD_DIM = 64
 SPAN = 4
 REPEAT = ATT_HEADS // KV_HEADS
+TOGETHER = 2
 NEG_FILL = -1e30
 F32 = jnp.float32
 BF16 = jnp.bfloat16
@@ -122,12 +123,15 @@
     return lax.ppermute(value, "dp", [(i, i ^ by) for i in range(lax.axis_size("dp"))])
 
 
+def behind(length):
+    return [(i, (i - (1 if i % 2 else 3)) % length) for i in range(length)]
+
+
 def two_and_last(value, sign):
     length = lax.axis_size("dp")
+    pairs = behind(length)
     if sign > 0:
-        pairs = [(i, (i + (3 if i % 2 else 1)) % length) for i in range(length)]
-    else:
-        pairs = [(i, (i - (1 if i % 2 else 3)) % length) for i in range(length)]
+        pairs = [(to, origin) for origin, to in pairs]
     return shift(value, 2 * sign), lax.ppermute(value, "dp", pairs)
 
 
@@ -162,7 +166,6 @@
     g_read,
     padded,
     shifted,
-    inner,
 ):
     resp = pl.program_id(0)
     length = inputs.shape[1]
@@ -189,7 +192,7 @@
     mixing = nt(write[0], read[0])
     live = lax.broadcasted_iota(jnp.int32, (length, 2 * HEAD_DIM), 0) < live_to
     first = lax.broadcasted_iota(jnp.int32, (length, 2 * HEAD_DIM), 1) < HEAD_DIM
-    inner[...] = jnp.zeros_like(inner)
+    inner = jnp.zeros((length, length), F32)
     for pair in range(width // (2 * HEAD_DIM)):
         lo = pair * 2 * HEAD_DIM
         lanes = slice(lo, lo + 2 * HEAD_DIM)
@@ -209,7 +212,7 @@
             lag = decay_rows[head : head + 1, :] - decay_sum[:, head : head + 1]
             decays.append(jnp.exp(jnp.where(causal, lag, NEG_FILL)))
         weights = jnp.concatenate([(d * mixing).astype(BF16) for d in decays], axis=1)
-        inner[...] += decays[0] * d_weights[:, :length] + decays[1] * d_weights[:, length:]
+        inner = inner + decays[0] * d_weights[:, :length] + decays[1] * d_weights[:, length:]
         gain = jnp.where(first[0:1], skip_gain[2 * pair], skip_gain[2 * pair + 1])
         d_act = nn(weights, both) + gain * d_out
         d_mixed = d_act * (gate * (1.0 + mixed * (1.0 - gate)))
@@ -228,16 +231,9 @@
         ]
         rows = jnp.concatenate(rows, axis=0)
 
-
-        @pl.when(resp == 0)
-        def _(rows=rows, lanes=lanes):
-            g_conv[:, lanes] = rows
-
-        @pl.when(resp > 0)
-        def _(rows=rows, lanes=lanes):
-            g_conv[:, lanes] += rows
-
-    g_read[0] = tn(inner[...].astype(BF16), write[0])
+        g_conv[:, lanes] = rows + jnp.where(resp == 0, 0.0, g_conv[:, lanes])
+
+    g_read[0] = tn(inner.astype(BF16), write[0])
 
 
 def mamba(rank, resp_prefix, resp_length, skip_gain, inputs, packs, conv_weight, write, read, log_decay, cotangent, devices):
@@ -280,7 +276,6 @@
         scratch_shapes=[
             pltpu.VMEM((length + 8, width), F32),
             pltpu.VMEM((length + 16, width), F32),
-            pltpu.VMEM((length, length), F32),
         ],
         compiler_params=pltpu.CompilerParams(vmem_limit_bytes=58 * 2**20),
         cost_estimate=pl.CostEstimate(flops=2 * 10**9, bytes_accessed=8 * 2**20, transcendentals=10**6),
@@ -330,18 +325,19 @@
 
     keys[rows : rows + length, :] = own_keys[0]
     values[rows : rows + length, :] = own_values[0]
-    j_index = lax.broadcasted_iota(jnp.int32, (rows + length, 2 * length), 0)
-    t_index = lax.broadcasted_iota(jnp.int32, (rows + length, 2 * length), 1)
-    t_index = jnp.where(t_index >= length, t_index - length, t_index)
+    j_index = lax.broadcasted_iota(jnp.int32, (rows + length, length), 0)
+    t_index = lax.broadcasted_iota(jnp.int32, (rows + length, length), 1)
     bound = jnp.where(j_index < rows, pref_len, t_index + rows + 1)
     bias = jnp.where(j_index < bound, 0.0, NEG_FILL)
+    bias = jnp.concatenate([bias] * TOGETHER, axis=1)
     live = lax.broadcasted_iota(jnp.int32, (length, ATT_DIM), 0) < live_to
     all_keys = keys[...]
     all_values = values[...]
+    keys_across = all_keys.T
     g_keys = jnp.zeros((rows, ATT_DIM), F32)
     g_values = jnp.zeros((rows, ATT_DIM), F32)
-    for duo in range(REPEAT // 2):
-        spans = [slice((2 * duo + i) * ATT_DIM, (2 * duo + i + 1) * ATT_DIM) for i in range(2)]
+    for at in range(0, REPEAT, TOGETHER):
+        spans = [slice(head * ATT_DIM, (head + 1) * ATT_DIM) for head in range(at, at + TOGETHER)]
         query = jnp.concatenate([queries[0, :, span] for span in spans], axis=0)
         d_out = jnp.concatenate(
             [jnp.where(live, cotangent[0, :, span].astype(F32), 0.0).astype(BF16) for span in spans], axis=0
@@ -354,9 +350,9 @@
         d_probs = nt(all_values, d_out)
         delta = jnp.sum(probs * d_probs, axis=0, keepdims=True)
         d_scores = (probs * (d_probs - delta)).astype(BF16)
-        g_query = tn(d_scores, all_keys) * scale
+        g_query = (nn(keys_across, d_scores) * scale).astype(BF16).T
         for i, span in enumerate(spans):
-            g_queries[0, :, span] = g_query[i * length : (i + 1) * length].astype(BF16)
+            g_queries[0, :, span] = g_query[i * length : (i + 1) * length]
         g_keys = g_keys + nn(d_scores[0:rows], query)
         g_values = g_values + nn(probs_low[0:rows], d_out)
 
@@ -370,7 +366,9 @@
     @pl.when(resp == 1)
     def _():
         before = distance_to(rank, resp_prefix[2 * rank], devices)
-        for step, back in enumerate((back0, back1, back2, back3)):
+        even = rank % 2 == 0
+        steps = (0, 2, jnp.where(even, 3, 1), jnp.where(even, 1, 3))
+        for step, back in zip(steps, (back0, back1, back2, back3)):
             one = jnp.where(before == step, 1.0, 0.0)
             two = jnp.where(gap == step, 1.0, 0.0)
             back[0, 0:rows, :] = (kept[0] * one + g_keys * two).astype(back.dtype)
@@ -490,11 +488,11 @@
     )(rank, resp_prefix, state, *carried)
 
 
-def sum_kernel(back0, back1, back2, back3, g_keys, g_values, g_tail):
+def sum_kernel(back0, back1, back2, g_keys, g_values, g_tail):
     rows = g_keys.shape[1]
     for half, out in enumerate((g_keys, g_values)):
         total = back0[half]
-        for back in (back1, back2, back3):
+        for back in (back1, back2):
             total = total + back[half].astype(F32)
         out[0] = total[0:rows]
         for part in range(2):
@@ -512,7 +510,7 @@
             jax.ShapeDtypeStruct((1, rows, width), F32),
             jax.ShapeDtypeStruct((tail_shape[1], 1, tail_shape[2]), F32),
         ],
-        in_specs=[VMEM] * 4,
+        in_specs=[VMEM] * 3,
         out_specs=[VMEM] * 3,
         name="sum_prefix",
     )(*backs)
@@ -572,17 +570,25 @@
     )
     *backs, moved, carry_two = lax.optimization_barrier((*backs, moved, carry_two))
     conv = conv + moved
+    own, two, last, other = backs
+    other = swap(other, 1)
+    last = lax.ppermute(last, "dp", behind(devices))
+    carry_relay = swap(carry_two, 1)
     moved = next_step()
-    carry_relay = swap(carry_two, 1)
-    backs = [backs[0]] + [shift(backs[by], -by) for by in range(1, SPAN)]
-    g_state, *reads = owner(rank, after(resp_prefix, moved), state, [carried, carry_two, carry_relay, carry_last], devices)
+    two = (two.astype(F32) + other.astype(F32)).astype(BF16)
+    chosen = after(resp_prefix, two, moved)
+    two = shift(two, -2)
+    g_state, *reads = owner(rank, chosen, state, [carried, carry_two, carry_relay, carry_last], devices)
+    reads = [reads[0]] + [shift(reads[by], by) for by in range(1, SPAN)]
+    conv = after(conv + moved, *reads[:1])
+    moved = next_step()
+    own, moved = lax.optimization_barrier((own, moved))
     conv = conv + moved
     moved = next_step()
-    reads = [reads[0]] + [shift(reads[by], by) for by in range(1, SPAN)]
-    sums = sum_back(backs, prefix_tail.shape)
+    sums = sum_back([own, two, last], prefix_tail.shape)
     *sums, moved, r0, r1, r2, r3 = lax.optimization_barrier((*sums, moved, *reads))
+    conv = conv + moved
     g_prefix_keys, g_prefix_values, g_prefix_tail = sums
-    conv = conv + moved
     for by in swaps:
         conv = conv + swap(conv, by)
     if not whole:

time: 84.1 us -> 76.5 us (0.910)
  Pallas kernels: 41.8 us -> 37 us
  starting transfers between devices: 16.3 us -> 13.7 us
  waiting for transfers between devices: 23 us -> 21.6 us
  other arithmetic: 1.38 us -> 2.42 us
    ppermute x8 -> x6, waiting for transfers between devices: 17.1 us -> 4.89 us  [shift(): lax.ppermute(value, 'dp', [(i, (i + by) % length) for i in range(length)])]
    ppermute x6 -> x7, waiting for transfers between devices: 3.59 us -> 11.4 us  [swap(): lax.ppermute(value, 'dp', [(i, i ^ by) for i in range(lax.axis_size('dp'))])]
    ppermute x8 -> x6, starting transfers between devices: 9.89 us -> 5.23 us  [shift(): lax.ppermute(value, 'dp', [(i, (i + by) % length) for i in range(length)])]
    ppermute x2, waiting for transfers between devices: 2.26 us -> 5.29 us  [two_and_last(): return (shift(value, 2 * sign), lax.ppermute(value, 'dp', pairs))]
    pallas_call x1, Pallas kernels: 12.5 us -> 9.58 us  [mamba(): pl.pallas_call(functools.partial(mamba_kernel, devices), grid=(count,), o...]
    ppermute x0 -> x1, starting transfers between devices: none -> 1.65 us  [on_device(): last = lax.ppermute(last, 'dp', behind(devices))]
    convert_element_type x0 -> x1, other arithmetic: none -> 1.04 us  [on_device(): two = (two.astype(F32) + other.astype(F32)).astype(BF16)]
    pallas_call x1, Pallas kernels: 17.6 us -> 16.7 us  [attention(): pl.pallas_call(functools.partial(attention_kernel, devices), grid=(KV_HEA...]
  transfers between devices with their start and end apart: 16 -> 16, of which waited for: 7 -> 6; matrix products, arithmetic and copies ran while one was open for 1% -> 1% of each run, Pallas kernels for 48% -> 46%
where the time goes in v6:
time: 76.5 us; the launch traced here: 76.2 us
  Pallas kernels  37 us (48%)
  waiting for transfers between devices  21.6 us (28%)
  starting transfers between devices  13.7 us (18%)
  other arithmetic  2.42 us (3%)
    pallas_call x1, Pallas kernels, attention(): pl.pallas_call(functools.partial(attention_kernel, devices), grid=(KV_HEA...  16.7 us
    ppermute x7, waiting for transfers between devices, swap(): lax.ppermute(value, 'dp', [(i, i ^ by) for i in range(lax.axis_size('dp'))])  11.4 us
    pallas_call x1, Pallas kernels, mamba(): pl.pallas_call(functools.partial(mamba_kernel, devices), grid=(count,), o...  9.58 us
    ppermute x2, waiting for transfers between devices, two_and_last(): return (shift(value, 2 * sign), lax.ppermute(value, 'dp', pairs))  5.29 us
    ppermute x6, starting transfers between devices, shift(): lax.ppermute(value, 'dp', [(i, (i + by) % length) for i in range(length)])  5.23 us
    ppermute x6, waiting for transfers between devices, shift(): lax.ppermute(value, 'dp', [(i, (i + by) % length) for i in range(length)])  4.89 us
    ppermute x7, starting transfers between devices, swap(): lax.ppermute(value, 'dp', [(i, i ^ by) for i in range(lax.axis_size('dp'))])  4.86 us
    pallas_call x1, Pallas kernels, carry(): pl.pallas_call(carry_kernel, grid=(count,), out_shape=jax.ShapeDtypeStruc...  3.88 us
  transfers between devices with their start and end apart: 16, of which 6 were waited for; matrix products, arithmetic and copies ran while one was open for 1% of the time, Pallas kernels for 46%

profile of v6, /device:TPU:0, one launch (start us, length us, event | category | flops | bytes accessed | tf_op | source)
XLA Modules:
  0.0 76.2 jit_solution(14760945353647268355)
XLA Ops:
  0.6 1.7 %pack_prefix.1.pack0 = bf16[2,144,512]{2,1,0:T(8,128)(2,1)} custom-call(bf16[1,128,512]{2,1,0:T(8,128)(2,1)} %keys.1, bf16[1,128,512]{2,1,0:T(8,128)(2,1)} %values.1, bf16[1,3,2048]{2,1,0:T(4,128)(2,1)} %tail.1), custom_call_target="tpu_custom_call" | custom-call | tf_op jit(solution)/shard_map/pack_prefix/pallas_call | solution.py:58
  2.4 0.5 collective-permute-start.1
  2.8 2.5 %collective-permute-start = (bf16[2,144,512]{2,1,0:T(8,128)(2,1)}, bf16[2,144,512]{2,1,0:T(8,128)(2,1)S(1)}, u32[]{:S(2)}, u32[]{:S(2)}) collective-permute-start(bf16[2,144,512]{2,1,0:T(8,128)(2,1)} %pack_prefix.1.pack0), channel_id=1, source_target_pairs={{0,2},{1,3},{2,4},{3,5},{4,6},{5,7},{6,8},{7,9},{8,10},{9,11},{10,... | collective-permute-start | bytes 884744 | tf_op jit(solution)/shard_map/ppermute | solution.py:29
  5.3 3.9 %carry_cotangent.1.car0 = bf16[2,128,2304]{2,1,0:T(8,128)(2,1)} custom-call(s32[2]{0:T(128)} %resp_length.4, f32[2,32,128]{2,1,0:T(8,128)} %bitcast.14, bf16[2,128,2048]{2,1,0:T(8,128)(2,1)} %cotangent.4, bf16[2,128,256]{2,1,0:T(8,128)(2,1)} %bitcast.12), custom_call_target="tpu_custom_call" | custom-call | tf_op jit(solution)/shard_map/carry_cotangent/pallas_call | solution.py:102
  9.2 2.2 %collective-permute-done.1.pack3 = bf16[2,144,512]{2,1,0:T(8,128)(2,1)S(1)} collective-permute-done((bf16[2,144,512]{2,1,0:T(8,128)(2,1)}, bf16[2,144,512]{2,1,0:T(8,128)(2,1)S(1)}, u32[]{:S(2)}, u32[]{:S(2)}) %collective-permute-start.1) | collective-permute-done | bytes 294944 | tf_op jit(solution)/shard_map/ppermute | solution.py:135
  11.5 4.9 %collective-permute-done.pack1 = bf16[2,144,512]{2,1,0:T(8,128)(2,1)S(1)} collective-permute-done((bf16[2,144,512]{2,1,0:T(8,128)(2,1)}, bf16[2,144,512]{2,1,0:T(8,128)(2,1)S(1)}, u32[]{:S(2)}, u32[]{:S(2)}) %collective-permute-start) | collective-permute-done | bytes 294944 | tf_op jit(solution)/shard_map/ppermute | solution.py:29
  16.3 1.5 %collective-permute-start.4 = (bf16[2,128,2304]{2,1,0:T(8,128)(2,1)}, bf16[2,128,2304]{2,1,0:T(8,128)(2,1)S(1)}, u32[]{:S(2)}, u32[]{:S(2)}) collective-permute-start(bf16[2,128,2304]{2,1,0:T(8,128)(2,1)} %carry_cotangent.1.car0), channel_id=1, source_target_pairs={{0,14},{1,15},{2,0},{3,1},{4,2},{5,3},{6,4},{7,5},{8,6},{9,7},{10,... | collective-permute-start | bytes 3538952 | tf_op jit(solution)/shard_map/ppermute | solution.py:29
  17.8 1.2 %collective-permute-start.2 = (bf16[2,144,512]{2,1,0:T(8,128)(2,1)S(1)}, bf16[2,144,512]{2,1,0:T(8,128)(2,1)S(1)}, u32[]{:S(2)}, u32[]{:S(2)}) collective-permute-start(bf16[2,144,512]{2,1,0:T(8,128)(2,1)S(1)} %collective-permute-done.pack1), channel_id=1, source_target_pairs={{0,1},{1,0},{2,3},{3,2},{4,5},{5,4},{6,7},{7,6},{8,9},{9,8},{10,11... | collective-permute-start | bytes 884744 | tf_op jit(solution)/shard_map/ppermute | solution.py:123
  19.1 1.5 %collective-permute-start.8 = (bf16[2,128,2304]{2,1,0:T(8,128)(2,1)}, bf16[2,128,2304]{2,1,0:T(8,128)(2,1)S(1)}, u32[]{:S(2)}, u32[]{:S(2)}) collective-permute-start(bf16[2,128,2304]{2,1,0:T(8,128)(2,1)} %carry_cotangent.1.car0), channel_id=1, source_target_pairs={{0,13},{1,0},{2,15},{3,2},{4,1},{5,4},{6,3},{7,6},{8,5},{9,8},{10,... | collective-permute-start | bytes 3538952 | tf_op jit(solution)/shard_map/ppermute | solution.py:135
  20.5 0.0 collective-permute-done.2.pack2
  20.5 0.0 copy-done.6
  20.5 0.0 copy-done.7
  20.5 0.7 copy-done.8
  21.3 9.6 %mamba_grads.1 = (bf16[2,128,2048]{2,1,0:T(8,128)(2,1)}, f32[2,4,8,512]{3,2,1,0:T(8,128)}, f32[4,2048]{1,0:T(4,128)}, f32[2,128,256]{2,1,0:T(8,128)}) custom-call(s32[1]{0:T(128)} %bitcast.rank_ref, s32[32]{0:T(128)} %resp_prefix.4, s32[2]{0:T(128)} %resp_length.4, f32[32]{0:T(128)} %skip_gain.1, bf16[2,128,2048]{2,1,0:T(8,128)(2,1)} %inputs.1, ...), custom_call_target="tpu_custom_call" | custom-call | flops 2000000000 | bytes 8388608 | tf_op jit(solution)/shard_map/mamba_grads/pallas_call | solution.py:245
  30.8 1.7 %collective-permute-start.3 = (f32[4,2048]{1,0:T(4,128)}, f32[4,2048]{1,0:T(4,128)S(1)}, u32[]{:S(2)}, u32[]{:S(2)}) collective-permute-start(f32[4,2048]{1,0:T(4,128)} %get-tuple-element.57), channel_id=1, source_target_pairs={{0,2},{1,3},{2,0},{3,1},{4,6},{5,7},{6,4},{7,5},{8,10},{9,11},{10,... | collective-permute-start | bytes 98312 | tf_op jit(solution)/shard_map/ppermute | solution.py:123
  32.6 16.7 %attention_grads.1 = (bf16[2,128,4096]{2,1,0:T(8,128)(2,1)}, f32[2,144,512]{2,1,0:T(8,128)}, bf16[2,144,512]{2,1,0:T(8,128)(2,1)}, bf16[2,144,512]{2,1,0:T(8,128)(2,1)}, bf16[2,144,512]{2,1,0:T(8,128)(2,1)}) custom-call(s32[1]{0:T(128)} %bitcast.rank_ref, s32[32]{0:T(128)} %resp_prefix.4, s32[2]{0:T(128)} %resp_length.4, s32[16]{0:T(128)} %prefix_length.1, ...), custom_call_target="tpu_custom_call" | custom-call | flops 4000000000 | bytes 8388608 | tf_op jit(solution)/shard_map/attention_grads/pallas_call | solution.py:388
  49.3 0.0 collective-permute-done.3
  49.3 0.0 collective-permute-done.4.car1
  49.3 0.1 collective-permute-start.7
  49.4 0.5 collective-permute-start.6
  49.9 0.0 copy-done.5
  49.9 0.1 collective-permute-start.5
  50.0 1.6 %collective-permute-start.11 = (bf16[2,144,512]{2,1,0:T(8,128)(2,1)}, bf16[2,144,512]{2,1,0:T(8,128)(2,1)S(1)}, u32[]{:S(2)}, u32[]{:S(2)}) collective-permute-start(bf16[2,144,512]{2,1,0:T(8,128)(2,1)} %get-tuple-element.68), channel_id=1, source_target_pairs={{0,13},{1,0},{2,15},{3,2},{4,1},{5,4},{6,3},{7,6},{8,5},{9,8},{10,... | collective-permute-start | bytes 884744 | tf_op jit(solution)/shard_map/ppermute | solution.py:575
  51.7 1.4 %collective-permute-done.5 = f32[4,2048]{1,0:T(4,128)S(1)} collective-permute-done((f32[4,2048]{1,0:T(4,128)S(1)}, f32[4,2048]{1,0:T(4,128)S(1)}, u32[]{:S(2)}, u32[]{:S(2)}) %collective-permute-start.5) | collective-permute-done | bytes 32800 | tf_op jit(solution)/shard_map/ppermute | solution.py:123
  53.1 0.0 collective-permute-done.6
  53.1 1.0 %add_convert_fusion = bf16[2,144,512]{2,1,0:T(8,128)(2,1)S(1)} fusion(bf16[2,144,512]{2,1,0:T(8,128)(2,1)S(1)} %collective-permute-done.6, bf16[2,144,512]{2,1,0:T(8,128)(2,1)} %get-tuple-element.61), kind=kLoop, calls=%fused_computation | loop fusion | flops 589824 | bytes 884736 | tf_op jit(solution)/shard_map/convert_element_type | solution.py:578
  54.2 1.2 %collective-permute-start.10 = (bf16[2,144,512]{2,1,0:T(8,128)(2,1)S(1)}, bf16[2,144,512]{2,1,0:T(8,128)(2,1)}, u32[]{:S(2)}, u32[]{:S(2)}) collective-permute-start(bf16[2,144,512]{2,1,0:T(8,128)(2,1)S(1)} %add_convert_fusion), channel_id=1, source_target_pairs={{0,14},{1,15},{2,0},{3,1},{4,2},{5,3},{6,4},{7,5},{8,6},{9,7},{10,... | collective-permute-start | bytes 884744 | tf_op jit(solution)/shard_map/ppermute | solution.py:29
  55.4 3.0 %collective-permute-done.8.car3 = bf16[2,128,2304]{2,1,0:T(8,128)(2,1)S(1)} collective-permute-done((bf16[2,128,2304]{2,1,0:T(8,128)(2,1)}, bf16[2,128,2304]{2,1,0:T(8,128)(2,1)S(1)}, u32[]{:S(2)}, u32[]{:S(2)}) %collective-permute-start.8) | collective-permute-done | bytes 1179680 | tf_op jit(solution)/shard_map/ppermute | solution.py:135
  58.5 0.0 collective-permute-done.7.car2
  58.5 0.0 copy-done
  58.5 0.0 copy-done.1
  58.5 3.1 %owner_state.1 = (bf16[2048,256]{1,0:T(8,128)(2,1)}, f32[2,128,256]{2,1,0:T(8,128)S(1)}, bf16[2,128,256]{2,1,0:T(8,128)(2,1)S(1)}, bf16[2,128,256]{2,1,0:T(8,128)(2,1)S(1)}, bf16[2,128,256]{2,1,0:T(8,128)(2,1)S(1)}) custom-call(s32[1]{0:T(128)} %bitcast.rank_ref, s32[32]{0:T(128)S(1)} %copy-done.2, bf16[2048,256]{1,0:T(8,128)(2,1)S(1)} %bitcast.11, ...), custom_call_target="tpu_custom_call" | custom-call | flops 2000000000 | bytes 8388608 | tf_op jit(solution)/shard_map/owner_state/pallas_call | solution.py:478
  61.6 0.1 collective-permute-start.9
  61.7 0.0 collective-permute-start.13
  61.7 0.0 collective-permute-start.14
  61.7 6.1 %collective-permute-done.9 = f32[4,2048]{1,0:T(4,128)S(1)} collective-permute-done((f32[4,2048]{1,0:T(4,128)S(1)}, f32[4,2048]{1,0:T(4,128)S(1)}, u32[]{:S(2)}, u32[]{:S(2)}) %collective-permute-start.9) | collective-permute-done | bytes 32800 | tf_op jit(solution)/shard_map/ppermute | solution.py:123
  67.8 0.0 collective-permute-start.15
  67.8 0.0 collective-permute-done.11.back2
  67.8 0.0 copy-start.3
  67.9 1.0 %collective-permute-start.12 = (f32[4,2048]{1,0:T(4,128)S(1)}, f32[4,2048]{1,0:T(4,128)S(1)}, u32[]{:S(2)}, u32[]{:S(2)}) collective-permute-start(f32[4,2048]{1,0:T(4,128)S(1)} %add.30), channel_id=1, source_target_pairs={{0,8},{1,9},{2,10},{3,11},{4,12},{5,13},{6,14},{7,15},{8,0},{9,1},... | collective-permute-start | bytes 98312 | tf_op jit(solution)/shard_map/ppermute | solution.py:123
  68.9 0.0 collective-permute-done.10.back1
  68.9 2.1 %sum_prefix.1 = (f32[1,128,512]{2,1,0:T(8,128)}, f32[1,128,512]{2,1,0:T(8,128)}, f32[3,1,2048]{2,1,0:T(1,128)}) custom-call(f32[2,144,512]{2,1,0:T(8,128)} %get-tuple-element.67.back0, bf16[2,144,512]{2,1,0:T(8,128)(2,1)} %collective-permute-done.10.back1, bf16[2,144,512]{2,1,0:T(8,128)(2,1)} %copy-done.3), custom_call_target="tpu_custom_call" | custom-call | tf_op jit(solution)/shard_map/sum_prefix/pallas_call | solution.py:506
  70.9 3.9 %collective-permute-done.12 = f32[4,2048]{1,0:T(4,128)S(1)} collective-permute-done((f32[4,2048]{1,0:T(4,128)S(1)}, f32[4,2048]{1,0:T(4,128)S(1)}, u32[]{:S(2)}, u32[]{:S(2)}) %collective-permute-start.12) | collective-permute-done | bytes 32800 | tf_op jit(solution)/shard_map/ppermute | solution.py:123
  74.9 0.0 collective-permute-done.13
  74.9 0.0 collective-permute-done.14
  74.9 0.0 collective-permute-done.15
  74.9 0.6 add_multiply_fusion
  75.5 0.7 fusion
  (14 shorter events, 0.1 us)
Async XLA Ops:
  2.4 9.1 %collective-permute-start.1 = (bf16[2,144,512]{2,1,0:T(8,128)(2,1)}, bf16[2,144,512]{2,1,0:T(8,128)(2,1)S(1)}, u32[]{:S(2)}, u32[]{:S(2)}) collective-permute-start(bf16[2,144,512]{2,1,0:T(8,128)(2,1)} %pack_prefix.1.pack0), channel_id=1, source_target_pairs={{13,0},{0,1},{15,2},{2,3},{1,4},{4,5},{3,6},{6,7},{5,8},{8,9},{7,1... | collective-permute-start | bytes 884744 | tf_op jit(solution)/shard_map/ppermute | solution.py:135
  2.8 13.5 %collective-permute-start = (bf16[2,144,512]{2,1,0:T(8,128)(2,1)}, bf16[2,144,512]{2,1,0:T(8,128)(2,1)S(1)}, u32[]{:S(2)}, u32[]{:S(2)}) collective-permute-start(bf16[2,144,512]{2,1,0:T(8,128)(2,1)} %pack_prefix.1.pack0), channel_id=1, source_target_pairs={{0,2},{1,3},{2,4},{3,5},{4,6},{5,7},{6,8},{7,9},{8,10},{9,11},{10,... | collective-permute-start | bytes 884744 | tf_op jit(solution)/shard_map/ppermute | solution.py:29
  11.5 9.1 %copy-start.6 = (bf16[2,144,512]{2,1,0:T(8,128)(2,1)}, bf16[2,144,512]{2,1,0:T(8,128)(2,1)S(1)}, u32[]{:S(2)}) copy-start(bf16[2,144,512]{2,1,0:T(8,128)(2,1)S(1)} %collective-permute-done.1.pack3) | copy-start | bytes 884740
  16.3 4.2 %copy-start.7 = (bf16[2,144,512]{2,1,0:T(8,128)(2,1)}, bf16[2,144,512]{2,1,0:T(8,128)(2,1)S(1)}, u32[]{:S(2)}) copy-start(bf16[2,144,512]{2,1,0:T(8,128)(2,1)S(1)} %collective-permute-done.pack1) | copy-start | bytes 884740
  16.3 33.0 %collective-permute-start.4 = (bf16[2,128,2304]{2,1,0:T(8,128)(2,1)}, bf16[2,128,2304]{2,1,0:T(8,128)(2,1)S(1)}, u32[]{:S(2)}, u32[]{:S(2)}) collective-permute-start(bf16[2,128,2304]{2,1,0:T(8,128)(2,1)} %carry_cotangent.1.car0), channel_id=1, source_target_pairs={{0,14},{1,15},{2,0},{3,1},{4,2},{5,3},{6,4},{7,5},{8,6},{9,7},{10,... | collective-permute-start | bytes 3538952 | tf_op jit(solution)/shard_map/ppermute | solution.py:29
  17.8 2.7 %collective-permute-start.2 = (bf16[2,144,512]{2,1,0:T(8,128)(2,1)S(1)}, bf16[2,144,512]{2,1,0:T(8,128)(2,1)S(1)}, u32[]{:S(2)}, u32[]{:S(2)}) collective-permute-start(bf16[2,144,512]{2,1,0:T(8,128)(2,1)S(1)} %collective-permute-done.pack1), channel_id=1, source_target_pairs={{0,1},{1,0},{2,3},{3,2},{4,5},{5,4},{6,7},{7,6},{8,9},{9,8},{10,11... | collective-permute-start | bytes 884744 | tf_op jit(solution)/shard_map/ppermute | solution.py:123
  19.1 39.4 %collective-permute-start.8 = (bf16[2,128,2304]{2,1,0:T(8,128)(2,1)}, bf16[2,128,2304]{2,1,0:T(8,128)(2,1)S(1)}, u32[]{:S(2)}, u32[]{:S(2)}) collective-permute-start(bf16[2,128,2304]{2,1,0:T(8,128)(2,1)} %carry_cotangent.1.car0), channel_id=1, source_target_pairs={{0,13},{1,0},{2,15},{3,2},{4,1},{5,4},{6,3},{7,6},{8,5},{9,8},{10,... | collective-permute-start | bytes 3538952 | tf_op jit(solution)/shard_map/ppermute | solution.py:135
  20.5 0.7 copy-start.8
  30.8 18.5 %collective-permute-start.3 = (f32[4,2048]{1,0:T(4,128)}, f32[4,2048]{1,0:T(4,128)S(1)}, u32[]{:S(2)}, u32[]{:S(2)}) collective-permute-start(f32[4,2048]{1,0:T(4,128)} %get-tuple-element.57), channel_id=1, source_target_pairs={{0,2},{1,3},{2,0},{3,1},{4,6},{5,7},{6,4},{7,5},{8,10},{9,11},{10,... | collective-permute-start | bytes 98312 | tf_op jit(solution)/shard_map/ppermute | solution.py:123
  32.6 17.3 %copy-start.5 = (f32[4,2048]{1,0:T(4,128)S(1)}, f32[4,2048]{1,0:T(4,128)}, u32[]{:S(2)}) copy-start(f32[4,2048]{1,0:T(4,128)} %get-tuple-element.57) | copy-start | bytes 98308
  32.6 25.9 %copy-start = (bf16[2,128,2304]{2,1,0:T(8,128)(2,1)S(1)}, bf16[2,128,2304]{2,1,0:T(8,128)(2,1)}, u32[]{:S(2)}) copy-start(bf16[2,128,2304]{2,1,0:T(8,128)(2,1)} %carry_cotangent.1.car0) | copy-start | bytes 3538948
  32.6 25.9 %copy-start.1 = (bf16[1,32,64,256]{3,2,1,0:T(8,128)(2,1)S(1)}, bf16[1,32,64,256]{3,2,1,0:T(8,128)(2,1)}, u32[]{:S(2)}) copy-start(bf16[1,32,64,256]{3,2,1,0:T(8,128)(2,1)} %param.31) | copy-start | bytes 3145732
  32.6 25.9 %copy-start.2 = (s32[32]{0:T(128)S(1)}, s32[32]{0:T(128)}, u32[]{:S(2)}) copy-start(s32[32]{0:T(128)} %resp_prefix.4) | copy-start | bytes 388
  49.3 9.1 %collective-permute-start.7 = (bf16[2,128,2304]{2,1,0:T(8,128)(2,1)S(1)}, bf16[2,128,2304]{2,1,0:T(8,128)(2,1)S(1)}, u32[]{:S(2)}, u32[]{:S(2)}) collective-permute-start(bf16[2,128,2304]{2,1,0:T(8,128)(2,1)S(1)} %collective-permute-done.4.car1), channel_id=1, source_target_pairs={{0,1},{1,0},{2,3},{3,2},{4,5},{5,4},{6,7},{7,6},{8,9},{9,8},{10,11... | collective-permute-start | bytes 3538952 | tf_op jit(solution)/shard_map/ppermute | solution.py:123
  49.4 3.7 %collective-permute-start.6 = (bf16[2,144,512]{2,1,0:T(8,128)(2,1)}, bf16[2,144,512]{2,1,0:T(8,128)(2,1)S(1)}, u32[]{:S(2)}, u32[]{:S(2)}) collective-permute-start(bf16[2,144,512]{2,1,0:T(8,128)(2,1)} %get-tuple-element.62), channel_id=1, source_target_pairs={{0,1},{1,0},{2,3},{3,2},{4,5},{5,4},{6,7},{7,6},{8,9},{9,8},{10,11... | collective-permute-start | bytes 884744 | tf_op jit(solution)/shard_map/ppermute | solution.py:123
  49.9 3.2 %collective-permute-start.5 = (f32[4,2048]{1,0:T(4,128)S(1)}, f32[4,2048]{1,0:T(4,128)S(1)}, u32[]{:S(2)}, u32[]{:S(2)}) collective-permute-start(f32[4,2048]{1,0:T(4,128)S(1)} %add.27), channel_id=1, source_target_pairs={{0,1},{1,0},{2,3},{3,2},{4,5},{5,4},{6,7},{7,6},{8,9},{9,8},{10,11... | collective-permute-start | bytes 98312 | tf_op jit(solution)/shard_map/ppermute | solution.py:123
  50.0 17.8 %collective-permute-start.11 = (bf16[2,144,512]{2,1,0:T(8,128)(2,1)}, bf16[2,144,512]{2,1,0:T(8,128)(2,1)S(1)}, u32[]{:S(2)}, u32[]{:S(2)}) collective-permute-start(bf16[2,144,512]{2,1,0:T(8,128)(2,1)} %get-tuple-element.68), channel_id=1, source_target_pairs={{0,13},{1,0},{2,15},{3,2},{4,1},{5,4},{6,3},{7,6},{8,5},{9,8},{10,... | collective-permute-start | bytes 884744 | tf_op jit(solution)/shard_map/ppermute | solution.py:575
  54.2 14.7 %collective-permute-start.10 = (bf16[2,144,512]{2,1,0:T(8,128)(2,1)S(1)}, bf16[2,144,512]{2,1,0:T(8,128)(2,1)}, u32[]{:S(2)}, u32[]{:S(2)}) collective-permute-start(bf16[2,144,512]{2,1,0:T(8,128)(2,1)S(1)} %add_convert_fusion), channel_id=1, source_target_pairs={{0,14},{1,15},{2,0},{3,1},{4,2},{5,3},{6,4},{7,5},{8,6},{9,7},{10,... | collective-permute-start | bytes 884744 | tf_op jit(solution)/shard_map/ppermute | solution.py:29
  61.6 13.9 %copy-start.4 = (f32[2,128,256]{2,1,0:T(8,128)S(1)}, f32[2,128,256]{2,1,0:T(8,128)}, u32[]{:S(2)}) copy-start(f32[2,128,256]{2,1,0:T(8,128)} %get-tuple-element.51) | copy-start | bytes 786436
  61.6 6.2 %collective-permute-start.9 = (f32[4,2048]{1,0:T(4,128)S(1)}, f32[4,2048]{1,0:T(4,128)S(1)}, u32[]{:S(2)}, u32[]{:S(2)}) collective-permute-start(f32[4,2048]{1,0:T(4,128)S(1)} %add.28), channel_id=1, source_target_pairs={{0,4},{1,5},{2,6},{3,7},{4,0},{5,1},{6,2},{7,3},{8,12},{9,13},{10,... | collective-permute-start | bytes 98312 | tf_op jit(solution)/shard_map/ppermute | solution.py:123
  61.7 13.1 %collective-permute-start.13 = (bf16[2,128,256]{2,1,0:T(8,128)(2,1)S(1)}, bf16[2,128,256]{2,1,0:T(8,128)(2,1)S(1)}, u32[]{:S(2)}, u32[]{:S(2)}) collective-permute-start(bf16[2,128,256]{2,1,0:T(8,128)(2,1)S(1)} %get-tuple-element.73), channel_id=1, source_target_pairs={{0,1},{1,2},{2,3},{3,4},{4,5},{5,6},{6,7},{7,8},{8,9},{9,10},{10,1... | collective-permute-start | bytes 393224 | tf_op jit(solution)/shard_map/ppermute | solution.py:29
  61.7 13.1 %collective-permute-start.14 = (bf16[2,128,256]{2,1,0:T(8,128)(2,1)S(1)}, bf16[2,128,256]{2,1,0:T(8,128)(2,1)S(1)}, u32[]{:S(2)}, u32[]{:S(2)}) collective-permute-start(bf16[2,128,256]{2,1,0:T(8,128)(2,1)S(1)} %get-tuple-element.74), channel_id=1, source_target_pairs={{0,2},{1,3},{2,4},{3,5},{4,6},{5,7},{6,8},{7,9},{8,10},{9,11},{10,... | collective-permute-start | bytes 393224 | tf_op jit(solution)/shard_map/ppermute | solution.py:29
  67.8 7.1 %collective-permute-start.15 = (bf16[2,128,256]{2,1,0:T(8,128)(2,1)S(1)}, bf16[2,128,256]{2,1,0:T(8,128)(2,1)S(1)}, u32[]{:S(2)}, u32[]{:S(2)}) collective-permute-start(bf16[2,128,256]{2,1,0:T(8,128)(2,1)S(1)} %get-tuple-element.75), channel_id=1, source_target_pairs={{0,3},{1,4},{2,5},{3,6},{4,7},{5,8},{6,9},{7,10},{8,11},{9,12},{10... | collective-permute-start | bytes 393224 | tf_op jit(solution)/shard_map/ppermute | solution.py:29
  67.8 1.0 %copy-start.3 = (bf16[2,144,512]{2,1,0:T(8,128)(2,1)}, bf16[2,144,512]{2,1,0:T(8,128)(2,1)S(1)}, u32[]{:S(2)}) copy-start(bf16[2,144,512]{2,1,0:T(8,128)(2,1)S(1)} %collective-permute-done.11.back2) | copy-start | bytes 884740
  67.9 7.0 %collective-permute-start.12 = (f32[4,2048]{1,0:T(4,128)S(1)}, f32[4,2048]{1,0:T(4,128)S(1)}, u32[]{:S(2)}, u32[]{:S(2)}) collective-permute-start(f32[4,2048]{1,0:T(4,128)S(1)} %add.30), channel_id=1, source_target_pairs={{0,8},{1,9},{2,10},{3,11},{4,12},{5,13},{6,14},{7,15},{8,0},{9,1},... | collective-permute-start | bytes 98312 | tf_op jit(solution)/shard_map/ppermute | solution.py:123
